TPU v7x, 512 devices: a whole 4x8x8 slice. The times are simulated.
512 devices in a mesh: dp: 32 (over z_hi, y, core), ctx: 16 (over x, z_lo).
Axes of the slice: x: 4, y: 8, z: 8 (z_hi: 2, z_lo: 4; z = z_hi * 4 + z_lo), core: 2. Of those that a mesh axis runs over, the one named last changes fastest.
Arguments:
- input_proj: bfloat16 [64, 1024, 1024], P('dp', 'ctx'), may hold values from -6 to 6
- value_proj: bfloat16 [64, 1024, 1024], P('dp', 'ctx'), may hold values from -6 to 6
- output_proj: bfloat16 [64, 1024, 1024], P('dp', 'ctx'), may hold values from -6 to 6
- grad_out: bfloat16 [64, 1024, 1024], P('dp', 'ctx'), may hold values from -6 to 6
- filter_spectrum: float32 [32, 2, 1024, 1024], P('dp', None, 'ctx'), may hold values from -4 to 4
Outputs:
- grad_input: bfloat16 [64, 1024, 1024], P('dp', 'ctx')
- grad_value: bfloat16 [64, 1024, 1024], P('dp', 'ctx')
- grad_output_proj: bfloat16 [64, 1024, 1024], P('dp', 'ctx')
- grad_filter: float32 [32, 2, 1024, 1024], P('dp', None, 'ctx')
All inputs are finite; a program needn't handle non-finite values.
Results may differ from a plain program's by a relative error of at most 0.014.
Values may be sent and summed in bfloat16 or wider, within the bound.
No kernel may reach another device: no remote copies, remote signals or barrier semaphores. Data moves between devices by JAX's collectives and lax.ppermute only.
A program may use at most 64 MiB of HBM per device.

v0:
```python
import functools

import jax
import jax.numpy as jnp
import ml_dtypes
import numpy as np
from jax import lax
from jax.experimental import pallas as pl
from jax.experimental.pallas import tpu as pltpu
from jax.sharding import Mesh
from jax.sharding import PartitionSpec as P

N = 1024
TOTAL = N * N
RANKS = 16
ROWS = 64
SLOTS = 32
SCALE = 1.0 / TOTAL
BF = jnp.bfloat16
F32 = jnp.float32
NT = (((1,), (1,)), ((), ()))
BLOCKS = 4
WIDE = N // BLOCKS


def kept_rows():
    rank = np.arange(RANKS)
    return (ROWS * rank + (rank >= RANKS // 2))[:, None] + np.arange(SLOTS)[None, :]


def dft_tables():
    index = np.arange(N, dtype=np.int64)
    phase = (index[:, None] * index[None, :] % N).astype(np.float64) * (2.0 * np.pi / N)
    return np.cos(phase), np.sin(phase)


def section_table():
    cos, sin = dft_tables()
    rows = kept_rows()
    imag = -sin[rows]
    imag[0, 0] = 1.0 - 2.0 * (np.arange(N) % 2)
    both = np.stack([cos[rows], imag])
    both = both.reshape(2, RANKS // 2, 2, SLOTS, N).transpose(1, 0, 2, 3, 4)
    return both.reshape(N, N).astype(ml_dtypes.bfloat16)


def forward_turn():
    rows = kept_rows().reshape(1, -1, 1)
    place = np.arange(N).reshape(RANKS, 1, ROWS)
    phase = (rows * place % TOTAL).astype(np.float64) * (2.0 * np.pi / TOTAL)
    return np.concatenate([np.cos(phase), np.sin(phase)], axis=2).astype(np.float32)


def inverse_turn():
    rows = kept_rows().reshape(RANKS, 1, SLOTS)
    place = np.arange(N).reshape(1, N, 1)
    phase = (rows * place % TOTAL).astype(np.float64) * (2.0 * np.pi / TOTAL)
    cos, sin = np.cos(phase), np.sin(phase)
    return np.concatenate([cos, cos, sin, sin], axis=2).astype(np.float32)


def half_turn():
    phase = np.arange(N) * (np.pi / N)
    return np.cos(phase), np.sin(phase)


def lanes_of(shape):
    return lax.broadcasted_iota(jnp.int32, shape, len(shape) - 1)


def rows_of(shape):
    return lax.broadcasted_iota(jnp.int32, shape, len(shape) - 2)


def swap_halves(value):
    half = value.shape[-1] // 2
    return jnp.concatenate([value[..., half:], value[..., :half]], axis=-1)


def split_turn(packed):
    swapped = swap_halves(packed)
    low = lanes_of(packed.shape) < packed.shape[-1] // 2
    return jnp.where(low, packed, swapped), jnp.where(low, swapped, packed)


def section_kernel(rank, inp, val, outp, grad, table, turn, out, signals):
    @pl.when(pl.program_id(0) == 0)
    def _():
        for chan in range(2):
            gated = inp[chan].astype(F32) * val[chan].astype(F32)
            conv = grad[chan].astype(F32) * outp[chan].astype(F32)
            signals[128 * chan : 128 * chan + 64, :] = gated.astype(BF)
            signals[128 * chan + 64 : 128 * chan + 128, :] = conv.astype(BF)

    section = lax.dot_general(table[...], signals[...], NT, preferred_element_type=F32)
    for pair in range(2):
        cos, sin = split_turn(turn[0, 64 * pair : 64 * pair + 64, :])
        for chan in range(2):
            lanes = slice(128 * chan, 128 * chan + 128)
            real = section[128 * pair : 128 * pair + 64, lanes]
            imag = section[128 * pair + 64 : 128 * pair + 128, lanes]
            turned_re = (real * cos + imag * sin).astype(BF)
            turned_im = (imag * cos - real * sin).astype(BF)
            for odd in range(2):
                rows = slice(32 * odd, 32 * odd + 32)
                out[chan, 2 * pair + odd, 0:32, :] = turned_re[rows]
                out[chan, 2 * pair + odd, 32:64, :] = turned_im[rows]


def reverse_lanes(value):
    shape = (128, 128)
    flip = jnp.where(rows_of(shape) + lanes_of(shape) == 127, 1.0, 0.0).astype(BF)
    value = value.astype(BF)
    parts = [
        jnp.dot(value[:, 128 * part : 128 * part + 128], flip, preferred_element_type=F32)
        for part in reversed(range(N // 128))
    ]
    return jnp.concatenate(parts, axis=1)


def filter_kernel(rank, own, other, special, out):
    me = rank[0]
    low = me < RANKS // 2
    shape = (SLOTS, SLOTS)
    wanted = jnp.where(low, 32, 31)
    pick = jnp.where(rows_of(shape) + lanes_of(shape) == wanted, 1.0, 0.0).astype(BF)
    top = rows_of((SLOTS, N)) == 0
    for part in range(2):
        sign = 1.0 if part == 0 else -1.0
        mine = jnp.where(low, own[0, part, 0:32, :], own[0, part, 1:33, :])
        moved = jnp.dot(pick, other[part], preferred_element_type=F32)
        mirror = reverse_lanes(moved)
        first = own[0, part, 0:8, :]
        extra = jnp.broadcast_to(special[part : part + 1, :].astype(F32), (8, N))
        flipped = reverse_lanes(jnp.concatenate([first, extra], axis=0))
        around = pltpu.roll(flipped[0:8], 1, 1)
        head = jnp.where(me == 0, around, flipped[8:16])[0:1]
        mirror = jnp.where(jnp.logical_and(top, low), head, mirror)
        out[part, 0:32, :] = 0.5 * (mine + sign * mirror)
        out[part, 32:40, :] = 0.5 * (extra + sign * flipped[8:16])


def spectrum_kernel(rank, turned, cos, sin, half, spec, grad, grad_low, grad_row, left):
    me = rank[0]

    @pl.when(pl.program_id(0) == 0)
    def _():
        for seq in range(2):
            for pair in range(RANKS // 2):
                even = turned[RANKS * seq + 2 * pair]
                odd = turned[RANKS * seq + 2 * pair + 1]
                here = slice(128 * pair, 128 * pair + 128)
                there = slice(N + 128 * pair, N + 128 * pair + 128)
                for sig in range(2):
                    lanes = slice(64 * sig, 64 * sig + 64)
                    both = jnp.concatenate([even[:, lanes], odd[:, lanes]], axis=1)
                    base = 32 * (2 * seq + sig)
                    left[base : base + 32, here] = both[0:32]
                    left[base : base + 32, there] = both[32:64]
                    left[128 + base : 160 + base, here] = both[32:64]
                    left[128 + base : 160 + base, there] = -both[0:32]
        heads = []
        packed = jnp.logical_and(rows_of((16, N)) == 0, me == 0)
        for which in range(4):
            base = 32 * which
            block = left[base : base + 16, N:].astype(F32)
            heads.append(block[0:1])
            kept = jnp.where(packed, 0.0, block).astype(BF)
            left[base : base + 16, N:] = kept
            left[128 + base : 144 + base, :N] = kept
        head = jnp.concatenate(heads + heads, axis=0)
        real = head * half[0:1, :]
        imag = -head * half[1:2, :]
        left[256:272, :N] = jnp.concatenate([real, imag], axis=0).astype(BF)
        left[256:272, N:] = jnp.concatenate([imag, -real], axis=0).astype(BF)

    result = jnp.dot(left[:, :N], cos[...], preferred_element_type=F32)
    result = result + jnp.dot(left[:, N:], sin[...], preferred_element_type=F32)
    spec[...] = result.astype(BF)
    real = 0.0
    imag = 0.0
    row_re = 0.0
    row_im = 0.0
    for seq in range(2):
        base = 64 * seq
        u_re, u_im = result[base : base + 32], result[base + 128 : base + 160]
        d_re, d_im = result[base + 32 : base + 64], result[base + 160 : base + 192]
        real = real + (u_re * d_re + u_im * d_im)
        imag = imag + (u_re * d_im - u_im * d_re)
        base = 256 + 2 * seq
        u_re, u_im = result[base : base + 1], result[base + 8 : base + 9]
        d_re, d_im = result[base + 1 : base + 2], result[base + 9 : base + 10]
        row_re = row_re + (u_re * d_re + u_im * d_im)
        row_im = row_im + (u_re * d_im - u_im * d_re)
    real = real * SCALE
    imag = imag * SCALE
    grad[0] = real
    grad[1] = imag
    grad_low[0] = real.astype(BF)
    grad_low[1] = imag.astype(BF)
    row_re = jnp.where(me == 0, row_re * SCALE, real[0:1])
    row_im = jnp.where(me == 0, row_im * SCALE, imag[0:1])
    grad_row[...] = jnp.concatenate([row_re, row_im], axis=0).astype(BF)


def inverse_kernel(rank, spec, filt, cos, sin, turn, half, out, total, extra):
    me = rank[0]
    step = pl.program_id(0)

    def products(u_re, u_im, d_re, d_im, h_re, h_im):
        return (
            u_re * h_re - u_im * h_im,
            u_re * h_im + u_im * h_re,
            h_re * d_re + h_im * d_im,
            h_re * d_im - h_im * d_re,
        )

    def back(real, imag):
        straight = jnp.concatenate([real, imag], axis=0).astype(BF)
        crossed = jnp.concatenate([-imag, real], axis=0).astype(BF)
        return lax.dot_general(
            cos[...], straight, NT, preferred_element_type=F32
        ) + lax.dot_general(sin[...], crossed, NT, preferred_element_type=F32)

    values = spec[...].astype(F32)
    h_re, h_im = filt[0, 0:32, :], filt[1, 0:32, :]
    reals, imags = [], []
    for seq in range(2):
        base = 64 * seq
        p_re, p_im, q_re, q_im = products(
            values[base : base + 32],
            values[base + 128 : base + 160],
            values[base + 32 : base + 64],
            values[base + 160 : base + 192],
            h_re,
            h_im,
        )
        reals += [p_re, q_re]
        imags += [p_im, q_im]
    part = back(jnp.concatenate(reals, axis=0), jnp.concatenate(imags, axis=0))

    @pl.when(step == 0)
    def _():
        total[...] = part

    @pl.when(step != 0)
    def _():
        total[...] += part

    @pl.when(me == 0)
    def _():
        h_re, h_im = filt[0, 32:33, :], filt[1, 32:33, :]
        top = rows_of((SLOTS, WIDE)) == 0
        reals, imags = [], []
        for seq in range(2):
            base = 256 + 2 * seq
            p_re, p_im, q_re, q_im = products(
                values[base : base + 1],
                values[base + 8 : base + 9],
                values[base + 1 : base + 2],
                values[base + 9 : base + 10],
                h_re,
                h_im,
            )
            reals += [jnp.where(top, p_re, 0.0), jnp.where(top, q_re, 0.0)]
            imags += [jnp.where(top, p_im, 0.0), jnp.where(top, q_im, 0.0)]
        more = back(jnp.concatenate(reals, axis=0), jnp.concatenate(imags, axis=0))
        more = more[:, :128] * half[:, 0:1] - more[:, 128:] * half[:, 1:2]

        @pl.when(step == 0)
        def _():
            extra[...] = more

        @pl.when(step != 0)
        def _():
            extra[...] += more

    @pl.when(step == BLOCKS - 1)
    def _():
        turn_cos, turn_sin = split_turn(turn[0])
        real = total[:, :128]
        imag = total[:, 128:]
        un_re = real * turn_cos - imag * turn_sin
        un_im = real * turn_sin + imag * turn_cos
        packed = jnp.logical_and(lanes_of((N, 128)) % SLOTS == 0, me == 0)
        un_re = jnp.where(packed, un_re, 2.0 * un_re).astype(BF)
        un_im = jnp.where(packed, extra[...], 2.0 * un_im).astype(BF)
        out[0] = jnp.concatenate([un_re[:, :64], un_im[:, :64]], axis=1)
        out[1] = jnp.concatenate([un_re[:, 64:], un_im[:, 64:]], axis=1)


def result_kernel(arrived, table, inp, val, grad, d_inp, d_val, d_outp, left):
    @pl.when(pl.program_id(0) == 0)
    def _():
        for chan in range(2):
            for pair in range(RANKS // 2):
                even = arrived[RANKS * chan + 2 * pair]
                odd = arrived[RANKS * chan + 2 * pair + 1]
                for sig in range(2):
                    low = slice(32 * sig, 32 * sig + 32)
                    high = slice(64 + 32 * sig, 96 + 32 * sig)
                    base = 64 * (2 * chan + sig)
                    left[base : base + 64, 128 * pair : 128 * pair + 128] = jnp.concatenate(
                        [even[:, low], odd[:, low], even[:, high], odd[:, high]], axis=1
                    )

    result = jnp.dot(left[...], table[...], preferred_element_type=F32) * SCALE
    for chan in range(2):
        conv = result[128 * chan : 128 * chan + 64]
        gated = result[128 * chan + 64 : 128 * chan + 128]
        d_outp[chan] = (grad[chan].astype(F32) * conv).astype(BF)
        d_inp[chan] = (gated * val[chan].astype(F32)).astype(BF)
        d_val[chan] = (gated * inp[chan].astype(F32)).astype(BF)


def assemble_kernel(rank, own, other, special, out):
    me = rank[0]
    low = me < RANKS // 2
    shape = (SLOTS, SLOTS)
    wanted = jnp.where(low, 31, 32)
    pick = jnp.where(rows_of(shape) + lanes_of(shape) == wanted, 1.0, 0.0).astype(BF)
    top = rows_of((SLOTS, N)) == 0
    for part in range(2):
        sign = 1.0 if part == 0 else -1.0
        mine = own[part]
        shifted = pltpu.roll(mine, 1, 0)
        moved = jnp.dot(pick, other[part], preferred_element_type=F32)
        mirror = sign * reverse_lanes(moved)
        row = jnp.broadcast_to(special[part : part + 1, :].astype(F32), (16, N))
        turned = sign * reverse_lanes(row)
        head = jnp.where(me == RANKS // 2, row, turned)[0:1]
        out[0, part, 0:32, :] = jnp.where(low, mine, jnp.where(top, head, shifted))
        out[0, part, 32:64, :] = jnp.where(jnp.logical_and(top, ~low), shifted, mirror)


def whole(shape):
    return pl.BlockSpec(shape, lambda *_: (0,) * len(shape))


def sizes(flops, count):
    return pl.CostEstimate(flops=flops, bytes_accessed=count, transcendentals=0)


def params(mib):
    return pltpu.CompilerParams(vmem_limit_bytes=mib * 2**20)


def local(input_proj, value_proj, output_proj, grad_out, filter_spectrum):
    cos64, sin64 = dft_tables()
    cos_table = jnp.asarray(cos64.astype(ml_dtypes.bfloat16))
    sin_table = jnp.asarray(sin64.astype(ml_dtypes.bfloat16))
    sections = jnp.asarray(section_table())
    turn_out = jnp.asarray(forward_turn())
    turn_back = jnp.asarray(inverse_turn())
    half_rows = jnp.asarray(np.stack(half_turn()).astype(np.float32))
    half_columns = jnp.asarray(np.stack(half_turn(), axis=1).astype(np.float32))
    ctx_rank = lax.axis_index("ctx")
    rank = ctx_rank.astype(jnp.int32).reshape(1)
    half_ranks = RANKS // 2
    mirror_of = [(r, RANKS - 1 - r) for r in range(RANKS)]
    special_of = [(r, RANKS - r) for r in range(1, RANKS) if r != half_ranks]
    special_of += [(0, half_ranks), (half_ranks, 0)]

    other_rows = lax.ppermute(filter_spectrum[0, :, 32:64, :].astype(BF), "ctx", mirror_of)
    other_row = lax.ppermute(filter_spectrum[0, :, 0, :].astype(BF), "ctx", special_of)

    turned = pl.pallas_call(
        section_kernel,
        out_shape=jax.ShapeDtypeStruct((2, RANKS, ROWS, 128), BF),
        grid_spec=pltpu.PrefetchScalarGridSpec(
            num_scalar_prefetch=1,
            grid=(BLOCKS,),
            in_specs=[whole((2, ROWS, N))] * 4
            + [
                pl.BlockSpec((WIDE, N), lambda i, r: (i, 0)),
                pl.BlockSpec((1, WIDE // 2, 128), lambda i, r: (r[0], i, 0)),
            ],
            out_specs=pl.BlockSpec((2, RANKS // BLOCKS, ROWS, 128), lambda i, r: (0, i, 0, 0)),
            scratch_shapes=[pltpu.VMEM((256, N), BF)],
        ),
        compiler_params=params(24),
        cost_estimate=sizes(2 * 256 * N * N, 4 * 2**20),
        name="sections",
    )(rank, input_proj, value_proj, output_proj, grad_out, sections, turn_out)
    arrived = lax.all_to_all(
        turned.reshape(2 * RANKS, ROWS, 128), ("core", "ctx"), 0, 0, tiled=True
    )

    folded_filter = pl.pallas_call(
        filter_kernel,
        out_shape=jax.ShapeDtypeStruct((2, 40, N), F32),
        grid_spec=pltpu.PrefetchScalarGridSpec(
            num_scalar_prefetch=1,
            grid=(1,),
            in_specs=[whole((1, 2, ROWS, N)), whole((2, SLOTS, N)), whole((2, N))],
            out_specs=whole((2, 40, N)),
        ),
        compiler_params=params(16),
        cost_estimate=sizes(2**24, 2**20),
        name="fold_filter",
    )(rank, filter_spectrum, other_rows, other_row)

    spectra, grad_own, grad_low, grad_row = pl.pallas_call(
        spectrum_kernel,
        out_shape=[
            jax.ShapeDtypeStruct((272, N), BF),
            jax.ShapeDtypeStruct((2, SLOTS, N), F32),
            jax.ShapeDtypeStruct((2, SLOTS, N), BF),
            jax.ShapeDtypeStruct((2, N), BF),
        ],
        grid_spec=pltpu.PrefetchScalarGridSpec(
            num_scalar_prefetch=1,
            grid=(BLOCKS,),
            in_specs=[
                whole((2 * RANKS, ROWS, 128)),
                pl.BlockSpec((N, WIDE), lambda i, r: (0, i)),
                pl.BlockSpec((N, WIDE), lambda i, r: (0, i)),
                whole((2, N)),
            ],
            out_specs=[
                pl.BlockSpec((272, WIDE), lambda i, r: (0, i)),
                pl.BlockSpec((2, SLOTS, WIDE), lambda i, r: (0, 0, i)),
                pl.BlockSpec((2, SLOTS, WIDE), lambda i, r: (0, 0, i)),
                pl.BlockSpec((2, WIDE), lambda i, r: (0, i)),
            ],
            scratch_shapes=[pltpu.VMEM((272, 2 * N), BF)],
        ),
        compiler_params=params(24),
        cost_estimate=sizes(4 * 256 * N * N, 6 * 2**20),
        name="spectra",
    )(rank, arrived, cos_table, sin_table, half_rows)

    mirror_grad = lax.ppermute(grad_low, "ctx", mirror_of)
    mirror_row = lax.ppermute(grad_row, "ctx", special_of)

    unturned = pl.pallas_call(
        inverse_kernel,
        out_shape=jax.ShapeDtypeStruct((2, N, 128), BF),
        grid_spec=pltpu.PrefetchScalarGridSpec(
            num_scalar_prefetch=1,
            grid=(BLOCKS,),
            in_specs=[
                pl.BlockSpec((272, WIDE), lambda i, r: (0, i)),
                pl.BlockSpec((2, 40, WIDE), lambda i, r: (0, 0, i)),
                pl.BlockSpec((N, WIDE), lambda i, r: (0, i)),
                pl.BlockSpec((N, WIDE), lambda i, r: (0, i)),
                pl.BlockSpec((1, N, 128), lambda i, r: (r[0], 0, 0)),
                whole((N, 2)),
            ],
            out_specs=whole((2, N, 128)),
            scratch_shapes=[pltpu.VMEM((N, 256), F32), pltpu.VMEM((N, 128), F32)],
        ),
        compiler_params=params(32),
        cost_estimate=sizes(4 * 256 * N * N, 6 * 2**20),
        name="inverse",
    )(rank, spectra, folded_filter, cos_table, sin_table, turn_back, half_columns)
    returned = lax.all_to_all(
        unturned.reshape(2 * RANKS, ROWS, 128), ("core", "ctx"), 0, 0, tiled=True
    )

    grad_filter = pl.pallas_call(
        assemble_kernel,
        out_shape=jax.ShapeDtypeStruct((1, 2, ROWS, N), F32),
        grid_spec=pltpu.PrefetchScalarGridSpec(
            num_scalar_prefetch=1,
            grid=(1,),
            in_specs=[whole((2, SLOTS, N)), whole((2, SLOTS, N)), whole((2, N))],
            out_specs=whole((1, 2, ROWS, N)),
        ),
        compiler_params=params(16),
        cost_estimate=sizes(2**24, 2**20),
        name="assemble",
    )(rank, grad_own, mirror_grad, mirror_row)

    column = pl.BlockSpec((2, ROWS, WIDE), lambda i: (0, 0, i))
    grad_input, grad_value, grad_output_proj = pl.pallas_call(
        result_kernel,
        out_shape=[jax.ShapeDtypeStruct((2, ROWS, N), BF)] * 3,
        grid=(BLOCKS,),
        in_specs=[
            whole((2 * RANKS, ROWS, 128)),
            pl.BlockSpec((N, WIDE), lambda i: (0, i)),
            column,
            column,
            column,
        ],
        out_specs=[column] * 3,
        scratch_shapes=[pltpu.VMEM((256, N), BF)],
        compiler_params=params(24),
        cost_estimate=sizes(2 * 256 * N * N, 4 * 2**20),
        name="results",
    )(returned, sections, input_proj, value_proj, grad_out)
    return (grad_input, grad_value, grad_output_proj, grad_filter)


def solution(mesh):
    split = Mesh(mesh.devices.reshape(-1, 2, RANKS), ("group", "core", "ctx"))
    data = P(("group", "core"), "ctx", None)
    filt = P(("group", "core"), None, "ctx", None)
    return jax.shard_map(
        local,
        mesh=split,
        in_specs=(data, data, data, data, filt),
        out_specs=(data, data, data, filt),
        check_vma=False,
    )
```

profile of v0, /device:TPU:80, one launch (start us, length us, event | category | flops | bytes accessed | tf_op | source)
XLA Modules:
  0.0 87.2 jit_solution(3489850158778850366)
XLA Ops:
  0.6 0.0 copy-start.4
  0.6 1.6 %copy-done.4 = bf16[1024,1024]{1,0:T(8,128)(2,1)S(1)} copy-done((bf16[1024,1024]{1,0:T(8,128)(2,1)S(1)}, bf16[1024,1024]{1,0:T(8,128)(2,1)}, u32[]{:S(2)}) %copy-start.4) | copy-done | bytes 2097176
  2.2 0.0 copy-start.6
  2.2 2.2 %copy-done.6 = f32[16,512,128]{2,1,0:T(8,128)S(1)} copy-done((f32[16,512,128]{2,1,0:T(8,128)S(1)}, f32[16,512,128]{2,1,0:T(8,128)}, u32[]{:S(2)}) %copy-start.6) | copy-done | bytes 4194328
  4.4 0.0 copy-start.9
  4.4 0.9 %copy-done.9 = bf16[2,64,1024]{2,1,0:T(8,128)(2,1)S(1)} copy-done((bf16[2,64,1024]{2,1,0:T(8,128)(2,1)S(1)}, bf16[2,64,1024]{2,1,0:T(8,128)(2,1)}, u32[]{:S(2)}) %copy-start.9) | copy-done | bytes 262168
  5.4 0.0 copy-start.11
  5.4 0.9 %copy-done.11 = bf16[2,64,1024]{2,1,0:T(8,128)(2,1)S(1)} copy-done((bf16[2,64,1024]{2,1,0:T(8,128)(2,1)S(1)}, bf16[2,64,1024]{2,1,0:T(8,128)(2,1)}, u32[]{:S(2)}) %copy-start.11) | copy-done | bytes 262168
  6.3 0.0 copy-start.13
  6.3 0.9 %copy-done.13 = bf16[2,64,1024]{2,1,0:T(8,128)(2,1)S(1)} copy-done((bf16[2,64,1024]{2,1,0:T(8,128)(2,1)S(1)}, bf16[2,64,1024]{2,1,0:T(8,128)(2,1)}, u32[]{:S(2)}) %copy-start.13) | copy-done | bytes 262168
  7.3 0.0 copy-start.16
  7.3 0.9 %copy-done.16 = bf16[2,64,1024]{2,1,0:T(8,128)(2,1)S(1)} copy-done((bf16[2,64,1024]{2,1,0:T(8,128)(2,1)S(1)}, bf16[2,64,1024]{2,1,0:T(8,128)(2,1)}, u32[]{:S(2)}) %copy-start.16) | copy-done | bytes 262168
  8.2 1.6 %sections.1 = bf16[2,16,64,128]{3,2,1,0:T(8,128)(2,1)S(1)} custom-call(s32[1]{0:T(128)} %bitcast.rank, bf16[2,64,1024]{2,1,0:T(8,128)(2,1)S(1)} %copy-done.9, bf16[2,64,1024]{2,1,0:T(8,128)(2,1)S(1)} %copy-done.11, bf16[2,64,1024]{2,1,0:T(8,128)(2,1)S(1)} %copy-done.16, bf16[2,64,1024]{2,1,0:T(8,128)(2,1)S(1)} %copy-done.13, ...), custom_call_target="tpu_custom_call" | custom-call | flops 536870912 | bytes 4194304 | tf_op jit(solution)/shard_map/sections/pallas_call | solution.py:367
  9.8 0.0 copy-start.8
  9.8 0.8 copy-done.8
  10.6 9.7 %all-to-all-start = ((bf16[32,64,128]{2,1,0:T(8,128)(2,1)}), bf16[32,64,128]{2,1,0:T(8,128)(2,1)S(1)}, u32[]{:S(2)}, u32[]{:S(2)}) async-start(bf16[32,64,128]{2,1,0:T(8,128)(2,1)} %bitcast.7), calls=%async_computation | async-start | bytes 1048576 | tf_op jit(solution)/shard_map/all_to_all | solution.py:385
  20.3 0.0 copy-done.7
  20.3 0.4 copy.19
  20.7 0.1 slice_bitcast_fusion
  20.8 5.5 %collective-permute-start = (bf16[2,32,1024]{2,0,1:T(2,128)(2,1)S(1)}, bf16[2,32,1024]{2,0,1:T(2,128)(2,1)S(1)}, u32[]{:S(2)}, u32[]{:S(2)}) collective-permute-start(bf16[2,32,1024]{2,0,1:T(2,128)(2,1)S(1)} %slice_bitcast_fusion), channel_id=1, source_target_pairs={{0,15},{1,14},{2,13},{3,12},{4,11},{5,10},{6,9},{7,8},{8,7},{9,6},... | collective-permute-start | bytes 393224 | tf_op jit(solution)/shard_map/ppermute | solution.py:364
  26.3 3.0 %collective-permute-start.1 = (bf16[2,1024]{1,0:T(2,128)(2,1)S(1)}, bf16[2,1024]{1,0:T(2,128)(2,1)S(1)}, u32[]{:S(2)}, u32[]{:S(2)}) collective-permute-start(bf16[2,1024]{1,0:T(2,128)(2,1)S(1)} %slice_bitcast_fusion.1), channel_id=1, source_target_pairs={{1,15},{2,14},{3,13},{4,12},{5,11},{6,10},{7,9},{9,7},{10,6},{11,5... | collective-permute-start | bytes 12296 | tf_op jit(solution)/shard_map/ppermute | solution.py:365
  29.4 12.6 %collective-permute-done = bf16[2,32,1024]{2,0,1:T(2,128)(2,1)S(1)} collective-permute-done((bf16[2,32,1024]{2,0,1:T(2,128)(2,1)S(1)}, bf16[2,32,1024]{2,0,1:T(2,128)(2,1)S(1)}, u32[]{:S(2)}, u32[]{:S(2)}) %collective-permute-start) | collective-permute-done | bytes 131104 | tf_op jit(solution)/shard_map/ppermute | solution.py:364
  42.0 0.0 collective-permute-done.1.special
  42.0 0.7 fold_filter.1.filt
  42.7 0.0 all-to-all-done.turned
  42.7 0.0 copy-done.1
  42.7 0.0 copy-done.17
  42.7 0.0 copy-start.2
  42.7 1.6 %copy-done.2 = bf16[1024,1024]{1,0:T(8,128)(2,1)S(1)} copy-done((bf16[1024,1024]{1,0:T(8,128)(2,1)S(1)}, bf16[1024,1024]{1,0:T(8,128)(2,1)}, u32[]{:S(2)}) %copy-start.2) | copy-done | bytes 2097176
  44.3 3.0 %spectra.1 = (bf16[272,1024]{1,0:T(8,128)(2,1)S(1)}, f32[2,32,1024]{2,1,0:T(8,128)S(1)}, bf16[2,32,1024]{2,1,0:T(8,128)(2,1)S(1)}, bf16[2,1024]{1,0:T(2,128)(2,1)S(1)}) custom-call(s32[1]{0:T(128)} %bitcast.rank, bf16[32,64,128]{2,1,0:T(8,128)(2,1)S(1)} %all-to-all-done.turned, bf16[1024,1024]{1,0:T(8,128)(2,1)S(1)} %copy-done.1, ...), custom_call_target="tpu_custom_call" | custom-call | flops 1073741824 | bytes 6291456 | tf_op jit(solution)/shard_map/spectra/pallas_call | solution.py:403
  47.3 0.0 copy-done.3
  47.3 0.0 copy-done.15
  47.3 0.0 copy-start
  47.3 3.4 %copy-done = f32[16,1024,128]{2,1,0:T(8,128)S(1)} copy-done((f32[16,1024,128]{2,1,0:T(8,128)S(1)}, f32[16,1024,128]{2,1,0:T(8,128)}, u32[]{:S(2)}) %copy-start) | copy-done | bytes 8388632
  50.7 4.3 %inverse.1 = bf16[2,1024,128]{2,1,0:T(8,128)(2,1)} custom-call(s32[1]{0:T(128)} %bitcast.rank, bf16[272,1024]{1,0:T(8,128)(2,1)S(1)} %get-tuple-element.11.spec, f32[2,40,1024]{2,1,0:T(8,128)S(1)} %fold_filter.1.filt, bf16[1024,1024]{1,0:T(8,128)(2,1)S(1)} %copy-done.1, bf16[1024,1024]{1,0:T(8,128)(2,1)S(1)} %copy-done.3, f32[16,1024,128]{2,1,0:T(8,128)S(1)} %copy-done, ...), custom_call_target="tpu_custom_call" | custom-call | flops 1073741824 | bytes 6291456 | tf_op jit(solution)/shard_map/inverse/pallas_call | solution.py:436
  55.0 4.7 %all-to-all-start.1 = ((bf16[32,64,128]{2,1,0:T(8,128)(2,1)}), bf16[32,64,128]{2,1,0:T(8,128)(2,1)S(1)}, u32[]{:S(2)}, u32[]{:S(2)}) async-start(bf16[32,64,128]{2,1,0:T(8,128)(2,1)} %bitcast.4), calls=%async_computation.1 | async-start | bytes 1048576 | tf_op jit(solution)/shard_map/all_to_all | solution.py:457
  59.7 5.5 %collective-permute-start.2 = (bf16[2,32,1024]{2,1,0:T(8,128)(2,1)S(1)}, bf16[2,32,1024]{2,1,0:T(8,128)(2,1)S(1)}, u32[]{:S(2)}, u32[]{:S(2)}) collective-permute-start(bf16[2,32,1024]{2,1,0:T(8,128)(2,1)S(1)} %get-tuple-element.16), channel_id=1, source_target_pairs={{0,15},{1,14},{2,13},{3,12},{4,11},{5,10},{6,9},{7,8},{8,7},{9,6},... | collective-permute-start | bytes 393224 | tf_op jit(solution)/shard_map/ppermute | solution.py:433
  65.2 3.0 %collective-permute-start.3 = (bf16[2,1024]{1,0:T(2,128)(2,1)S(1)}, bf16[2,1024]{1,0:T(2,128)(2,1)S(1)}, u32[]{:S(2)}, u32[]{:S(2)}) collective-permute-start(bf16[2,1024]{1,0:T(2,128)(2,1)S(1)} %get-tuple-element.17), channel_id=1, source_target_pairs={{1,15},{2,14},{3,13},{4,12},{5,11},{6,10},{7,9},{9,7},{10,6},{11,5... | collective-permute-start | bytes 12296 | tf_op jit(solution)/shard_map/ppermute | solution.py:434
  68.2 9.0 %collective-permute-done.3.special = bf16[2,1024]{1,0:T(2,128)(2,1)S(1)} collective-permute-done((bf16[2,1024]{1,0:T(2,128)(2,1)S(1)}, bf16[2,1024]{1,0:T(2,128)(2,1)S(1)}, u32[]{:S(2)}, u32[]{:S(2)}) %collective-permute-start.3) | collective-permute-done | bytes 4128 | tf_op jit(solution)/shard_map/ppermute | solution.py:434
  77.2 4.1 %collective-permute-done.2.other = bf16[2,32,1024]{2,1,0:T(8,128)(2,1)S(1)} collective-permute-done((bf16[2,32,1024]{2,1,0:T(8,128)(2,1)S(1)}, bf16[2,32,1024]{2,1,0:T(8,128)(2,1)S(1)}, u32[]{:S(2)}, u32[]{:S(2)}) %collective-permute-start.2) | collective-permute-done | bytes 131104 | tf_op jit(solution)/shard_map/ppermute | solution.py:433
  81.3 1.4 %assemble.1 = f32[1,2,64,1024]{3,2,1,0:T(8,128)} custom-call(s32[1]{0:T(128)} %bitcast.rank, f32[2,32,1024]{2,1,0:T(8,128)S(1)} %get-tuple-element.15.own, bf16[2,32,1024]{2,1,0:T(8,128)(2,1)S(1)} %collective-permute-done.2.other, bf16[2,1024]{1,0:T(2,128)(2,1)S(1)} %collective-permute-done.3.special), custom_call_target="tpu_custom_call" | custom-call | flops 16777216 | bytes 1048576 | tf_op jit(solution)/shard_map/assemble/pallas_call | solution.py:461
  82.8 0.0 all-to-all-done.1.arrived
  82.8 0.0 copy-done.10
  82.8 0.0 copy-done.12
  82.8 0.0 copy-done.14
  82.8 0.0 copy-start.5
  82.8 1.6 %copy-done.5 = bf16[1024,1024]{1,0:T(8,128)(2,1)S(1)} copy-done((bf16[1024,1024]{1,0:T(8,128)(2,1)S(1)}, bf16[1024,1024]{1,0:T(8,128)(2,1)}, u32[]{:S(2)}) %copy-start.5) | copy-done | bytes 2097176
  84.4 2.9 %results.1 = (bf16[2,64,1024]{2,1,0:T(8,128)(2,1)}, bf16[2,64,1024]{2,1,0:T(8,128)(2,1)}, bf16[2,64,1024]{2,1,0:T(8,128)(2,1)}) custom-call(bf16[32,64,128]{2,1,0:T(8,128)(2,1)S(1)} %all-to-all-done.1.arrived, bf16[1024,1024]{1,0:T(8,128)(2,1)S(1)} %copy-done.5, bf16[2,64,1024]{2,1,0:T(8,128)(2,1)S(1)} %copy-done.10, bf16[2,64,1024]{2,1,0:T(8,128)(2,1)S(1)} %copy-done.12, ...), custom_call_target="tpu_custom_call" | custom-call | flops 536870912 | bytes 4194304 | tf_op jit(solution)/shard_map/results/pallas_call | solution.py:476
  (10 shorter events, 0.0 us)
Async XLA Ops:
  0.6 1.6 %copy-start.4 = (bf16[1024,1024]{1,0:T(8,128)(2,1)S(1)}, bf16[1024,1024]{1,0:T(8,128)(2,1)}, u32[]{:S(2)}) copy-start(bf16[1024,1024]{1,0:T(8,128)(2,1)} %constant.20.clone.table) | copy-start | bytes 6291460
  2.2 2.2 %copy-start.6 = (f32[16,512,128]{2,1,0:T(8,128)S(1)}, f32[16,512,128]{2,1,0:T(8,128)}, u32[]{:S(2)}) copy-start(f32[16,512,128]{2,1,0:T(8,128)} %constant.21.clone.turn) | copy-start | bytes 12582916
  4.4 0.9 %copy-start.9 = (bf16[2,64,1024]{2,1,0:T(8,128)(2,1)S(1)}, bf16[2,64,1024]{2,1,0:T(8,128)(2,1)}, u32[]{:S(2)}) copy-start(bf16[2,64,1024]{2,1,0:T(8,128)(2,1)} %inp.3) | copy-start | bytes 786436
  5.4 0.9 %copy-start.11 = (bf16[2,64,1024]{2,1,0:T(8,128)(2,1)S(1)}, bf16[2,64,1024]{2,1,0:T(8,128)(2,1)}, u32[]{:S(2)}) copy-start(bf16[2,64,1024]{2,1,0:T(8,128)(2,1)} %val.3) | copy-start | bytes 786436
  6.3 0.9 %copy-start.13 = (bf16[2,64,1024]{2,1,0:T(8,128)(2,1)S(1)}, bf16[2,64,1024]{2,1,0:T(8,128)(2,1)}, u32[]{:S(2)}) copy-start(bf16[2,64,1024]{2,1,0:T(8,128)(2,1)} %grad.3) | copy-start | bytes 786436
  7.3 0.9 %copy-start.16 = (bf16[2,64,1024]{2,1,0:T(8,128)(2,1)S(1)}, bf16[2,64,1024]{2,1,0:T(8,128)(2,1)}, u32[]{:S(2)}) copy-start(bf16[2,64,1024]{2,1,0:T(8,128)(2,1)} %outp.1) | copy-start | bytes 786436
  8.2 12.1 %copy-start.7 = (f32[1,2,64,1024]{3,2,1,0:T(8,128)S(1)}, f32[1,2,64,1024]{3,2,1,0:T(8,128)}, u32[]{:S(2)}) copy-start(f32[1,2,64,1024]{3,2,1,0:T(8,128)} %own.1) | copy-start | bytes 1572868
  9.8 0.8 copy-start.8
  10.6 32.1 %copy-start.1 = (bf16[1024,1024]{1,0:T(8,128)(2,1)S(1)}, bf16[1024,1024]{1,0:T(8,128)(2,1)}, u32[]{:S(2)}) copy-start(bf16[1024,1024]{1,0:T(8,128)(2,1)} %constant.18.clone.cos) | copy-start | bytes 6291460
  10.6 32.1 %copy-start.17 = (f32[2,1024]{1,0:T(2,128)S(1)}, f32[2,1024]{1,0:T(2,128)}, u32[]{:S(2)}) copy-start(f32[2,1024]{1,0:T(2,128)} %constant.23.clone.half) | copy-start | bytes 24580
  10.6 32.1 %all-to-all-start = ((bf16[32,64,128]{2,1,0:T(8,128)(2,1)}), bf16[32,64,128]{2,1,0:T(8,128)(2,1)S(1)}, u32[]{:S(2)}, u32[]{:S(2)}) async-start(bf16[32,64,128]{2,1,0:T(8,128)(2,1)} %bitcast.7), calls=%async_computation | async-start | bytes 1048576 | tf_op jit(solution)/shard_map/all_to_all | solution.py:385
  20.8 21.1 %collective-permute-start = (bf16[2,32,1024]{2,0,1:T(2,128)(2,1)S(1)}, bf16[2,32,1024]{2,0,1:T(2,128)(2,1)S(1)}, u32[]{:S(2)}, u32[]{:S(2)}) collective-permute-start(bf16[2,32,1024]{2,0,1:T(2,128)(2,1)S(1)} %slice_bitcast_fusion), channel_id=1, source_target_pairs={{0,15},{1,14},{2,13},{3,12},{4,11},{5,10},{6,9},{7,8},{8,7},{9,6},... | collective-permute-start | bytes 393224 | tf_op jit(solution)/shard_map/ppermute | solution.py:364
  26.3 15.7 %collective-permute-start.1 = (bf16[2,1024]{1,0:T(2,128)(2,1)S(1)}, bf16[2,1024]{1,0:T(2,128)(2,1)S(1)}, u32[]{:S(2)}, u32[]{:S(2)}) collective-permute-start(bf16[2,1024]{1,0:T(2,128)(2,1)S(1)} %slice_bitcast_fusion.1), channel_id=1, source_target_pairs={{1,15},{2,14},{3,13},{4,12},{5,11},{6,10},{7,9},{9,7},{10,6},{11,5... | collective-permute-start | bytes 12296 | tf_op jit(solution)/shard_map/ppermute | solution.py:365
  42.7 1.6 %copy-start.2 = (bf16[1024,1024]{1,0:T(8,128)(2,1)S(1)}, bf16[1024,1024]{1,0:T(8,128)(2,1)}, u32[]{:S(2)}) copy-start(bf16[1024,1024]{1,0:T(8,128)(2,1)} %constant.19.clone.sin) | copy-start | bytes 6291460
  44.3 3.0 %copy-start.3 = (bf16[1024,1024]{1,0:T(8,128)(2,1)S(1)}, bf16[1024,1024]{1,0:T(8,128)(2,1)}, u32[]{:S(2)}) copy-start(bf16[1024,1024]{1,0:T(8,128)(2,1)} %constant.19.clone.sin) | copy-start | bytes 6291460
  44.3 3.0 %copy-start.15 = (f32[1024,2]{1,0:T(8,128)S(1)}, f32[1024,2]{1,0:T(8,128)}, u32[]{:S(2)}) copy-start(f32[1024,2]{1,0:T(8,128)} %constant.24.clone.half) | copy-start | bytes 24580
  47.3 3.4 %copy-start = (f32[16,1024,128]{2,1,0:T(8,128)S(1)}, f32[16,1024,128]{2,1,0:T(8,128)}, u32[]{:S(2)}) copy-start(f32[16,1024,128]{2,1,0:T(8,128)} %constant.22.clone.turn) | copy-start | bytes 25165828
  54.9 27.8 %copy-start.10 = (bf16[2,64,1024]{2,1,0:T(8,128)(2,1)S(1)}, bf16[2,64,1024]{2,1,0:T(8,128)(2,1)}, u32[]{:S(2)}) copy-start(bf16[2,64,1024]{2,1,0:T(8,128)(2,1)} %inp.3) | copy-start | bytes 786436
  55.0 27.8 %copy-start.12 = (bf16[2,64,1024]{2,1,0:T(8,128)(2,1)S(1)}, bf16[2,64,1024]{2,1,0:T(8,128)(2,1)}, u32[]{:S(2)}) copy-start(bf16[2,64,1024]{2,1,0:T(8,128)(2,1)} %val.3) | copy-start | bytes 786436
  55.0 27.8 %copy-start.14 = (bf16[2,64,1024]{2,1,0:T(8,128)(2,1)S(1)}, bf16[2,64,1024]{2,1,0:T(8,128)(2,1)}, u32[]{:S(2)}) copy-start(bf16[2,64,1024]{2,1,0:T(8,128)(2,1)} %grad.3) | copy-start | bytes 786436
  55.0 27.8 %all-to-all-start.1 = ((bf16[32,64,128]{2,1,0:T(8,128)(2,1)}), bf16[32,64,128]{2,1,0:T(8,128)(2,1)S(1)}, u32[]{:S(2)}, u32[]{:S(2)}) async-start(bf16[32,64,128]{2,1,0:T(8,128)(2,1)} %bitcast.4), calls=%async_computation.1 | async-start | bytes 1048576 | tf_op jit(solution)/shard_map/all_to_all | solution.py:457
  59.7 21.7 %collective-permute-start.2 = (bf16[2,32,1024]{2,1,0:T(8,128)(2,1)S(1)}, bf16[2,32,1024]{2,1,0:T(8,128)(2,1)S(1)}, u32[]{:S(2)}, u32[]{:S(2)}) collective-permute-start(bf16[2,32,1024]{2,1,0:T(8,128)(2,1)S(1)} %get-tuple-element.16), channel_id=1, source_target_pairs={{0,15},{1,14},{2,13},{3,12},{4,11},{5,10},{6,9},{7,8},{8,7},{9,6},... | collective-permute-start | bytes 393224 | tf_op jit(solution)/shard_map/ppermute | solution.py:433
  65.2 12.1 %collective-permute-start.3 = (bf16[2,1024]{1,0:T(2,128)(2,1)S(1)}, bf16[2,1024]{1,0:T(2,128)(2,1)S(1)}, u32[]{:S(2)}, u32[]{:S(2)}) collective-permute-start(bf16[2,1024]{1,0:T(2,128)(2,1)S(1)} %get-tuple-element.17), channel_id=1, source_target_pairs={{1,15},{2,14},{3,13},{4,12},{5,11},{6,10},{7,9},{9,7},{10,6},{11,5... | collective-permute-start | bytes 12296 | tf_op jit(solution)/shard_map/ppermute | solution.py:434
  82.8 1.6 %copy-start.5 = (bf16[1024,1024]{1,0:T(8,128)(2,1)S(1)}, bf16[1024,1024]{1,0:T(8,128)(2,1)}, u32[]{:S(2)}) copy-start(bf16[1024,1024]{1,0:T(8,128)(2,1)} %constant.20.clone.table) | copy-start | bytes 6291460
where the time goes:
time: 87.9 us; the launch traced here: 87.2 us
  starting transfers between devices  31.4 us (36%)
  waiting for transfers between devices  25.7 us (29%)
  local copies, waits for them, and re-layouts  15.5 us (18%)
  Pallas kernels  13.8 us (16%)
    unnamed x37, local copies, waits for them, and re-layouts  15.3 us
    ppermute x1, waiting for transfers between devices, local(): lax.ppermute(filter_spectrum[0, :, 32:64, :].astype(BF), 'ctx', mirror_of)  12.6 us
    all_to_all x1, starting transfers between devices, local(): lax.all_to_all(turned.reshape(2 * RANKS, ROWS, 128), ('core', 'ctx'), 0,...  9.67 us
    ppermute x1, waiting for transfers between devices, local(): mirror_row = lax.ppermute(grad_row, 'ctx', special_of)  9.02 us
    ppermute x1, starting transfers between devices, local(): mirror_grad = lax.ppermute(grad_low, 'ctx', mirror_of)  5.49 us
    ppermute x1, starting transfers between devices, local(): lax.ppermute(filter_spectrum[0, :, 32:64, :].astype(BF), 'ctx', mirror_of)  5.49 us
    all_to_all x1, starting transfers between devices, local(): lax.all_to_all(unturned.reshape(2 * RANKS, ROWS, 128), ('core', 'ctx'), 0...  4.69 us
    pallas_call x1, Pallas kernels, local(): pl.pallas_call(inverse_kernel, out_shape=jax.ShapeDtypeStruct((2, N, 128)...  4.25 us
  transfers between devices with their start and end apart: 6, of which 3 were waited for; matrix products, arithmetic and copies ran while one was open for 1% of the time, Pallas kernels for 2%

commit v1 on v0

v1 whole, which is shorter than its diff:
```python
import functools

import jax
import jax.numpy as jnp
import ml_dtypes
import numpy as np
from jax import lax
from jax.experimental import pallas as pl
from jax.experimental.pallas import tpu as pltpu
from jax.sharding import Mesh
from jax.sharding import PartitionSpec as P

N = 1024
TOTAL = N * N
RANKS = 16
ROWS = 64
SLOTS = 32
SCALE = 1.0 / TOTAL
BF = jnp.bfloat16
F32 = jnp.float32
NT = (((1,), (1,)), ((), ()))
BLOCKS = 4
WIDE = N // BLOCKS
A_COST = 10**10
B_COST = 10**10
W_COST = 4 * 10**10


def kept_rows():
    rank = np.arange(RANKS)
    return (ROWS * rank + (rank >= RANKS // 2))[:, None] + np.arange(SLOTS)[None, :]


def dft_tables():
    index = np.arange(N, dtype=np.int64)
    phase = (index[:, None] * index[None, :] % N).astype(np.float64) * (2.0 * np.pi / N)
    return np.cos(phase), np.sin(phase)


def section_table():
    cos, sin = dft_tables()
    rows = kept_rows()
    imag = -sin[rows]
    imag[0, 0] = 1.0 - 2.0 * (np.arange(N) % 2)
    both = np.stack([cos[rows], imag])
    both = both.reshape(2, RANKS // 2, 2, SLOTS, N).transpose(1, 0, 2, 3, 4)
    return both.reshape(N, N).astype(ml_dtypes.bfloat16)


def forward_turn():
    rows = kept_rows().reshape(1, -1, 1)
    place = np.arange(N).reshape(RANKS, 1, ROWS)
    phase = (rows * place % TOTAL).astype(np.float64) * (2.0 * np.pi / TOTAL)
    return np.concatenate([np.cos(phase), np.sin(phase)], axis=2).astype(np.float32)


def inverse_turn():
    rows = kept_rows().reshape(RANKS, 1, SLOTS)
    place = np.arange(N).reshape(1, N, 1)
    phase = (rows * place % TOTAL).astype(np.float64) * (2.0 * np.pi / TOTAL)
    cos, sin = np.cos(phase), np.sin(phase)
    return np.concatenate([cos, cos, sin, sin], axis=2).astype(np.float32)


def half_turn():
    phase = np.arange(N) * (np.pi / N)
    return np.cos(phase), np.sin(phase)


def lanes_of(shape):
    return lax.broadcasted_iota(jnp.int32, shape, len(shape) - 1)


def rows_of(shape):
    return lax.broadcasted_iota(jnp.int32, shape, len(shape) - 2)


def swap_halves(value):
    half = value.shape[-1] // 2
    return jnp.concatenate([value[..., half:], value[..., :half]], axis=-1)


def split_turn(packed):
    swapped = swap_halves(packed)
    low = lanes_of(packed.shape) < packed.shape[-1] // 2
    return jnp.where(low, packed, swapped), jnp.where(low, swapped, packed)


def start_all(copies):
    for copy in copies:
        copy.start()


def section_kernel(
    rank, inp, val, outp, grad, table, turn, filt, out, row,
    gates, sections, turns, ready, signals, lines, sems
):
    gate_copies = [
        pltpu.make_async_copy(source, gates.at[which], sems.at[which])
        for which, source in enumerate((inp, val, outp, grad))
    ]
    turn_copy = pltpu.make_async_copy(turn.at[rank[0]], turns, sems.at[4])
    blocks = [pl.ds(WIDE * block, WIDE) for block in range(BLOCKS)]
    table_copies = [
        pltpu.make_async_copy(table.at[rows], sections.at[rows], sems.at[5 + block])
        for block, rows in enumerate(blocks)
    ]
    row_copy = pltpu.make_async_copy(
        filt.at[0, :, pl.ds(0, 8)], lines, sems.at[9 + 2 * BLOCKS]
    )
    start_all(gate_copies + table_copies[:1] + [turn_copy] + table_copies[1:] + [row_copy])
    for copy in gate_copies:
        copy.wait()
    for chan in range(2):
        gated = gates[0, chan].astype(F32) * gates[1, chan].astype(F32)
        conv = gates[3, chan].astype(F32) * gates[2, chan].astype(F32)
        signals[128 * chan : 128 * chan + 64, :] = gated.astype(BF)
        signals[128 * chan + 64 : 128 * chan + 128, :] = conv.astype(BF)
    out_copies = []
    for block, rows in enumerate(blocks):
        table_copies[block].wait()
        section = lax.dot_general(
            sections[rows, :], signals[...], NT, preferred_element_type=F32
        )
        if block == 0:
            turn_copy.wait()
        for pair in range(2):
            base = WIDE // 2 * block + 64 * pair
            cos, sin = split_turn(turns[base : base + 64, :])
            for chan in range(2):
                lanes = slice(128 * chan, 128 * chan + 128)
                real = section[128 * pair : 128 * pair + 64, lanes]
                imag = section[128 * pair + 64 : 128 * pair + 128, lanes]
                turned_re = (real * cos + imag * sin).astype(BF)
                turned_im = (imag * cos - real * sin).astype(BF)
                for odd in range(2):
                    some = slice(32 * odd, 32 * odd + 32)
                    peer = 4 * block + 2 * pair + odd
                    ready[chan, peer, 0:32, :] = turned_re[some]
                    ready[chan, peer, 32:64, :] = turned_im[some]
        peers = pl.ds(4 * block, 4)
        for chan in range(2):
            copy = pltpu.make_async_copy(
                ready.at[chan, peers], out.at[chan, peers], sems.at[9 + 2 * block + chan]
            )
            copy.start()
            out_copies.append(copy)
    row_copy.wait()
    row[...] = jnp.concatenate([lines[0, 0:1], lines[1, 0:1]], axis=0).astype(BF)
    for copy in out_copies:
        copy.wait()


def reverse_lanes(value):
    shape = (128, 128)
    flip = jnp.where(rows_of(shape) + lanes_of(shape) == 127, 1.0, 0.0).astype(BF)
    value = value.astype(BF)
    parts = [
        jnp.dot(value[:, 128 * part : 128 * part + 128], flip, preferred_element_type=F32)
        for part in reversed(range(N // 128))
    ]
    return jnp.concatenate(parts, axis=1)


def near_kernel_one(after, table, table_out, sems):
    copy = pltpu.make_async_copy(table, table_out, sems.at[0])
    copy.start()
    copy.wait()


def near_kernel(after, table, first, second, third, table_out, stack, sems):
    copies = [pltpu.make_async_copy(table, table_out, sems.at[0])] + [
        pltpu.make_async_copy(source, stack.at[which], sems.at[1 + which])
        for which, source in enumerate((first, second, third))
    ]
    start_all(copies)
    for copy in copies:
        copy.wait()


def bring_near(after, table, *others):
    shapes = [pltpu.VMEM(table.shape, table.dtype)]
    if others:
        shapes.append(pltpu.VMEM((len(others),) + others[0].shape, others[0].dtype))
    return pl.pallas_call(
        near_kernel if others else near_kernel_one,
        out_shape=shapes,
        in_specs=[HBM] * (2 + len(others)),
        out_specs=[VMEM] * len(shapes),
        scratch_shapes=[pltpu.SemaphoreType.DMA((1 + len(others),))],
        compiler_params=params(16),
        cost_estimate=sizes(W_COST),
        name="bring_near",
    )(after, kept(table), *[kept(value) for value in others])


def filter_kernel(rank, own, other, special, out, mine, sem):
    me = rank[0]
    copy = pltpu.make_async_copy(own.at[0], mine, sem)
    copy.start()
    low = me < RANKS // 2
    shape = (SLOTS, SLOTS)
    wanted = jnp.where(low, 32, 31)
    pick = jnp.where(rows_of(shape) + lanes_of(shape) == wanted, 1.0, 0.0).astype(BF)
    top = rows_of((SLOTS, N)) == 0
    copy.wait()
    for part in range(2):
        sign = 1.0 if part == 0 else -1.0
        kept = jnp.where(low, mine[part, 0:32, :], mine[part, 1:33, :])
        moved = jnp.dot(pick, other[32 * part : 32 * part + 32], preferred_element_type=F32)
        mirror = reverse_lanes(moved)
        first = mine[part, 0:8, :]
        extra = jnp.broadcast_to(special[part : part + 1, :].astype(F32), (8, N))
        flipped = reverse_lanes(jnp.concatenate([first, extra], axis=0))
        around = pltpu.roll(flipped[0:8], 1, 1)
        head = jnp.where(me == 0, around, flipped[8:16])[0:1]
        mirror = jnp.where(jnp.logical_and(top, low), head, mirror)
        out[part, 0:32, :] = 0.5 * (kept + sign * mirror)
        out[part, 32:40, :] = 0.5 * (extra + sign * flipped[8:16])


def alternating(shape):
    return 1 - 2 * (lanes_of(shape) % 2)


def spectrum_kernel(
    rank, turned, tables, filt_far, turn_far, half,
    spec, grad, grad_low, grad_row, tables_out, filt, turn, left, sems
):
    me = rank[0]
    middle = N // 2
    copies = [
        pltpu.make_async_copy(tables, tables_out, sems.at[0]),
        pltpu.make_async_copy(filt_far, filt, sems.at[1]),
        pltpu.make_async_copy(turn_far.at[me], turn, sems.at[2]),
    ]
    start_all(copies)
    for seq in range(2):
        for pair in range(RANKS // 2):
            even = turned[RANKS * seq + 2 * pair]
            odd = turned[RANKS * seq + 2 * pair + 1]
            here = slice(128 * (pair % 4), 128 * (pair % 4) + 128)
            there = slice(middle + 128 * (pair % 4), middle + 128 * (pair % 4) + 128)
            for sig in range(2):
                lanes = slice(64 * sig, 64 * sig + 64)
                both = jnp.concatenate([even[:, lanes], odd[:, lanes]], axis=1)
                base = 272 * (pair // 4) + 32 * (2 * seq + sig)
                left[base : base + 32, here] = both[0:32]
                left[base : base + 32, there] = both[32:64]
                left[128 + base : 160 + base, here] = both[32:64]
                left[128 + base : 160 + base, there] = -both[0:32]
    packed = jnp.logical_and(rows_of((16, middle)) == 0, me == 0)
    for part in range(2):
        heads = []
        for which in range(4):
            base = 272 * part + 32 * which
            block = left[base : base + 16, middle:].astype(F32)
            heads.append(block[0:1])
            cleared = jnp.where(packed, 0.0, block).astype(BF)
            left[base : base + 16, middle:] = cleared
            left[128 + base : 144 + base, :middle] = cleared
        head = jnp.concatenate(heads + heads, axis=0)
        places = slice(middle * part, middle * part + middle)
        real = head * half[0:1, places]
        imag = -head * half[1:2, places]
        lines = slice(272 * part + 256, 272 * part + 272)
        left[lines, :middle] = jnp.concatenate([real, imag], axis=0).astype(BF)
        left[lines, middle:] = jnp.concatenate([imag, -real], axis=0).astype(BF)

    sign = alternating((1, WIDE)).astype(F32)
    for block in range(BLOCKS):
        wide = slice(WIDE * block, WIDE * block + WIDE)
        halves = jnp.dot(left[...], tables[:, wide], preferred_element_type=F32)
        result = halves[:272] + sign * halves[272:]
        spec[:, wide] = result.astype(BF)
        real = 0.0
        imag = 0.0
        row_re = 0.0
        row_im = 0.0
        for seq in range(2):
            base = 64 * seq
            u_re, u_im = result[base : base + 32], result[base + 128 : base + 160]
            d_re, d_im = result[base + 32 : base + 64], result[base + 160 : base + 192]
            real = real + (u_re * d_re + u_im * d_im)
            imag = imag + (u_re * d_im - u_im * d_re)
            base = 256 + 2 * seq
            u_re, u_im = result[base : base + 1], result[base + 8 : base + 9]
            d_re, d_im = result[base + 1 : base + 2], result[base + 9 : base + 10]
            row_re = row_re + (u_re * d_re + u_im * d_im)
            row_im = row_im + (u_re * d_im - u_im * d_re)
        real = real * SCALE
        imag = imag * SCALE
        grad[0, :, wide] = real
        grad[1, :, wide] = imag
        grad_low[0:32, wide] = real.astype(BF)
        grad_low[32:64, wide] = imag.astype(BF)
        row_re = jnp.where(me == 0, row_re * SCALE, real[0:1])
        row_im = jnp.where(me == 0, row_im * SCALE, imag[0:1])
        grad_row[:, wide] = jnp.concatenate([row_re, row_im], axis=0).astype(BF)
    for copy in copies:
        copy.wait()


def products(u_re, u_im, d_re, d_im, h_re, h_im):
    return (
        u_re * h_re - u_im * h_im,
        u_re * h_im + u_im * h_re,
        h_re * d_re + h_im * d_im,
        h_re * d_im - h_im * d_re,
    )


def inverse_kernel(rank, spec, filt, tables, turn, half, grad, out, grad_far, total, sem):
    me = rank[0]
    copy = pltpu.make_async_copy(grad, grad_far, sem)
    copy.start()
    outer, inner = (0, 3), (1, 2)
    sign = alternating((1, WIDE)).astype(BF)
    packed_row = jnp.logical_and(rows_of((SLOTS, WIDE)) == 0, me == 0)
    for block in range(BLOCKS):
        wide = slice(WIDE * block, WIDE * block + WIDE)
        values = spec[:, wide].astype(F32)
        h_re, h_im = filt[0, 0:32, wide], filt[1, 0:32, wide]
        x_re, x_im = filt[0, 32:33, wide], filt[1, 32:33, wide]
        reals, imags, extra_re, extra_im = [], [], [], []
        for seq in range(2):
            base = 64 * seq
            p_re, p_im, q_re, q_im = products(
                values[base : base + 32],
                values[base + 128 : base + 160],
                values[base + 32 : base + 64],
                values[base + 160 : base + 192],
                h_re,
                h_im,
            )
            reals += [p_re, q_re]
            imags += [p_im, q_im]
            base = 256 + 2 * seq
            p_re, p_im, q_re, q_im = products(
                values[base : base + 1],
                values[base + 8 : base + 9],
                values[base + 1 : base + 2],
                values[base + 9 : base + 10],
                x_re,
                x_im,
            )
            extra_re += [p_re, q_re]
            extra_im += [p_im, q_im]

        def mixed(plain, extra, sign):
            return [jnp.where(packed_row, sign * e, p) for p, e in zip(plain, extra)]

        def joined(first, second):
            return jnp.concatenate(first + second, axis=0).astype(BF)

        less = [-value for value in imags]
        for parts, extra, crossed in (
            (outer, extra_re, mixed(reals, extra_im, -1.0)),
            (inner, extra_im, mixed(reals, extra_re, 1.0)),
        ):
            straight = joined(reals, mixed(imags, extra, 1.0))
            crossing = joined(less, crossed)
            for quarter in parts:
                rows = slice(WIDE * quarter, WIDE * quarter + WIDE)
                start = WIDE * (quarter % 2)
                cos = tables[start : start + WIDE, wide]
                sin = tables[N // 2 + start : N // 2 + start + WIDE, wide]
                if quarter >= 2:
                    cos, sin = cos * sign, sin * sign
                part = lax.dot_general(
                    cos, straight, NT, preferred_element_type=F32
                ) + lax.dot_general(sin, crossing, NT, preferred_element_type=F32)
                if block == 0:
                    total[rows, :] = part
                else:
                    total[rows, :] += part

    for piece in range(BLOCKS):
        rows = slice(WIDE * piece, WIDE * piece + WIDE)
        turn_cos, turn_sin = split_turn(turn[rows, :])
        real = total[rows, :128]
        imag = total[rows, 128:]
        un_re = real * turn_cos - imag * turn_sin
        un_im = real * turn_sin + imag * turn_cos
        packed = jnp.logical_and(lanes_of((WIDE, 128)) % SLOTS == 0, me == 0)
        un_im = jnp.where(packed, imag * half[rows, 0:1], 2.0 * un_im).astype(BF)
        un_re = jnp.where(packed, real, 2.0 * un_re).astype(BF)
        out[0, rows, :] = jnp.concatenate([un_re[:, :64], un_im[:, :64]], axis=1)
        out[1, rows, :] = jnp.concatenate([un_re[:, 64:], un_im[:, 64:]], axis=1)
    copy.wait()


def result_kernel(arrived, table, gates, d_inp, d_val, d_outp, left, ready, sems):
    for chan in range(2):
        for pair in range(RANKS // 2):
            even = arrived[RANKS * chan + 2 * pair]
            odd = arrived[RANKS * chan + 2 * pair + 1]
            for sig in range(2):
                low = slice(32 * sig, 32 * sig + 32)
                high = slice(64 + 32 * sig, 96 + 32 * sig)
                base = 64 * (2 * chan + sig)
                left[base : base + 64, 128 * pair : 128 * pair + 128] = jnp.concatenate(
                    [even[:, low], odd[:, low], even[:, high], odd[:, high]], axis=1
                )
    copies = []
    for block in range(BLOCKS):
        wide = slice(WIDE * block, WIDE * block + WIDE)
        result = jnp.dot(left[...], table[:, wide], preferred_element_type=F32) * SCALE
        for chan in range(2):
            conv = result[128 * chan : 128 * chan + 64]
            gated = result[128 * chan + 64 : 128 * chan + 128]
            ready[2, chan, :, wide] = (gates[2, chan, :, wide].astype(F32) * conv).astype(BF)
            ready[0, chan, :, wide] = (gated * gates[1, chan, :, wide].astype(F32)).astype(BF)
            ready[1, chan, :, wide] = (gated * gates[0, chan, :, wide].astype(F32)).astype(BF)
        for which, target in enumerate((d_inp, d_val, d_outp)):
            copy = pltpu.make_async_copy(
                ready.at[which, :, :, pl.ds(WIDE * block, WIDE)],
                target.at[:, :, pl.ds(WIDE * block, WIDE)],
                sems.at[3 * block + which],
            )
            copy.start()
            copies.append(copy)
    for copy in copies:
        copy.wait()


def assemble_kernel(rank, own, other, special, out):
    me = rank[0]
    low = me < RANKS // 2
    shape = (SLOTS, SLOTS)
    wanted = jnp.where(low, 31, 32)
    pick = jnp.where(rows_of(shape) + lanes_of(shape) == wanted, 1.0, 0.0).astype(BF)
    top = rows_of((SLOTS, N)) == 0
    for part in range(2):
        sign = 1.0 if part == 0 else -1.0
        mine = own[part]
        shifted = pltpu.roll(mine, 1, 0)
        moved = jnp.dot(pick, other[32 * part : 32 * part + 32], preferred_element_type=F32)
        mirror = sign * reverse_lanes(moved)
        row = jnp.broadcast_to(special[part : part + 1, :].astype(F32), (16, N))
        turned = sign * reverse_lanes(row)
        head = jnp.where(me == RANKS // 2, row, turned)[0:1]
        out[0, part, 0:32, :] = jnp.where(low, mine, jnp.where(top, head, shifted))
        out[0, part, 32:64, :] = jnp.where(jnp.logical_and(top, ~low), shifted, mirror)


HBM = pl.BlockSpec(memory_space=pltpu.HBM)
VMEM = pl.BlockSpec(memory_space=pltpu.VMEM)
SMEM = pl.BlockSpec(memory_space=pltpu.SMEM)


def kept(value):
    return pltpu.with_memory_space_constraint(value, pltpu.HBM)


def sizes(flops, count=2**20):
    return pl.CostEstimate(flops=flops, bytes_accessed=count, transcendentals=0)


def params(mib):
    return pltpu.CompilerParams(vmem_limit_bytes=mib * 2**20)


def local(input_proj, value_proj, output_proj, grad_out, filter_spectrum):
    cos64, sin64 = dft_tables()
    half_tables = np.concatenate([cos64[: N // 2], sin64[: N // 2]]).astype(ml_dtypes.bfloat16)
    half_tables = jnp.asarray(half_tables)
    sections = jnp.asarray(section_table())
    turn_out = jnp.asarray(forward_turn())
    turn_back = jnp.asarray(inverse_turn())
    half_rows = jnp.asarray(np.stack(half_turn()).astype(np.float32))
    cosine, sine = half_turn()
    middle = np.abs(np.arange(N) - N // 2 + 0.5) < N // 4
    spread = np.where(middle, -1.0 / np.where(middle, sine, 1.0), 1.0 / np.where(middle, 1.0, cosine))
    half_columns = jnp.asarray(spread[:, None].astype(np.float32))
    ctx_rank = lax.axis_index("ctx")
    rank = ctx_rank.astype(jnp.int32).reshape(1)
    half_ranks = RANKS // 2
    mirror_of = [(r, RANKS - 1 - r) for r in range(RANKS)]
    special_of = [(r, RANKS - r) for r in range(1, RANKS) if r != half_ranks]
    special_of += [(0, half_ranks), (half_ranks, 0)]

    filter_rows = filter_spectrum.reshape(2, ROWS, N)[:, 32:64, :].astype(BF)
    other_rows = lax.ppermute(filter_rows.reshape(2 * SLOTS, N), "ctx", mirror_of)

    turned, filter_row = pl.pallas_call(
        section_kernel,
        out_shape=[pltpu.HBM((2, RANKS, ROWS, 128), BF), pltpu.VMEM((2, N), BF)],
        in_specs=[SMEM] + [HBM] * 7,
        out_specs=[HBM, VMEM],
        scratch_shapes=[
            pltpu.VMEM((4, 2, ROWS, N), BF),
            pltpu.VMEM((N, N), BF),
            pltpu.VMEM((N // 2, 128), F32),
            pltpu.VMEM((2, RANKS, ROWS, 128), BF),
            pltpu.VMEM((256, N), BF),
            pltpu.VMEM((2, 8, N), F32),
            pltpu.SemaphoreType.DMA((10 + 2 * BLOCKS,)),
        ],
        compiler_params=params(24),
        cost_estimate=sizes(A_COST),
        name="sections",
    )(
        rank,
        kept(input_proj),
        kept(value_proj),
        kept(output_proj),
        kept(grad_out),
        kept(sections),
        kept(turn_out),
        kept(filter_spectrum),
    )
    other_row = lax.ppermute(filter_row, "ctx", special_of)
    arrived = lax.all_to_all(
        turned.reshape(2 * RANKS, ROWS, 128), ("core", "ctx"), 0, 0, tiled=True
    )

    (tables,) = bring_near(other_rows, half_tables)
    folded_filter = pl.pallas_call(
        filter_kernel,
        out_shape=pltpu.HBM((2, 40, N), F32),
        in_specs=[SMEM, HBM, VMEM, VMEM],
        out_specs=VMEM,
        scratch_shapes=[pltpu.VMEM((2, ROWS, N), F32), pltpu.SemaphoreType.DMA(())],
        compiler_params=params(16),
        cost_estimate=sizes(2**24),
        name="fold_filter",
    )(rank, kept(filter_spectrum), other_rows, other_row)

    spectra, grad_own, grad_low, grad_row, tables_again, filter_near, turn_near = pl.pallas_call(
        spectrum_kernel,
        out_shape=[
            pltpu.VMEM((272, N), BF),
            pltpu.VMEM((2, SLOTS, N), F32),
            pltpu.VMEM((2 * SLOTS, N), BF),
            pltpu.VMEM((2, N), BF),
            pltpu.VMEM((N, N), BF),
            pltpu.VMEM((2, 40, N), F32),
            pltpu.VMEM((N, 128), F32),
        ],
        in_specs=[SMEM, VMEM, VMEM, HBM, HBM, VMEM],
        out_specs=[VMEM] * 7,
        scratch_shapes=[
            pltpu.VMEM((544, N), BF),
            pltpu.SemaphoreType.DMA((3,)),
        ],
        compiler_params=params(20),
        cost_estimate=sizes(B_COST),
        name="spectra",
    )(
        rank,
        arrived,
        pltpu.with_memory_space_constraint(tables, pltpu.VMEM),
        kept(folded_filter),
        kept(turn_back),
        half_rows,
    )

    mirror_grad = lax.ppermute(grad_low, "ctx", mirror_of)
    mirror_row = lax.ppermute(grad_row, "ctx", special_of)

    unturned, grad_far = pl.pallas_call(
        inverse_kernel,
        out_shape=[
            jax.ShapeDtypeStruct((2, N, 128), BF),
            pltpu.HBM((2, SLOTS, N), F32),
        ],
        in_specs=[SMEM] + [VMEM] * 6,
        out_specs=[VMEM, HBM],
        scratch_shapes=[pltpu.VMEM((N, 256), F32), pltpu.SemaphoreType.DMA(())],
        compiler_params=params(24),
        cost_estimate=sizes(B_COST),
        name="inverse",
    )(rank, spectra, filter_near, tables_again, turn_near, half_columns, grad_own)
    returned = lax.all_to_all(
        unturned.reshape(2 * RANKS, ROWS, 128), ("core", "ctx"), 0, 0, tiled=True
    )

    sections_near, gates_near = bring_near(
        mirror_grad, sections, input_proj, value_proj, grad_out
    )
    grad_filter = pl.pallas_call(
        assemble_kernel,
        out_shape=jax.ShapeDtypeStruct((1, 2, ROWS, N), F32),
        in_specs=[SMEM] + [VMEM] * 3,
        out_specs=VMEM,
        compiler_params=params(16),
        cost_estimate=sizes(2**24),
        name="assemble",
    )(rank, grad_far, mirror_grad, mirror_row)

    grad_input, grad_value, grad_output_proj = pl.pallas_call(
        result_kernel,
        out_shape=[pltpu.HBM((2, ROWS, N), BF)] * 3,
        in_specs=[VMEM] * 3,
        out_specs=[HBM] * 3,
        scratch_shapes=[
            pltpu.VMEM((256, N), BF),
            pltpu.VMEM((3, 2, ROWS, N), BF),
            pltpu.SemaphoreType.DMA((3 * BLOCKS,)),
        ],
        compiler_params=params(20),
        cost_estimate=sizes(2 * 256 * N * N),
        name="results",
    )(returned, sections_near, gates_near)
    return (grad_input, grad_value, grad_output_proj, grad_filter)


def solution(mesh):
    split = Mesh(mesh.devices.reshape(-1, 2, RANKS), ("group", "core", "ctx"))
    data = P(("group", "core"), "ctx", None)
    filt = P(("group", "core"), None, "ctx", None)
    return jax.shard_map(
        local,
        mesh=split,
        in_specs=(data, data, data, data, filt),
        out_specs=(data, data, data, filt),
        check_vma=False,
    )
```

time: 87.9 us -> 72.9 us (0.83)
  the two profiles are of different devices: /device:TPU:80 before, /device:TPU:1 now
where the time goes in v1:
time: 72.9 us; the launch traced here: 72.2 us
  starting transfers between devices  38.1 us (52%)
  Pallas kernels  17.1 us (23%)
  waiting for transfers between devices  12.1 us (17%)
  local copies, waits for them, and re-layouts  2.96 us (4%)
  other arithmetic  1.07 us (1%)
  between operations  0.82 us (1%)
    ppermute x1, starting transfers between devices, local(): lax.ppermute(filter_rows.reshape(2 * SLOTS, N), 'ctx', mirror_of)  10.6 us
    ppermute x1, starting transfers between devices, local(): mirror_grad = lax.ppermute(grad_low, 'ctx', mirror_of)  7.2 us
    all_to_all x1, waiting for transfers between devices, local(): lax.all_to_all(unturned.reshape(2 * RANKS, ROWS, 128), ('core', 'ctx'), 0...  7.11 us
    all_to_all x1, starting transfers between devices, local(): lax.all_to_all(turned.reshape(2 * RANKS, ROWS, 128), ('core', 'ctx'), 0,...  5.53 us
    all_to_all x1, starting transfers between devices, local(): lax.all_to_all(unturned.reshape(2 * RANKS, ROWS, 128), ('core', 'ctx'), 0...  5.04 us
    all_to_all x1, waiting for transfers between devices, local(): lax.all_to_all(turned.reshape(2 * RANKS, ROWS, 128), ('core', 'ctx'), 0,...  5.02 us
    ppermute x1, starting transfers between devices, local(): mirror_row = lax.ppermute(grad_row, 'ctx', special_of)  4.93 us
    ppermute x1, starting transfers between devices, local(): other_row = lax.ppermute(filter_row, 'ctx', special_of)  4.8 us
  transfers between devices with their start and end apart: 6, of which 2 were waited for; matrix products, arithmetic and copies ran while one was open for 0% of the time, Pallas kernels for 19%

profile of v1, /device:TPU:1, one launch (start us, length us, event | category | flops | bytes accessed | tf_op | source)
XLA Modules:
  0.0 72.2 jit_solution(4491361127930194522)
XLA Ops:
  0.6 1.1 %convert_bitcast_fusion = bf16[2,64,1024]{2,1,0:T(8,128)(2,1)S(1)} fusion(f32[1,2,64,1024]{3,2,1,0:T(8,128)} %own.1), kind=kLoop, calls=%fused_computation | loop fusion | flops 131072 | bytes 786432 | tf_op jit(solution)/shard_map/reshape | solution.py:483
  1.7 10.6 %collective-permute-start = (bf16[64,1024]{1,0:T(8,128)(2,1)S(1)}, bf16[64,1024]{1,0:T(8,128)(2,1)S(1)}, u32[]{:S(2)}, u32[]{:S(2)}) collective-permute-start(bf16[64,1024]{1,0:T(8,128)(2,1)S(1)} %bitcast.7), channel_id=1, source_target_pairs={{0,15},{1,14},{2,13},{3,12},{4,11},{5,10},{6,9},{7,8},{8,7},{9,6},... | collective-permute-start | bytes 393224 | tf_op jit(solution)/shard_map/ppermute | solution.py:484
  12.4 4.1 %sections.1 = (bf16[2,16,64,128]{3,2,1,0:T(8,128)(2,1)}, bf16[2,1024]{1,0:T(2,128)(2,1)S(1)}) custom-call(s32[1]{0:T(128)} %bitcast.rank, bf16[2,64,1024]{2,1,0:T(8,128)(2,1)} %first.1, bf16[2,64,1024]{2,1,0:T(8,128)(2,1)} %second.1, bf16[2,64,1024]{2,1,0:T(8,128)(2,1)} %outp.1, bf16[2,64,1024]{2,1,0:T(8,128)(2,1)} %third.1, ...), custom_call_target="tpu_custom_call" | custom-call | flops 10000000000 | bytes 1048576 | tf_op jit(solution)/shard_map/sections/pallas_call | solution.py:486
  16.5 5.5 %all-to-all-start = ((bf16[32,64,128]{2,1,0:T(8,128)(2,1)}), bf16[32,64,128]{2,1,0:T(8,128)(2,1)S(1)}, u32[]{:S(2)}, u32[]{:S(2)}) async-start(bf16[32,64,128]{2,1,0:T(8,128)(2,1)} %bitcast.6), calls=%async_computation | async-start | bytes 1048576 | tf_op jit(solution)/shard_map/all_to_all | solution.py:514
  22.0 0.0 copy-start.2
  22.0 4.8 %collective-permute-start.1 = (bf16[2,1024]{1,0:T(2,128)(2,1)S(1)}, bf16[2,1024]{1,0:T(2,128)(2,1)S(1)}, u32[]{:S(2)}, u32[]{:S(2)}) collective-permute-start(bf16[2,1024]{1,0:T(2,128)(2,1)S(1)} %get-tuple-element.21), channel_id=1, source_target_pairs={{1,15},{2,14},{3,13},{4,12},{5,11},{6,10},{7,9},{9,7},{10,6},{11,5... | collective-permute-start | bytes 12296 | tf_op jit(solution)/shard_map/ppermute | solution.py:513
  26.8 0.0 collective-permute-done.after.other
  26.9 1.6 %bring_near.2.tables = bf16[1024,1024]{1,0:T(8,128)(2,1)S(1)} custom-call(bf16[64,1024]{1,0:T(8,128)(2,1)S(1)} %collective-permute-done.after.other, bf16[1024,1024]{1,0:T(8,128)(2,1)} %constant.16.clone.table), custom_call_target="tpu_custom_call" | custom-call | flops 40000000000 | bytes 1048576 | tf_op jit(solution)/shard_map/bring_near/pallas_call | solution.py:185
  28.5 0.0 copy-start.3
  28.5 1.3 %copy-done.3 = bf16[1024,1024]{1,0:T(8,128)(2,1)} copy-done((bf16[1024,1024]{1,0:T(8,128)(2,1)}, bf16[1024,1024]{1,0:T(8,128)(2,1)S(1)}, u32[]{:S(2)}) %copy-start.3) | copy-done | bytes 2097176
  29.8 0.0 collective-permute-done.1.special
  29.8 2.5 %fold_filter.1.filt_far = f32[2,40,1024]{2,1,0:T(8,128)} custom-call(s32[1]{0:T(128)} %bitcast.rank, f32[1,2,64,1024]{3,2,1,0:T(8,128)} %own.1, bf16[64,1024]{1,0:T(8,128)(2,1)S(1)} %collective-permute-done.after.other, bf16[2,1024]{1,0:T(2,128)(2,1)S(1)} %collective-permute-done.1.special), custom_call_target="tpu_custom_call" | custom-call | flops 16777216 | bytes 1048576 | tf_op jit(solution)/shard_map/fold_filter/pallas_call | solution.py:519
  32.3 0.0 copy-start.1
  32.3 5.0 %all-to-all-done.turned = bf16[32,64,128]{2,1,0:T(8,128)(2,1)S(1)} async-done(((bf16[32,64,128]{2,1,0:T(8,128)(2,1)}), bf16[32,64,128]{2,1,0:T(8,128)(2,1)S(1)}, u32[]{:S(2)}, u32[]{:S(2)}) %all-to-all-start) | async-done | bytes 524320 | tf_op jit(solution)/shard_map/all_to_all | solution.py:514
  37.4 0.0 copy-done.2
  37.4 0.0 copy-start.4
  37.4 1.6 %copy-done.4 = bf16[1024,1024]{1,0:T(8,128)(2,1)S(1)} copy-done((bf16[1024,1024]{1,0:T(8,128)(2,1)S(1)}, bf16[1024,1024]{1,0:T(8,128)(2,1)}, u32[]{:S(2)}) %copy-start.4) | copy-done | bytes 2097176
  38.9 1.7 %spectra.1 = (bf16[272,1024]{1,0:T(8,128)(2,1)S(1)}, f32[2,32,1024]{2,1,0:T(8,128)S(1)}, bf16[64,1024]{1,0:T(8,128)(2,1)S(1)}, bf16[2,1024]{1,0:T(2,128)(2,1)S(1...) custom-call(s32[1]{0:T(128)} %bitcast.rank, ...), custom_call_target="tpu_custom_call" | custom-call | flops 10000000000 | bytes 1048576 | tf_op jit(solution)/shard_map/spectra/pallas_call | solution.py:530
  40.6 7.2 %collective-permute-start.2 = (bf16[64,1024]{1,0:T(8,128)(2,1)S(1)}, bf16[64,1024]{1,0:T(8,128)(2,1)S(1)}, u32[]{:S(2)}, u32[]{:S(2)}) collective-permute-start(bf16[64,1024]{1,0:T(8,128)(2,1)S(1)} %get-tuple-element.28), channel_id=1, source_target_pairs={{0,15},{1,14},{2,13},{3,12},{4,11},{5,10},{6,9},{7,8},{8,7},{9,6},... | collective-permute-start | bytes 393224 | tf_op jit(solution)/shard_map/ppermute | solution.py:559
  47.8 0.0 copy-done.1
  47.8 2.4 %inverse.1 = (bf16[2,1024,128]{2,1,0:T(8,128)(2,1)}, f32[2,32,1024]{2,1,0:T(8,128)}) custom-call(s32[1]{0:T(128)} %bitcast.rank, bf16[272,1024]{1,0:T(8,128)(2,1)S(1)} %get-tuple-element.22.spec, f32[2,40,1024]{2,1,0:T(8,128)S(1)} %get-tuple-element.23.filt, bf16[1024,1024]{1,0:T(8,128)(2,1)S(1)} %get-tuple-element.24.tables, ...), custom_call_target="tpu_custom_call" | custom-call | flops 10000000000 | bytes 1048576 | tf_op jit(solution)/shard_map/inverse/pallas_call | solution.py:562
  50.2 5.0 %all-to-all-start.1 = ((bf16[32,64,128]{2,1,0:T(8,128)(2,1)}), bf16[32,64,128]{2,1,0:T(8,128)(2,1)S(1)}, u32[]{:S(2)}, u32[]{:S(2)}) async-start(bf16[32,64,128]{2,1,0:T(8,128)(2,1)} %bitcast.4), calls=%async_computation.1 | async-start | bytes 1048576 | tf_op jit(solution)/shard_map/all_to_all | solution.py:575
  55.2 0.0 copy-start
  55.3 4.9 %collective-permute-start.3 = (bf16[2,1024]{1,0:T(2,128)(2,1)S(1)}, bf16[2,1024]{1,0:T(2,128)(2,1)S(1)}, u32[]{:S(2)}, u32[]{:S(2)}) collective-permute-start(bf16[2,1024]{1,0:T(2,128)(2,1)S(1)} %get-tuple-element.35), channel_id=1, source_target_pairs={{1,15},{2,14},{3,13},{4,12},{5,11},{6,10},{7,9},{9,7},{10,6},{11,5... | collective-permute-start | bytes 12296 | tf_op jit(solution)/shard_map/ppermute | solution.py:560
  60.2 0.0 collective-permute-done.2.after.other
  60.2 1.8 %bring_near.3 = (bf16[1024,1024]{1,0:T(8,128)(2,1)S(1)}, bf16[3,2,64,1024]{3,2,1,0:T(8,128)(2,1)S(1)}) custom-call(bf16[64,1024]{1,0:T(8,128)(2,1)S(1)} %collective-permute-done.2.after.other, bf16[1024,1024]{1,0:T(8,128)(2,1)} %constant.17.clone.table, bf16[2,64,1024]{2,1,0:T(8,128)(2,1)} %first.1, bf16[2,64,1024]{2,1,0:T(8,128)(2,1)} %second.1, ...), custom_call_target="tpu_custom_call" | custom-call | flops 40000000000 | bytes 1048576 | tf_op jit(solution)/shard_map/bring_near/pallas_call | solution.py:185
  62.0 0.0 collective-permute-done.3.special
  62.0 0.0 copy-done
  62.0 1.4 %assemble.1 = f32[1,2,64,1024]{3,2,1,0:T(8,128)} custom-call(s32[1]{0:T(128)} %bitcast.rank, f32[2,32,1024]{2,1,0:T(8,128)S(1)} %copy-done, bf16[64,1024]{1,0:T(8,128)(2,1)S(1)} %collective-permute-done.2.after.other, bf16[2,1024]{1,0:T(2,128)(2,1)S(1)} %collective-permute-done.3.special), custom_call_target="tpu_custom_call" | custom-call | flops 16777216 | bytes 1048576 | tf_op jit(solution)/shard_map/assemble/pallas_call | solution.py:582
  63.5 7.1 %all-to-all-done.1.arrived = bf16[32,64,128]{2,1,0:T(8,128)(2,1)S(1)} async-done(((bf16[32,64,128]{2,1,0:T(8,128)(2,1)}), bf16[32,64,128]{2,1,0:T(8,128)(2,1)S(1)}, u32[]{:S(2)}, u32[]{:S(2)}) %all-to-all-start.1) | async-done | bytes 524320 | tf_op jit(solution)/shard_map/all_to_all | solution.py:575
  70.6 1.7 %results.1 = (bf16[2,64,1024]{2,1,0:T(8,128)(2,1)}, bf16[2,64,1024]{2,1,0:T(8,128)(2,1)}, bf16[2,64,1024]{2,1,0:T(8,128)(2,1)}) custom-call(bf16[32,64,128]{2,1,0:T(8,128)(2,1)S(1)} %all-to-all-done.1.arrived, bf16[1024,1024]{1,0:T(8,128)(2,1)S(1)} %get-tuple-element.29.table, bf16[3,2,64,1024]{3,2,1,0:T(8,128)(2,1)S(1)} %get-tuple-element.30.gates), custom_call_target="tpu_custom_call" | custom-call | flops 536870912 | bytes 1048576 | tf_op jit(solution)/shard_map/results/pallas_call | solution.py:592
  (1 shorter events, 0.0 us)
Async XLA Ops:
  1.7 25.1 %collective-permute-start = (bf16[64,1024]{1,0:T(8,128)(2,1)S(1)}, bf16[64,1024]{1,0:T(8,128)(2,1)S(1)}, u32[]{:S(2)}, u32[]{:S(2)}) collective-permute-start(bf16[64,1024]{1,0:T(8,128)(2,1)S(1)} %bitcast.7), channel_id=1, source_target_pairs={{0,15},{1,14},{2,13},{3,12},{4,11},{5,10},{6,9},{7,8},{8,7},{9,6},... | collective-permute-start | bytes 393224 | tf_op jit(solution)/shard_map/ppermute | solution.py:484
  16.5 20.9 %all-to-all-start = ((bf16[32,64,128]{2,1,0:T(8,128)(2,1)}), bf16[32,64,128]{2,1,0:T(8,128)(2,1)S(1)}, u32[]{:S(2)}, u32[]{:S(2)}) async-start(bf16[32,64,128]{2,1,0:T(8,128)(2,1)} %bitcast.6), calls=%async_computation | async-start | bytes 1048576 | tf_op jit(solution)/shard_map/all_to_all | solution.py:514
  22.0 15.3 %copy-start.2 = (f32[2,1024]{1,0:T(2,128)S(1)}, f32[2,1024]{1,0:T(2,128)}, u32[]{:S(2)}) copy-start(f32[2,1024]{1,0:T(2,128)} %constant.20.clone.half) | copy-start | bytes 24580
  22.0 7.8 %collective-permute-start.1 = (bf16[2,1024]{1,0:T(2,128)(2,1)S(1)}, bf16[2,1024]{1,0:T(2,128)(2,1)S(1)}, u32[]{:S(2)}, u32[]{:S(2)}) collective-permute-start(bf16[2,1024]{1,0:T(2,128)(2,1)S(1)} %get-tuple-element.21), channel_id=1, source_target_pairs={{1,15},{2,14},{3,13},{4,12},{5,11},{6,10},{7,9},{9,7},{10,6},{11,5... | collective-permute-start | bytes 12296 | tf_op jit(solution)/shard_map/ppermute | solution.py:513
  28.5 1.3 %copy-start.3 = (bf16[1024,1024]{1,0:T(8,128)(2,1)}, bf16[1024,1024]{1,0:T(8,128)(2,1)S(1)}, u32[]{:S(2)}) copy-start(bf16[1024,1024]{1,0:T(8,128)(2,1)S(1)} %bring_near.2.tables) | copy-start | bytes 6291460
  32.3 15.5 %copy-start.1 = (f32[1024,1]{1,0:T(8,128)S(1)}, f32[1024,1]{1,0:T(8,128)}, u32[]{:S(2)}) copy-start(f32[1024,1]{1,0:T(8,128)} %constant.21.clone.half) | copy-start | bytes 12292
  37.4 1.6 %copy-start.4 = (bf16[1024,1024]{1,0:T(8,128)(2,1)S(1)}, bf16[1024,1024]{1,0:T(8,128)(2,1)}, u32[]{:S(2)}) copy-start(bf16[1024,1024]{1,0:T(8,128)(2,1)} %copy-done.3) | copy-start | bytes 6291460
  40.6 19.6 %collective-permute-start.2 = (bf16[64,1024]{1,0:T(8,128)(2,1)S(1)}, bf16[64,1024]{1,0:T(8,128)(2,1)S(1)}, u32[]{:S(2)}, u32[]{:S(2)}) collective-permute-start(bf16[64,1024]{1,0:T(8,128)(2,1)S(1)} %get-tuple-element.28), channel_id=1, source_target_pairs={{0,15},{1,14},{2,13},{3,12},{4,11},{5,10},{6,9},{7,8},{8,7},{9,6},... | collective-permute-start | bytes 393224 | tf_op jit(solution)/shard_map/ppermute | solution.py:559
  50.2 20.4 %all-to-all-start.1 = ((bf16[32,64,128]{2,1,0:T(8,128)(2,1)}), bf16[32,64,128]{2,1,0:T(8,128)(2,1)S(1)}, u32[]{:S(2)}, u32[]{:S(2)}) async-start(bf16[32,64,128]{2,1,0:T(8,128)(2,1)} %bitcast.4), calls=%async_computation.1 | async-start | bytes 1048576 | tf_op jit(solution)/shard_map/all_to_all | solution.py:575
  55.2 6.8 %copy-start = (f32[2,32,1024]{2,1,0:T(8,128)S(1)}, f32[2,32,1024]{2,1,0:T(8,128)}, u32[]{:S(2)}) copy-start(f32[2,32,1024]{2,1,0:T(8,128)} %get-tuple-element.34.own) | copy-start | bytes 786436
  55.3 6.7 %collective-permute-start.3 = (bf16[2,1024]{1,0:T(2,128)(2,1)S(1)}, bf16[2,1024]{1,0:T(2,128)(2,1)S(1)}, u32[]{:S(2)}, u32[]{:S(2)}) collective-permute-start(bf16[2,1024]{1,0:T(2,128)(2,1)S(1)} %get-tuple-element.35), channel_id=1, source_target_pairs={{1,15},{2,14},{3,13},{4,12},{5,11},{6,10},{7,9},{9,7},{10,6},{11,5... | collective-permute-start | bytes 12296 | tf_op jit(solution)/shard_map/ppermute | solution.py:560

commit v2 on v1

--- a/solution.py
+++ b/solution.py
@@ -59,12 +59,19 @@
     place = np.arange(N).reshape(1, N, 1)
     phase = (rows * place % TOTAL).astype(np.float64) * (2.0 * np.pi / TOTAL)
     cos, sin = np.cos(phase), np.sin(phase)
+    sin[0, :, 0] = packed_turn()
     return np.concatenate([cos, cos, sin, sin], axis=2).astype(np.float32)
 
 
 def half_turn():
     phase = np.arange(N) * (np.pi / N)
     return np.cos(phase), np.sin(phase)
+
+
+def packed_turn():
+    cos, sin = half_turn()
+    middle = np.abs(np.arange(N) - N // 2 + 0.5) < N // 4
+    return np.where(middle, -1.0 / np.where(middle, sin, 1.0), 1.0 / np.where(middle, 1.0, cos))
 
 
 def lanes_of(shape):
@@ -109,19 +116,25 @@
         filt.at[0, :, pl.ds(0, 8)], lines, sems.at[9 + 2 * BLOCKS]
     )
     start_all(gate_copies + table_copies[:1] + [turn_copy] + table_copies[1:] + [row_copy])
+    middle = N // 2
     for copy in gate_copies:
         copy.wait()
     for chan in range(2):
         gated = gates[0, chan].astype(F32) * gates[1, chan].astype(F32)
         conv = gates[3, chan].astype(F32) * gates[2, chan].astype(F32)
-        signals[128 * chan : 128 * chan + 64, :] = gated.astype(BF)
-        signals[128 * chan + 64 : 128 * chan + 128, :] = conv.astype(BF)
+        for part in range(2):
+            base = 256 * part + 128 * chan
+            lanes = slice(middle * part, middle * part + middle)
+            signals[base : base + 64, :] = gated[:, lanes].astype(BF)
+            signals[base + 64 : base + 128, :] = conv[:, lanes].astype(BF)
     out_copies = []
     for block, rows in enumerate(blocks):
         table_copies[block].wait()
-        section = lax.dot_general(
+        halves = lax.dot_general(
             sections[rows, :], signals[...], NT, preferred_element_type=F32
         )
+        odd_rows = (rows_of((WIDE, 1)) + (block >= BLOCKS // 2)) % 2
+        section = halves[:, :256] + (1 - 2 * odd_rows).astype(F32) * halves[:, 256:]
         if block == 0:
             turn_copy.wait()
         for pair in range(2):
@@ -162,10 +175,14 @@
     return jnp.concatenate(parts, axis=1)
 
 
-def near_kernel_one(after, table, table_out, sems):
-    copy = pltpu.make_async_copy(table, table_out, sems.at[0])
-    copy.start()
-    copy.wait()
+def table_kernel(after, *refs):
+    copies = [
+        pltpu.make_async_copy(refs[0].at[which], refs[1 + which], refs[-1].at[which])
+        for which in range(4)
+    ]
+    start_all(copies)
+    for copy in copies:
+        copy.wait()
 
 
 def near_kernel(after, table, first, second, third, table_out, stack, sems):
@@ -176,22 +193,6 @@
     start_all(copies)
     for copy in copies:
         copy.wait()
-
-
-def bring_near(after, table, *others):
-    shapes = [pltpu.VMEM(table.shape, table.dtype)]
-    if others:
-        shapes.append(pltpu.VMEM((len(others),) + others[0].shape, others[0].dtype))
-    return pl.pallas_call(
-        near_kernel if others else near_kernel_one,
-        out_shape=shapes,
-        in_specs=[HBM] * (2 + len(others)),
-        out_specs=[VMEM] * len(shapes),
-        scratch_shapes=[pltpu.SemaphoreType.DMA((1 + len(others),))],
-        compiler_params=params(16),
-        cost_estimate=sizes(W_COST),
-        name="bring_near",
-    )(after, kept(table), *[kept(value) for value in others])
 
 
 def filter_kernel(rank, own, other, special, out, mine, sem):
@@ -224,15 +225,14 @@
 
 
 def spectrum_kernel(
-    rank, turned, tables, filt_far, turn_far, half,
-    spec, grad, grad_low, grad_row, tables_out, filt, turn, left, sems
+    rank, turned, cos_0, cos_1, sin_0, sin_1, filt_far, turn_far, half,
+    spec, grad, grad_low, grad_row, filt, turn, left, sems
 ):
     me = rank[0]
     middle = N // 2
     copies = [
-        pltpu.make_async_copy(tables, tables_out, sems.at[0]),
-        pltpu.make_async_copy(filt_far, filt, sems.at[1]),
-        pltpu.make_async_copy(turn_far.at[me], turn, sems.at[2]),
+        pltpu.make_async_copy(filt_far, filt, sems.at[0]),
+        pltpu.make_async_copy(turn_far.at[me], turn, sems.at[1]),
     ]
     start_all(copies)
     for seq in range(2):
@@ -270,7 +270,10 @@
     sign = alternating((1, WIDE)).astype(F32)
     for block in range(BLOCKS):
         wide = slice(WIDE * block, WIDE * block + WIDE)
-        halves = jnp.dot(left[...], tables[:, wide], preferred_element_type=F32)
+        pieces = [table[:, wide] for table in (cos_0, cos_1, sin_0, sin_1)]
+        halves = jnp.dot(
+            left[...], jnp.concatenate(pieces, axis=0), preferred_element_type=F32
+        )
         result = halves[:272] + sign * halves[272:]
         spec[:, wide] = result.astype(BF)
         real = 0.0
@@ -310,7 +313,9 @@
     )
 
 
-def inverse_kernel(rank, spec, filt, tables, turn, half, grad, out, grad_far, total, sem):
+def inverse_kernel(
+    rank, spec, filt, cos_0, cos_1, sin_0, sin_1, turn, grad, out, grad_far, total, sem
+):
     me = rank[0]
     copy = pltpu.make_async_copy(grad, grad_far, sem)
     copy.start()
@@ -362,9 +367,8 @@
             crossing = joined(less, crossed)
             for quarter in parts:
                 rows = slice(WIDE * quarter, WIDE * quarter + WIDE)
-                start = WIDE * (quarter % 2)
-                cos = tables[start : start + WIDE, wide]
-                sin = tables[N // 2 + start : N // 2 + start + WIDE, wide]
+                cos = (cos_0, cos_1)[quarter % 2][:, wide]
+                sin = (sin_0, sin_1)[quarter % 2][:, wide]
                 if quarter >= 2:
                     cos, sin = cos * sign, sin * sign
                 part = lax.dot_general(
@@ -383,7 +387,7 @@
         un_re = real * turn_cos - imag * turn_sin
         un_im = real * turn_sin + imag * turn_cos
         packed = jnp.logical_and(lanes_of((WIDE, 128)) % SLOTS == 0, me == 0)
-        un_im = jnp.where(packed, imag * half[rows, 0:1], 2.0 * un_im).astype(BF)
+        un_im = jnp.where(packed, imag * turn_sin, 2.0 * un_im).astype(BF)
         un_re = jnp.where(packed, real, 2.0 * un_re).astype(BF)
         out[0, rows, :] = jnp.concatenate([un_re[:, :64], un_im[:, :64]], axis=1)
         out[1, rows, :] = jnp.concatenate([un_re[:, 64:], un_im[:, 64:]], axis=1)
@@ -463,16 +467,14 @@
 
 def local(input_proj, value_proj, output_proj, grad_out, filter_spectrum):
     cos64, sin64 = dft_tables()
-    half_tables = np.concatenate([cos64[: N // 2], sin64[: N // 2]]).astype(ml_dtypes.bfloat16)
-    half_tables = jnp.asarray(half_tables)
-    sections = jnp.asarray(section_table())
+    half_tables = np.concatenate([cos64[: N // 2], sin64[: N // 2]]).reshape(4, WIDE, N)
+    half_tables = jnp.asarray(half_tables.astype(ml_dtypes.bfloat16))
+    sections = section_table()
+    half_sections = jnp.asarray(sections[:, : N // 2])
+    sections = jnp.asarray(sections)
     turn_out = jnp.asarray(forward_turn())
     turn_back = jnp.asarray(inverse_turn())
     half_rows = jnp.asarray(np.stack(half_turn()).astype(np.float32))
-    cosine, sine = half_turn()
-    middle = np.abs(np.arange(N) - N // 2 + 0.5) < N // 4
-    spread = np.where(middle, -1.0 / np.where(middle, sine, 1.0), 1.0 / np.where(middle, 1.0, cosine))
-    half_columns = jnp.asarray(spread[:, None].astype(np.float32))
     ctx_rank = lax.axis_index("ctx")
     rank = ctx_rank.astype(jnp.int32).reshape(1)
     half_ranks = RANKS // 2
@@ -490,10 +492,10 @@
         out_specs=[HBM, VMEM],
         scratch_shapes=[
             pltpu.VMEM((4, 2, ROWS, N), BF),
-            pltpu.VMEM((N, N), BF),
+            pltpu.VMEM((N, N // 2), BF),
             pltpu.VMEM((N // 2, 128), F32),
             pltpu.VMEM((2, RANKS, ROWS, 128), BF),
-            pltpu.VMEM((256, N), BF),
+            pltpu.VMEM((512, N // 2), BF),
             pltpu.VMEM((2, 8, N), F32),
             pltpu.SemaphoreType.DMA((10 + 2 * BLOCKS,)),
         ],
@@ -506,7 +508,7 @@
         kept(value_proj),
         kept(output_proj),
         kept(grad_out),
-        kept(sections),
+        kept(half_sections),
         kept(turn_out),
         kept(filter_spectrum),
     )
@@ -515,7 +517,16 @@
         turned.reshape(2 * RANKS, ROWS, 128), ("core", "ctx"), 0, 0, tiled=True
     )
 
-    (tables,) = bring_near(other_rows, half_tables)
+    tables = pl.pallas_call(
+        table_kernel,
+        out_shape=[pltpu.VMEM((WIDE, N), BF)] * 4,
+        in_specs=[HBM] * 2,
+        out_specs=[VMEM] * 4,
+        scratch_shapes=[pltpu.SemaphoreType.DMA((4,))],
+        compiler_params=params(16),
+        cost_estimate=sizes(W_COST),
+        name="bring_tables",
+    )(other_rows, kept(half_tables))
     folded_filter = pl.pallas_call(
         filter_kernel,
         out_shape=pltpu.HBM((2, 40, N), F32),
@@ -527,22 +538,21 @@
         name="fold_filter",
     )(rank, kept(filter_spectrum), other_rows, other_row)
 
-    spectra, grad_own, grad_low, grad_row, tables_again, filter_near, turn_near = pl.pallas_call(
+    spectra, grad_own, grad_low, grad_row, filter_near, turn_near = pl.pallas_call(
         spectrum_kernel,
         out_shape=[
             pltpu.VMEM((272, N), BF),
             pltpu.VMEM((2, SLOTS, N), F32),
             pltpu.VMEM((2 * SLOTS, N), BF),
             pltpu.VMEM((2, N), BF),
-            pltpu.VMEM((N, N), BF),
             pltpu.VMEM((2, 40, N), F32),
             pltpu.VMEM((N, 128), F32),
         ],
-        in_specs=[SMEM, VMEM, VMEM, HBM, HBM, VMEM],
-        out_specs=[VMEM] * 7,
+        in_specs=[SMEM] + [VMEM] * 5 + [HBM, HBM, VMEM],
+        out_specs=[VMEM] * 6,
         scratch_shapes=[
             pltpu.VMEM((544, N), BF),
-            pltpu.SemaphoreType.DMA((3,)),
+            pltpu.SemaphoreType.DMA((2,)),
         ],
         compiler_params=params(20),
         cost_estimate=sizes(B_COST),
@@ -550,7 +560,7 @@
     )(
         rank,
         arrived,
-        pltpu.with_memory_space_constraint(tables, pltpu.VMEM),
+        *tables,
         kept(folded_filter),
         kept(turn_back),
         half_rows,
@@ -565,20 +575,27 @@
             jax.ShapeDtypeStruct((2, N, 128), BF),
             pltpu.HBM((2, SLOTS, N), F32),
         ],
-        in_specs=[SMEM] + [VMEM] * 6,
+        in_specs=[SMEM] + [VMEM] * 8,
         out_specs=[VMEM, HBM],
         scratch_shapes=[pltpu.VMEM((N, 256), F32), pltpu.SemaphoreType.DMA(())],
         compiler_params=params(24),
         cost_estimate=sizes(B_COST),
         name="inverse",
-    )(rank, spectra, filter_near, tables_again, turn_near, half_columns, grad_own)
+    )(rank, spectra, filter_near, *tables, turn_near, grad_own)
     returned = lax.all_to_all(
         unturned.reshape(2 * RANKS, ROWS, 128), ("core", "ctx"), 0, 0, tiled=True
     )
 
-    sections_near, gates_near = bring_near(
-        mirror_grad, sections, input_proj, value_proj, grad_out
-    )
+    sections_near, gates_near = pl.pallas_call(
+        near_kernel,
+        out_shape=[pltpu.VMEM((N, N), BF), pltpu.VMEM((3, 2, ROWS, N), BF)],
+        in_specs=[HBM] * 5,
+        out_specs=[VMEM] * 2,
+        scratch_shapes=[pltpu.SemaphoreType.DMA((4,))],
+        compiler_params=params(16),
+        cost_estimate=sizes(W_COST),
+        name="bring_near",
+    )(mirror_grad, kept(sections), kept(input_proj), kept(value_proj), kept(grad_out))
     grad_filter = pl.pallas_call(
         assemble_kernel,
         out_shape=jax.ShapeDtypeStruct((1, 2, ROWS, N), F32),

time: 72.9 us -> 70.9 us (0.973)
  local copies, waits for them, and re-layouts: 2.96 us -> 0.02 us
  waiting for transfers between devices: 12.1 us -> 13.5 us
    unnamed x10 -> x4, local copies, waits for them, and re-layouts: 2.95 us -> 0.01 us
    all_to_all x1, waiting for transfers between devices: 5.02 us -> 6.42 us  [local(): lax.all_to_all(turned.reshape(2 * RANKS, ROWS, 128), ('core', 'ctx'), 0,...]
where the time goes in v2:
time: 70.9 us; the launch traced here: 70.3 us
  starting transfers between devices  38.1 us (54%)
  Pallas kernels  16.7 us (24%)
  waiting for transfers between devices  13.5 us (19%)
  other arithmetic  1.07 us (2%)
  between operations  0.8 us (1%)
    ppermute x1, starting transfers between devices, local(): lax.ppermute(filter_rows.reshape(2 * SLOTS, N), 'ctx', mirror_of)  10.6 us
    ppermute x1, starting transfers between devices, local(): mirror_grad = lax.ppermute(grad_low, 'ctx', mirror_of)  7.13 us
    all_to_all x1, waiting for transfers between devices, local(): lax.all_to_all(unturned.reshape(2 * RANKS, ROWS, 128), ('core', 'ctx'), 0...  7.11 us
    all_to_all x1, waiting for transfers between devices, local(): lax.all_to_all(turned.reshape(2 * RANKS, ROWS, 128), ('core', 'ctx'), 0,...  6.42 us
    all_to_all x1, starting transfers between devices, local(): lax.all_to_all(turned.reshape(2 * RANKS, ROWS, 128), ('core', 'ctx'), 0,...  5.53 us
    all_to_all x1, starting transfers between devices, local(): lax.all_to_all(unturned.reshape(2 * RANKS, ROWS, 128), ('core', 'ctx'), 0...  5.06 us
    ppermute x1, starting transfers between devices, local(): mirror_row = lax.ppermute(grad_row, 'ctx', special_of)  4.93 us
    ppermute x1, starting transfers between devices, local(): other_row = lax.ppermute(filter_row, 'ctx', special_of)  4.8 us
  transfers between devices with their start and end apart: 6, of which 2 were waited for; matrix products, arithmetic and copies ran while one was open for 0% of the time, Pallas kernels for 19%

profile of v2, /device:TPU:1, one launch (start us, length us, event | category | flops | bytes accessed | tf_op | source)
XLA Modules:
  0.0 70.3 jit_solution(17788281336748303729)
XLA Ops:
  0.6 1.1 %convert_bitcast_fusion = bf16[2,64,1024]{2,1,0:T(8,128)(2,1)S(1)} fusion(f32[1,2,64,1024]{3,2,1,0:T(8,128)} %own.1), kind=kLoop, calls=%fused_computation | loop fusion | flops 131072 | bytes 786432 | tf_op jit(solution)/shard_map/reshape | solution.py:485
  1.7 10.6 %collective-permute-start = (bf16[64,1024]{1,0:T(8,128)(2,1)S(1)}, bf16[64,1024]{1,0:T(8,128)(2,1)S(1)}, u32[]{:S(2)}, u32[]{:S(2)}) collective-permute-start(bf16[64,1024]{1,0:T(8,128)(2,1)S(1)} %bitcast.7), channel_id=1, source_target_pairs={{0,15},{1,14},{2,13},{3,12},{4,11},{5,10},{6,9},{7,8},{8,7},{9,6},... | collective-permute-start | bytes 393224 | tf_op jit(solution)/shard_map/ppermute | solution.py:486
  12.4 3.6 %sections.1 = (bf16[2,16,64,128]{3,2,1,0:T(8,128)(2,1)}, bf16[2,1024]{1,0:T(2,128)(2,1)S(1)}) custom-call(s32[1]{0:T(128)} %bitcast.rank, bf16[2,64,1024]{2,1,0:T(8,128)(2,1)} %first.1, bf16[2,64,1024]{2,1,0:T(8,128)(2,1)} %second.1, bf16[2,64,1024]{2,1,0:T(8,128)(2,1)} %outp.1, bf16[2,64,1024]{2,1,0:T(8,128)(2,1)} %third.1, ...), custom_call_target="tpu_custom_call" | custom-call | flops 10000000000 | bytes 1048576 | tf_op jit(solution)/shard_map/sections/pallas_call | solution.py:488
  16.0 5.5 %all-to-all-start = ((bf16[32,64,128]{2,1,0:T(8,128)(2,1)}), bf16[32,64,128]{2,1,0:T(8,128)(2,1)S(1)}, u32[]{:S(2)}, u32[]{:S(2)}) async-start(bf16[32,64,128]{2,1,0:T(8,128)(2,1)} %bitcast.6), calls=%async_computation | async-start | bytes 1048576 | tf_op jit(solution)/shard_map/all_to_all | solution.py:516
  21.6 0.0 copy-start.1
  21.6 4.8 %collective-permute-start.1 = (bf16[2,1024]{1,0:T(2,128)(2,1)S(1)}, bf16[2,1024]{1,0:T(2,128)(2,1)S(1)}, u32[]{:S(2)}, u32[]{:S(2)}) collective-permute-start(bf16[2,1024]{1,0:T(2,128)(2,1)S(1)} %get-tuple-element.28), channel_id=1, source_target_pairs={{1,15},{2,14},{3,13},{4,12},{5,11},{6,10},{7,9},{9,7},{10,6},{11,5... | collective-permute-start | bytes 12296 | tf_op jit(solution)/shard_map/ppermute | solution.py:515
  26.4 0.0 collective-permute-done.after.other
  26.4 1.6 %bring_tables.1 = (bf16[256,1024]{1,0:T(8,128)(2,1)S(1)}, bf16[256,1024]{1,0:T(8,128)(2,1)S(1)}, bf16[256,1024]{1,0:T(8,128)(2,1)S(1)}, bf16[256,1024]{1,0:T(8,128)(2,1)S(1)}) custom-call(bf16[64,1024]{1,0:T(8,128)(2,1)S(1)} %collective-permute-done.after.other, bf16[4,256,1024]{2,1,0:T(8,128)(2,1)} %constant.16.clone.refs_0_), custom_call_target="tpu_custom_call" | custom-call | flops 40000000000 | bytes 1048576 | tf_op jit(solution)/shard_map/bring_tables/pallas_call | solution.py:520
  28.0 0.0 collective-permute-done.1.special
  28.0 2.5 %fold_filter.1.filt_far = f32[2,40,1024]{2,1,0:T(8,128)} custom-call(s32[1]{0:T(128)} %bitcast.rank, f32[1,2,64,1024]{3,2,1,0:T(8,128)} %own.1, bf16[64,1024]{1,0:T(8,128)(2,1)S(1)} %collective-permute-done.after.other, bf16[2,1024]{1,0:T(2,128)(2,1)S(1)} %collective-permute-done.1.special), custom_call_target="tpu_custom_call" | custom-call | flops 16777216 | bytes 1048576 | tf_op jit(solution)/shard_map/fold_filter/pallas_call | solution.py:530
  30.5 6.4 %all-to-all-done.turned = bf16[32,64,128]{2,1,0:T(8,128)(2,1)S(1)} async-done(((bf16[32,64,128]{2,1,0:T(8,128)(2,1)}), bf16[32,64,128]{2,1,0:T(8,128)(2,1)S(1)}, u32[]{:S(2)}, u32[]{:S(2)}) %all-to-all-start) | async-done | bytes 524320 | tf_op jit(solution)/shard_map/all_to_all | solution.py:516
  36.9 0.0 copy-done.1
  36.9 1.8 %spectra.1 = (bf16[272,1024]{1,0:T(8,128)(2,1)S(1)}, f32[2,32,1024]{2,1,0:T(8,128)S(1)}, bf16[64,1024]{1,0:T(8,128)(2,1)S(1)}, bf16[2,1024]{1,0:T(2,128)(2,1)S(1...) custom-call(s32[1]{0:T(128)} %bitcast.rank, bf16[32,64,128]{2,1,0:T(8,128)(2,1)S(1)} %all-to-all-done.turned, ...), custom_call_target="tpu_custom_call" | custom-call | flops 10000000000 | bytes 1048576 | tf_op jit(solution)/shard_map/spectra/pallas_call | solution.py:541
  38.7 7.1 %collective-permute-start.2 = (bf16[64,1024]{1,0:T(8,128)(2,1)S(1)}, bf16[64,1024]{1,0:T(8,128)(2,1)S(1)}, u32[]{:S(2)}, u32[]{:S(2)}) collective-permute-start(bf16[64,1024]{1,0:T(8,128)(2,1)S(1)} %get-tuple-element.34), channel_id=1, source_target_pairs={{0,15},{1,14},{2,13},{3,12},{4,11},{5,10},{6,9},{7,8},{8,7},{9,6},... | collective-permute-start | bytes 393224 | tf_op jit(solution)/shard_map/ppermute | solution.py:569
  45.8 2.3 %inverse.1 = (bf16[2,1024,128]{2,1,0:T(8,128)(2,1)}, f32[2,32,1024]{2,1,0:T(8,128)}) custom-call(s32[1]{0:T(128)} %bitcast.rank, bf16[272,1024]{1,0:T(8,128)(2,1)S(1)} %get-tuple-element.29.spec, f32[2,40,1024]{2,1,0:T(8,128)S(1)} %get-tuple-element.30.filt, bf16[256,1024]{1,0:T(8,128)(2,1)S(1)} %get-tuple-element.24.cos_0, ...), custom_call_target="tpu_custom_call" | custom-call | flops 10000000000 | bytes 1048576 | tf_op jit(solution)/shard_map/inverse/pallas_call | solution.py:572
  48.2 5.1 %all-to-all-start.1 = ((bf16[32,64,128]{2,1,0:T(8,128)(2,1)}), bf16[32,64,128]{2,1,0:T(8,128)(2,1)S(1)}, u32[]{:S(2)}, u32[]{:S(2)}) async-start(bf16[32,64,128]{2,1,0:T(8,128)(2,1)} %bitcast.4), calls=%async_computation.1 | async-start | bytes 1048576 | tf_op jit(solution)/shard_map/all_to_all | solution.py:585
  53.2 0.0 copy-start
  53.2 4.9 %collective-permute-start.3 = (bf16[2,1024]{1,0:T(2,128)(2,1)S(1)}, bf16[2,1024]{1,0:T(2,128)(2,1)S(1)}, u32[]{:S(2)}, u32[]{:S(2)}) collective-permute-start(bf16[2,1024]{1,0:T(2,128)(2,1)S(1)} %get-tuple-element.41), channel_id=1, source_target_pairs={{1,15},{2,14},{3,13},{4,12},{5,11},{6,10},{7,9},{9,7},{10,6},{11,5... | collective-permute-start | bytes 12296 | tf_op jit(solution)/shard_map/ppermute | solution.py:570
  58.2 0.0 collective-permute-done.2.after.other
  58.2 1.8 %bring_near.1 = (bf16[1024,1024]{1,0:T(8,128)(2,1)S(1)}, bf16[3,2,64,1024]{3,2,1,0:T(8,128)(2,1)S(1)}) custom-call(bf16[64,1024]{1,0:T(8,128)(2,1)S(1)} %collective-permute-done.2.after.other, bf16[1024,1024]{1,0:T(8,128)(2,1)} %constant.18.clone.table, bf16[2,64,1024]{2,1,0:T(8,128)(2,1)} %first.1, bf16[2,64,1024]{2,1,0:T(8,128)(2,1)} %second.1, ...), custom_call_target="tpu_custom_call" | custom-call | flops 40000000000 | bytes 1048576 | tf_op jit(solution)/shard_map/bring_near/pallas_call | solution.py:589
  60.0 0.0 collective-permute-done.3.special
  60.0 0.0 copy-done
  60.0 1.4 %assemble.1 = f32[1,2,64,1024]{3,2,1,0:T(8,128)} custom-call(s32[1]{0:T(128)} %bitcast.rank, f32[2,32,1024]{2,1,0:T(8,128)S(1)} %copy-done, bf16[64,1024]{1,0:T(8,128)(2,1)S(1)} %collective-permute-done.2.after.other, bf16[2,1024]{1,0:T(2,128)(2,1)S(1)} %collective-permute-done.3.special), custom_call_target="tpu_custom_call" | custom-call | flops 16777216 | bytes 1048576 | tf_op jit(solution)/shard_map/assemble/pallas_call | solution.py:599
  61.4 7.1 %all-to-all-done.1.arrived = bf16[32,64,128]{2,1,0:T(8,128)(2,1)S(1)} async-done(((bf16[32,64,128]{2,1,0:T(8,128)(2,1)}), bf16[32,64,128]{2,1,0:T(8,128)(2,1)S(1)}, u32[]{:S(2)}, u32[]{:S(2)}) %all-to-all-start.1) | async-done | bytes 524320 | tf_op jit(solution)/shard_map/all_to_all | solution.py:585
  68.6 1.7 %results.1 = (bf16[2,64,1024]{2,1,0:T(8,128)(2,1)}, bf16[2,64,1024]{2,1,0:T(8,128)(2,1)}, bf16[2,64,1024]{2,1,0:T(8,128)(2,1)}) custom-call(bf16[32,64,128]{2,1,0:T(8,128)(2,1)S(1)} %all-to-all-done.1.arrived, bf16[1024,1024]{1,0:T(8,128)(2,1)S(1)} %get-tuple-element.35.table, bf16[3,2,64,1024]{3,2,1,0:T(8,128)(2,1)S(1)} %get-tuple-element.36.gates), custom_call_target="tpu_custom_call" | custom-call | flops 536870912 | bytes 1048576 | tf_op jit(solution)/shard_map/results/pallas_call | solution.py:609
  (1 shorter events, 0.0 us)
Async XLA Ops:
  1.7 24.7 %collective-permute-start = (bf16[64,1024]{1,0:T(8,128)(2,1)S(1)}, bf16[64,1024]{1,0:T(8,128)(2,1)S(1)}, u32[]{:S(2)}, u32[]{:S(2)}) collective-permute-start(bf16[64,1024]{1,0:T(8,128)(2,1)S(1)} %bitcast.7), channel_id=1, source_target_pairs={{0,15},{1,14},{2,13},{3,12},{4,11},{5,10},{6,9},{7,8},{8,7},{9,6},... | collective-permute-start | bytes 393224 | tf_op jit(solution)/shard_map/ppermute | solution.py:486
  16.0 20.9 %all-to-all-start = ((bf16[32,64,128]{2,1,0:T(8,128)(2,1)}), bf16[32,64,128]{2,1,0:T(8,128)(2,1)S(1)}, u32[]{:S(2)}, u32[]{:S(2)}) async-start(bf16[32,64,128]{2,1,0:T(8,128)(2,1)} %bitcast.6), calls=%async_computation | async-start | bytes 1048576 | tf_op jit(solution)/shard_map/all_to_all | solution.py:516
  21.6 15.3 %copy-start.1 = (f32[2,1024]{1,0:T(2,128)S(1)}, f32[2,1024]{1,0:T(2,128)}, u32[]{:S(2)}) copy-start(f32[2,1024]{1,0:T(2,128)} %constant.21.clone.half) | copy-start | bytes 24580
  21.6 6.4 %collective-permute-start.1 = (bf16[2,1024]{1,0:T(2,128)(2,1)S(1)}, bf16[2,1024]{1,0:T(2,128)(2,1)S(1)}, u32[]{:S(2)}, u32[]{:S(2)}) collective-permute-start(bf16[2,1024]{1,0:T(2,128)(2,1)S(1)} %get-tuple-element.28), channel_id=1, source_target_pairs={{1,15},{2,14},{3,13},{4,12},{5,11},{6,10},{7,9},{9,7},{10,6},{11,5... | collective-permute-start | bytes 12296 | tf_op jit(solution)/shard_map/ppermute | solution.py:515
  38.7 19.5 %collective-permute-start.2 = (bf16[64,1024]{1,0:T(8,128)(2,1)S(1)}, bf16[64,1024]{1,0:T(8,128)(2,1)S(1)}, u32[]{:S(2)}, u32[]{:S(2)}) collective-permute-start(bf16[64,1024]{1,0:T(8,128)(2,1)S(1)} %get-tuple-element.34), channel_id=1, source_target_pairs={{0,15},{1,14},{2,13},{3,12},{4,11},{5,10},{6,9},{7,8},{8,7},{9,6},... | collective-permute-start | bytes 393224 | tf_op jit(solution)/shard_map/ppermute | solution.py:569
  48.2 20.4 %all-to-all-start.1 = ((bf16[32,64,128]{2,1,0:T(8,128)(2,1)}), bf16[32,64,128]{2,1,0:T(8,128)(2,1)S(1)}, u32[]{:S(2)}, u32[]{:S(2)}) async-start(bf16[32,64,128]{2,1,0:T(8,128)(2,1)} %bitcast.4), calls=%async_computation.1 | async-start | bytes 1048576 | tf_op jit(solution)/shard_map/all_to_all | solution.py:585
  53.2 6.8 %copy-start = (f32[2,32,1024]{2,1,0:T(8,128)S(1)}, f32[2,32,1024]{2,1,0:T(8,128)}, u32[]{:S(2)}) copy-start(f32[2,32,1024]{2,1,0:T(8,128)} %get-tuple-element.40.own) | copy-start | bytes 786436
  53.2 6.7 %collective-permute-start.3 = (bf16[2,1024]{1,0:T(2,128)(2,1)S(1)}, bf16[2,1024]{1,0:T(2,128)(2,1)S(1)}, u32[]{:S(2)}, u32[]{:S(2)}) collective-permute-start(bf16[2,1024]{1,0:T(2,128)(2,1)S(1)} %get-tuple-element.41), channel_id=1, source_target_pairs={{1,15},{2,14},{3,13},{4,12},{5,11},{6,10},{7,9},{9,7},{10,6},{11,5... | collective-permute-start | bytes 12296 | tf_op jit(solution)/shard_map/ppermute | solution.py:570

commit v3 on v2

--- a/solution.py
+++ b/solution.py
@@ -195,7 +195,7 @@
         copy.wait()
 
 
-def filter_kernel(rank, own, other, special, out, mine, sem):
+def filter_kernel(rank, own, other, out, mine, sem):
     me = rank[0]
     copy = pltpu.make_async_copy(own.at[0], mine, sem)
     copy.start()
@@ -211,13 +211,16 @@
         moved = jnp.dot(pick, other[32 * part : 32 * part + 32], preferred_element_type=F32)
         mirror = reverse_lanes(moved)
         first = mine[part, 0:8, :]
-        extra = jnp.broadcast_to(special[part : part + 1, :].astype(F32), (8, N))
-        flipped = reverse_lanes(jnp.concatenate([first, extra], axis=0))
-        around = pltpu.roll(flipped[0:8], 1, 1)
-        head = jnp.where(me == 0, around, flipped[8:16])[0:1]
+        flipped = reverse_lanes(jnp.concatenate([first, first], axis=0))
+        head = jnp.where(me == 0, pltpu.roll(flipped[0:8], 1, 1)[0:1], 0.0)
         mirror = jnp.where(jnp.logical_and(top, low), head, mirror)
-        out[part, 0:32, :] = 0.5 * (kept + sign * mirror)
-        out[part, 32:40, :] = 0.5 * (extra + sign * flipped[8:16])
+        out[part] = 0.5 * (kept + sign * mirror)
+
+
+def special_rows(special):
+    rows = [jnp.broadcast_to(special[part : part + 1, :], (8, N)) for part in range(2)]
+    both = jnp.concatenate(rows, axis=0)
+    return both.astype(F32), reverse_lanes(both)
 
 
 def alternating(shape):
@@ -314,19 +317,25 @@
 
 
 def inverse_kernel(
-    rank, spec, filt, cos_0, cos_1, sin_0, sin_1, turn, grad, out, grad_far, total, sem
+    rank, spec, filt, special, cos_0, cos_1, sin_0, sin_1, turn, grad, out, grad_far, total, sem
 ):
     me = rank[0]
     copy = pltpu.make_async_copy(grad, grad_far, sem)
     copy.start()
     outer, inner = (0, 3), (1, 2)
     sign = alternating((1, WIDE)).astype(BF)
-    packed_row = jnp.logical_and(rows_of((SLOTS, WIDE)) == 0, me == 0)
+    top = rows_of((SLOTS, WIDE)) == 0
+    packed_row = jnp.logical_and(top, me == 0)
+    lone, flipped = special_rows(special)
+    lone_re, lone_im = 0.5 * lone[0:1], 0.5 * lone[8:9]
+    flip_re, flip_im = 0.5 * flipped[0:1], -0.5 * flipped[8:9]
+    patched_row = jnp.logical_and(top, jnp.logical_and(me > 0, me < RANKS // 2))
     for block in range(BLOCKS):
         wide = slice(WIDE * block, WIDE * block + WIDE)
         values = spec[:, wide].astype(F32)
-        h_re, h_im = filt[0, 0:32, wide], filt[1, 0:32, wide]
-        x_re, x_im = filt[0, 32:33, wide], filt[1, 32:33, wide]
+        h_re = filt[0, :, wide] + jnp.where(patched_row, flip_re[:, wide], 0.0)
+        h_im = filt[1, :, wide] + jnp.where(patched_row, flip_im[:, wide], 0.0)
+        x_re, x_im = (lone_re + flip_re)[:, wide], (lone_im + flip_im)[:, wide]
         reals, imags, extra_re, extra_im = [], [], [], []
         for seq in range(2):
             base = 64 * seq
@@ -394,41 +403,69 @@
     copy.wait()
 
 
-def result_kernel(arrived, table, gates, d_inp, d_val, d_outp, left, ready, sems):
+def result_kernel(
+    rank, arrived, table, gates, most, first, special,
+    d_inp, d_val, d_outp, d_filt, left, ready, patch, sems
+):
+    me = rank[0]
+    lone, flipped = special_rows(special)
+    top = jnp.logical_and(rows_of((8, N)) == 0, me >= RANKS // 2)
+    for part in range(2):
+        lines = slice(8 * part, 8 * part + 8)
+        sign = 1.0 if part == 0 else -1.0
+        head = jnp.where(me == RANKS // 2, lone[lines], sign * flipped[lines])
+        patch[part] = jnp.where(top, head, first[part])
+    patch_copy = pltpu.make_async_copy(
+        patch, d_filt.at[0, :, pl.ds(0, 8)], sems.at[3 * BLOCKS]
+    )
+    patch_copy.start()
+    half = N // 2
     for chan in range(2):
         for pair in range(RANKS // 2):
             even = arrived[RANKS * chan + 2 * pair]
             odd = arrived[RANKS * chan + 2 * pair + 1]
+            sign = alternating((1, 128)) * (1 if pair < RANKS // 4 else -1)
             for sig in range(2):
                 low = slice(32 * sig, 32 * sig + 32)
                 high = slice(64 + 32 * sig, 96 + 32 * sig)
                 base = 64 * (2 * chan + sig)
-                left[base : base + 64, 128 * pair : 128 * pair + 128] = jnp.concatenate(
+                lanes = slice(128 * pair, 128 * pair + 128)
+                block = jnp.concatenate(
                     [even[:, low], odd[:, low], even[:, high], odd[:, high]], axis=1
                 )
+                left[base : base + 64, lanes] = block
+                left[256 + base : 320 + base, lanes] = block * sign.astype(BF)
     copies = []
-    for block in range(BLOCKS):
-        wide = slice(WIDE * block, WIDE * block + WIDE)
-        result = jnp.dot(left[...], table[:, wide], preferred_element_type=F32) * SCALE
-        for chan in range(2):
-            conv = result[128 * chan : 128 * chan + 64]
-            gated = result[128 * chan + 64 : 128 * chan + 128]
-            ready[2, chan, :, wide] = (gates[2, chan, :, wide].astype(F32) * conv).astype(BF)
-            ready[0, chan, :, wide] = (gated * gates[1, chan, :, wide].astype(F32)).astype(BF)
-            ready[1, chan, :, wide] = (gated * gates[0, chan, :, wide].astype(F32)).astype(BF)
-        for which, target in enumerate((d_inp, d_val, d_outp)):
-            copy = pltpu.make_async_copy(
-                ready.at[which, :, :, pl.ds(WIDE * block, WIDE)],
-                target.at[:, :, pl.ds(WIDE * block, WIDE)],
-                sems.at[3 * block + which],
-            )
-            copy.start()
-            copies.append(copy)
+    for block in range(BLOCKS // 2):
+        near = slice(WIDE * block, WIDE * block + WIDE)
+        halves = jnp.dot(left[...], table[:, near], preferred_element_type=F32) * SCALE
+        for part in range(2):
+            start = half * part + WIDE * block
+            wide = slice(start, start + WIDE)
+            result = halves[256 * part : 256 * part + 256]
+            for chan in range(2):
+                conv = result[128 * chan : 128 * chan + 64]
+                gated = result[128 * chan + 64 : 128 * chan + 128]
+                out_grad = gates[2, chan, :, wide].astype(F32) * conv
+                ready[2, chan, :, wide] = out_grad.astype(BF)
+                in_grad = gated * gates[1, chan, :, wide].astype(F32)
+                ready[0, chan, :, wide] = in_grad.astype(BF)
+                val_grad = gated * gates[0, chan, :, wide].astype(F32)
+                ready[1, chan, :, wide] = val_grad.astype(BF)
+            for which, target in enumerate((d_inp, d_val, d_outp)):
+                copy = pltpu.make_async_copy(
+                    ready.at[which, :, :, pl.ds(start, WIDE)],
+                    target.at[:, :, pl.ds(start, WIDE)],
+                    sems.at[3 * (2 * block + part) + which],
+                )
+                copy.start()
+                copies.append(copy)
     for copy in copies:
         copy.wait()
-
-
-def assemble_kernel(rank, own, other, special, out):
+    patch_copy.wait()
+
+
+def assemble_kernel(rank, own, other, out, first, ready, sem):
     me = rank[0]
     low = me < RANKS // 2
     shape = (SLOTS, SLOTS)
@@ -441,11 +478,15 @@
         shifted = pltpu.roll(mine, 1, 0)
         moved = jnp.dot(pick, other[32 * part : 32 * part + 32], preferred_element_type=F32)
         mirror = sign * reverse_lanes(moved)
-        row = jnp.broadcast_to(special[part : part + 1, :].astype(F32), (16, N))
-        turned = sign * reverse_lanes(row)
-        head = jnp.where(me == RANKS // 2, row, turned)[0:1]
-        out[0, part, 0:32, :] = jnp.where(low, mine, jnp.where(top, head, shifted))
-        out[0, part, 32:64, :] = jnp.where(jnp.logical_and(top, ~low), shifted, mirror)
+        lines = jnp.where(low, mine, shifted)
+        first[part] = lines[0:8]
+        ready[part, 0:32, :] = lines
+        ready[part, 32:64, :] = jnp.where(jnp.logical_and(top, ~low), shifted, mirror)
+    copy = pltpu.make_async_copy(
+        ready.at[:, pl.ds(8, ROWS - 8)], out.at[0, :, pl.ds(8, ROWS - 8)], sem
+    )
+    copy.start()
+    copy.wait()
 
 
 HBM = pl.BlockSpec(memory_space=pltpu.HBM)
@@ -469,9 +510,7 @@
     cos64, sin64 = dft_tables()
     half_tables = np.concatenate([cos64[: N // 2], sin64[: N // 2]]).reshape(4, WIDE, N)
     half_tables = jnp.asarray(half_tables.astype(ml_dtypes.bfloat16))
-    sections = section_table()
-    half_sections = jnp.asarray(sections[:, : N // 2])
-    sections = jnp.asarray(sections)
+    half_sections = jnp.asarray(section_table()[:, : N // 2])
     turn_out = jnp.asarray(forward_turn())
     turn_back = jnp.asarray(inverse_turn())
     half_rows = jnp.asarray(np.stack(half_turn()).astype(np.float32))
@@ -529,14 +568,14 @@
     )(other_rows, kept(half_tables))
     folded_filter = pl.pallas_call(
         filter_kernel,
-        out_shape=pltpu.HBM((2, 40, N), F32),
-        in_specs=[SMEM, HBM, VMEM, VMEM],
+        out_shape=pltpu.HBM((2, SLOTS, N), F32),
+        in_specs=[SMEM, HBM, VMEM],
         out_specs=VMEM,
         scratch_shapes=[pltpu.VMEM((2, ROWS, N), F32), pltpu.SemaphoreType.DMA(())],
         compiler_params=params(16),
         cost_estimate=sizes(2**24),
         name="fold_filter",
-    )(rank, kept(filter_spectrum), other_rows, other_row)
+    )(rank, kept(filter_spectrum), other_rows)
 
     spectra, grad_own, grad_low, grad_row, filter_near, turn_near = pl.pallas_call(
         spectrum_kernel,
@@ -545,7 +584,7 @@
             pltpu.VMEM((2, SLOTS, N), F32),
             pltpu.VMEM((2 * SLOTS, N), BF),
             pltpu.VMEM((2, N), BF),
-            pltpu.VMEM((2, 40, N), F32),
+            pltpu.VMEM((2, SLOTS, N), F32),
             pltpu.VMEM((N, 128), F32),
         ],
         in_specs=[SMEM] + [VMEM] * 5 + [HBM, HBM, VMEM],
@@ -555,7 +594,7 @@
             pltpu.SemaphoreType.DMA((2,)),
         ],
         compiler_params=params(20),
-        cost_estimate=sizes(B_COST),
+        cost_estimate=sizes(2**24),
         name="spectra",
     )(
         rank,
@@ -575,51 +614,57 @@
             jax.ShapeDtypeStruct((2, N, 128), BF),
             pltpu.HBM((2, SLOTS, N), F32),
         ],
-        in_specs=[SMEM] + [VMEM] * 8,
+        in_specs=[SMEM] + [VMEM] * 9,
         out_specs=[VMEM, HBM],
         scratch_shapes=[pltpu.VMEM((N, 256), F32), pltpu.SemaphoreType.DMA(())],
         compiler_params=params(24),
         cost_estimate=sizes(B_COST),
         name="inverse",
-    )(rank, spectra, filter_near, *tables, turn_near, grad_own)
+    )(rank, spectra, filter_near, other_row, *tables, turn_near, grad_own)
     returned = lax.all_to_all(
         unturned.reshape(2 * RANKS, ROWS, 128), ("core", "ctx"), 0, 0, tiled=True
     )
 
     sections_near, gates_near = pl.pallas_call(
         near_kernel,
-        out_shape=[pltpu.VMEM((N, N), BF), pltpu.VMEM((3, 2, ROWS, N), BF)],
+        out_shape=[pltpu.VMEM((N, N // 2), BF), pltpu.VMEM((3, 2, ROWS, N), BF)],
         in_specs=[HBM] * 5,
         out_specs=[VMEM] * 2,
         scratch_shapes=[pltpu.SemaphoreType.DMA((4,))],
         compiler_params=params(16),
         cost_estimate=sizes(W_COST),
         name="bring_near",
-    )(mirror_grad, kept(sections), kept(input_proj), kept(value_proj), kept(grad_out))
-    grad_filter = pl.pallas_call(
+    )(mirror_grad, kept(half_sections), kept(input_proj), kept(value_proj), kept(grad_out))
+    most_rows, first_rows = pl.pallas_call(
         assemble_kernel,
-        out_shape=jax.ShapeDtypeStruct((1, 2, ROWS, N), F32),
-        in_specs=[SMEM] + [VMEM] * 3,
-        out_specs=VMEM,
+        out_shape=[
+            pltpu.HBM((1, 2, ROWS, N), F32),
+            pltpu.VMEM((2, 8, N), F32),
+        ],
+        in_specs=[SMEM] + [VMEM] * 2,
+        out_specs=[HBM, VMEM],
+        scratch_shapes=[pltpu.VMEM((2, ROWS, N), F32), pltpu.SemaphoreType.DMA(())],
         compiler_params=params(16),
         cost_estimate=sizes(2**24),
         name="assemble",
-    )(rank, grad_far, mirror_grad, mirror_row)
-
-    grad_input, grad_value, grad_output_proj = pl.pallas_call(
+    )(rank, grad_far, mirror_grad)
+
+    grad_input, grad_value, grad_output_proj, grad_filter = pl.pallas_call(
         result_kernel,
-        out_shape=[pltpu.HBM((2, ROWS, N), BF)] * 3,
-        in_specs=[VMEM] * 3,
-        out_specs=[HBM] * 3,
+        out_shape=[pltpu.HBM((2, ROWS, N), BF)] * 3 + [pltpu.HBM((1, 2, ROWS, N), F32)],
+        in_specs=[SMEM] + [VMEM] * 3 + [HBM, VMEM, VMEM],
+        out_specs=[HBM] * 4,
+        input_output_aliases={4: 3},
         scratch_shapes=[
-            pltpu.VMEM((256, N), BF),
+            pltpu.VMEM((512, N), BF),
             pltpu.VMEM((3, 2, ROWS, N), BF),
-            pltpu.SemaphoreType.DMA((3 * BLOCKS,)),
+            pltpu.VMEM((2, 8, N), F32),
+            pltpu.SemaphoreType.DMA((3 * BLOCKS + 1,)),
         ],
         compiler_params=params(20),
         cost_estimate=sizes(2 * 256 * N * N),
         name="results",
-    )(returned, sections_near, gates_near)
+    )(rank, returned, sections_near, gates_near, most_rows, first_rows, mirror_row)
     return (grad_input, grad_value, grad_output_proj, grad_filter)
 
 

time: 70.9 us -> 69.7 us (0.983)
  starting transfers between devices: 38.1 us -> 36.7 us
    ppermute x1, starting transfers between devices: 7.13 us -> 5.2 us  [local(): mirror_grad = lax.ppermute(grad_low, 'ctx', mirror_of)]
  transfers between devices with their start and end apart: 6 -> 6, of which waited for: 2 -> 2; matrix products, arithmetic and copies ran while one was open for 0% -> 0% of each run, Pallas kernels for 19% -> 21%
where the time goes in v3:
time: 69.7 us; the launch traced here: 69.1 us
  starting transfers between devices  36.7 us (53%)
  Pallas kernels  16.4 us (24%)
  waiting for transfers between devices  14 us (20%)
  other arithmetic  1.07 us (2%)
  between operations  0.81 us (1%)
    ppermute x1, starting transfers between devices, local(): lax.ppermute(filter_rows.reshape(2 * SLOTS, N), 'ctx', mirror_of)  10.6 us
    all_to_all x1, waiting for transfers between devices, local(): lax.all_to_all(unturned.reshape(2 * RANKS, ROWS, 128), ('core', 'ctx'), 0...  7.58 us
    all_to_all x1, waiting for transfers between devices, local(): lax.all_to_all(turned.reshape(2 * RANKS, ROWS, 128), ('core', 'ctx'), 0,...  6.45 us
    all_to_all x1, starting transfers between devices, local(): lax.all_to_all(unturned.reshape(2 * RANKS, ROWS, 128), ('core', 'ctx'), 0...  5.63 us
    all_to_all x1, starting transfers between devices, local(): lax.all_to_all(turned.reshape(2 * RANKS, ROWS, 128), ('core', 'ctx'), 0,...  5.53 us
    ppermute x1, starting transfers between devices, local(): mirror_grad = lax.ppermute(grad_low, 'ctx', mirror_of)  5.2 us
    ppermute x1, starting transfers between devices, local(): mirror_row = lax.ppermute(grad_row, 'ctx', special_of)  4.93 us
    ppermute x1, starting transfers between devices, local(): other_row = lax.ppermute(filter_row, 'ctx', special_of)  4.8 us
  transfers between devices with their start and end apart: 6, of which 2 were waited for; matrix products, arithmetic and copies ran while one was open for 0% of the time, Pallas kernels for 21%

profile of v3, /device:TPU:1, one launch (start us, length us, event | category | flops | bytes accessed | tf_op | source)
XLA Modules:
  0.0 69.1 jit_solution(16455391186247670661)
XLA Ops:
  0.6 1.1 %convert_bitcast_fusion = bf16[2,64,1024]{2,1,0:T(8,128)(2,1)S(1)} fusion(f32[1,2,64,1024]{3,2,1,0:T(8,128)} %own.1), kind=kLoop, calls=%fused_computation | loop fusion | flops 131072 | bytes 786432 | tf_op jit(solution)/shard_map/reshape | solution.py:524
  1.7 10.6 %collective-permute-start = (bf16[64,1024]{1,0:T(8,128)(2,1)S(1)}, bf16[64,1024]{1,0:T(8,128)(2,1)S(1)}, u32[]{:S(2)}, u32[]{:S(2)}) collective-permute-start(bf16[64,1024]{1,0:T(8,128)(2,1)S(1)} %bitcast.7), channel_id=1, source_target_pairs={{0,15},{1,14},{2,13},{3,12},{4,11},{5,10},{6,9},{7,8},{8,7},{9,6},... | collective-permute-start | bytes 393224 | tf_op jit(solution)/shard_map/ppermute | solution.py:525
  12.4 3.6 %sections.1 = (bf16[2,16,64,128]{3,2,1,0:T(8,128)(2,1)}, bf16[2,1024]{1,0:T(2,128)(2,1)S(1)}) custom-call(s32[1]{0:T(128)} %bitcast.rank, bf16[2,64,1024]{2,1,0:T(8,128)(2,1)} %first.1, bf16[2,64,1024]{2,1,0:T(8,128)(2,1)} %second.1, bf16[2,64,1024]{2,1,0:T(8,128)(2,1)} %outp.1, bf16[2,64,1024]{2,1,0:T(8,128)(2,1)} %third.1, ...), custom_call_target="tpu_custom_call" | custom-call | flops 10000000000 | bytes 1048576 | tf_op jit(solution)/shard_map/sections/pallas_call | solution.py:527
  16.0 5.5 %all-to-all-start = ((bf16[32,64,128]{2,1,0:T(8,128)(2,1)}), bf16[32,64,128]{2,1,0:T(8,128)(2,1)S(1)}, u32[]{:S(2)}, u32[]{:S(2)}) async-start(bf16[32,64,128]{2,1,0:T(8,128)(2,1)} %bitcast.6), calls=%async_computation | async-start | bytes 1048576 | tf_op jit(solution)/shard_map/all_to_all | solution.py:555
  21.6 0.0 copy-start.1
  21.6 4.8 %collective-permute-start.1 = (bf16[2,1024]{1,0:T(2,128)(2,1)S(1)}, bf16[2,1024]{1,0:T(2,128)(2,1)S(1)}, u32[]{:S(2)}, u32[]{:S(2)}) collective-permute-start(bf16[2,1024]{1,0:T(2,128)(2,1)S(1)} %get-tuple-element.29), channel_id=1, source_target_pairs={{1,15},{2,14},{3,13},{4,12},{5,11},{6,10},{7,9},{9,7},{10,6},{11,5... | collective-permute-start | bytes 12296 | tf_op jit(solution)/shard_map/ppermute | solution.py:554
  26.4 0.0 collective-permute-done.after.other
  26.4 1.6 %bring_tables.1 = (bf16[256,1024]{1,0:T(8,128)(2,1)S(1)}, bf16[256,1024]{1,0:T(8,128)(2,1)S(1)}, bf16[256,1024]{1,0:T(8,128)(2,1)S(1)}, bf16[256,1024]{1,0:T(8,128)(2,1)S(1)}) custom-call(bf16[64,1024]{1,0:T(8,128)(2,1)S(1)} %collective-permute-done.after.other, bf16[4,256,1024]{2,1,0:T(8,128)(2,1)} %constant.14.clone.refs_0_), custom_call_target="tpu_custom_call" | custom-call | flops 40000000000 | bytes 1048576 | tf_op jit(solution)/shard_map/bring_tables/pallas_call | solution.py:559
  28.0 2.5 %fold_filter.1.filt_far = f32[2,32,1024]{2,1,0:T(8,128)} custom-call(s32[1]{0:T(128)} %bitcast.rank, f32[1,2,64,1024]{3,2,1,0:T(8,128)} %own.1, bf16[64,1024]{1,0:T(8,128)(2,1)S(1)} %collective-permute-done.after.other), custom_call_target="tpu_custom_call" | custom-call | flops 16777216 | bytes 1048576 | tf_op jit(solution)/shard_map/fold_filter/pallas_call | solution.py:569
  30.4 6.4 %all-to-all-done.turned = bf16[32,64,128]{2,1,0:T(8,128)(2,1)S(1)} async-done(((bf16[32,64,128]{2,1,0:T(8,128)(2,1)}), bf16[32,64,128]{2,1,0:T(8,128)(2,1)S(1)}, u32[]{:S(2)}, u32[]{:S(2)}) %all-to-all-start) | async-done | bytes 524320 | tf_op jit(solution)/shard_map/all_to_all | solution.py:555
  36.9 0.0 copy-done.1
  36.9 1.8 %spectra.1 = (bf16[272,1024]{1,0:T(8,128)(2,1)S(1)}, f32[2,32,1024]{2,1,0:T(8,128)S(1)}, bf16[64,1024]{1,0:T(8,128)(2,1)S(1)}, bf16[2,1024]{1,0:T(2,128)(2,1)S(1...) custom-call(s32[1]{0:T(128)} %bitcast.rank, bf16[32,64,128]{2,1,0:T(8,128)(2,1)S(1)} %all-to-all-done.turned, ...), custom_call_target="tpu_custom_call" | custom-call | flops 16777216 | bytes 1048576 | tf_op jit(solution)/shard_map/spectra/pallas_call | solution.py:580
  38.7 5.2 %collective-permute-start.2 = (bf16[64,1024]{1,0:T(8,128)(2,1)S(1)}, bf16[64,1024]{1,0:T(8,128)(2,1)S(1)}, u32[]{:S(2)}, u32[]{:S(2)}) collective-permute-start(bf16[64,1024]{1,0:T(8,128)(2,1)S(1)} %get-tuple-element.33), channel_id=1, source_target_pairs={{0,15},{1,14},{2,13},{3,12},{4,11},{5,10},{6,9},{7,8},{8,7},{9,6},... | collective-permute-start | bytes 393224 | tf_op jit(solution)/shard_map/ppermute | solution.py:608
  43.9 0.0 collective-permute-done.1.special
  43.9 2.5 %inverse.1 = (bf16[2,1024,128]{2,1,0:T(8,128)(2,1)}, f32[2,32,1024]{2,1,0:T(8,128)}) custom-call(s32[1]{0:T(128)} %bitcast.rank, bf16[272,1024]{1,0:T(8,128)(2,1)S(1)} %get-tuple-element.27.spec, f32[2,32,1024]{2,1,0:T(8,128)S(1)} %get-tuple-element.28.filt, bf16[2,1024]{1,0:T(2,128)(2,1)S(1)} %collective-permute-done.1.special, ...), custom_call_target="tpu_custom_call" | custom-call | flops 10000000000 | bytes 1048576 | tf_op jit(solution)/shard_map/inverse/pallas_call | solution.py:611
  46.3 5.6 %all-to-all-start.1 = ((bf16[32,64,128]{2,1,0:T(8,128)(2,1)}), bf16[32,64,128]{2,1,0:T(8,128)(2,1)S(1)}, u32[]{:S(2)}, u32[]{:S(2)}) async-start(bf16[32,64,128]{2,1,0:T(8,128)(2,1)} %bitcast.4), calls=%async_computation.1 | async-start | bytes 1048576 | tf_op jit(solution)/shard_map/all_to_all | solution.py:624
  52.0 0.0 copy-start
  52.0 4.9 %collective-permute-start.3 = (bf16[2,1024]{1,0:T(2,128)(2,1)S(1)}, bf16[2,1024]{1,0:T(2,128)(2,1)S(1)}, u32[]{:S(2)}, u32[]{:S(2)}) collective-permute-start(bf16[2,1024]{1,0:T(2,128)(2,1)S(1)} %get-tuple-element.39), channel_id=1, source_target_pairs={{1,15},{2,14},{3,13},{4,12},{5,11},{6,10},{7,9},{9,7},{10,6},{11,5... | collective-permute-start | bytes 12296 | tf_op jit(solution)/shard_map/ppermute | solution.py:609
  56.9 0.0 collective-permute-done.2.after.other
  56.9 1.5 %bring_near.1 = (bf16[1024,512]{1,0:T(8,128)(2,1)S(1)}, bf16[3,2,64,1024]{3,2,1,0:T(8,128)(2,1)S(1)}) custom-call(bf16[64,1024]{1,0:T(8,128)(2,1)S(1)} %collective-permute-done.2.after.other, bf16[1024,512]{1,0:T(8,128)(2,1)} %constant.15.clone.table, bf16[2,64,1024]{2,1,0:T(8,128)(2,1)} %first.1, bf16[2,64,1024]{2,1,0:T(8,128)(2,1)} %second.1, ...), custom_call_target="tpu_custom_call" | custom-call | flops 40000000000 | bytes 1048576 | tf_op jit(solution)/shard_map/bring_near/pallas_call | solution.py:628
  58.4 0.0 copy-done
  58.4 1.3 %assemble.1 = (f32[1,2,64,1024]{3,2,1,0:T(8,128)}, f32[2,8,1024]{2,1,0:T(8,128)S(1)}) custom-call(s32[1]{0:T(128)} %bitcast.rank, f32[2,32,1024]{2,1,0:T(8,128)S(1)} %copy-done, bf16[64,1024]{1,0:T(8,128)(2,1)S(1)} %collective-permute-done.2.after.other), custom_call_target="tpu_custom_call" | custom-call | flops 16777216 | bytes 1048576 | tf_op jit(solution)/shard_map/assemble/pallas_call | solution.py:638
  59.7 0.0 collective-permute-done.3.special
  59.7 7.6 %all-to-all-done.1.arrived = bf16[32,64,128]{2,1,0:T(8,128)(2,1)S(1)} async-done(((bf16[32,64,128]{2,1,0:T(8,128)(2,1)}), bf16[32,64,128]{2,1,0:T(8,128)(2,1)S(1)}, u32[]{:S(2)}, u32[]{:S(2)}) %all-to-all-start.1) | async-done | bytes 524320 | tf_op jit(solution)/shard_map/all_to_all | solution.py:624
  67.3 1.8 %results.1 = (bf16[2,64,1024]{2,1,0:T(8,128)(2,1)}, bf16[2,64,1024]{2,1,0:T(8,128)(2,1)}, bf16[2,64,1024]{2,1,0:T(8,128)(2,1)}, f32[1,2,64,1024]{3,2,1,0:T(8,128)}) custom-call(s32[1]{0:T(128)} %bitcast.rank, bf16[32,64,128]{2,1,0:T(8,128)(2,1)S(1)} %all-to-all-done.1.arrived, ...), custom_call_target="tpu_custom_call", output_to_operand_aliasing={{3}: (4, {})} | custom-call | flops 536870912 | bytes 1048576 | tf_op jit(solution)/shard_map/results/pallas_call | solution.py:652
  (1 shorter events, 0.0 us)
Async XLA Ops:
  1.7 24.7 %collective-permute-start = (bf16[64,1024]{1,0:T(8,128)(2,1)S(1)}, bf16[64,1024]{1,0:T(8,128)(2,1)S(1)}, u32[]{:S(2)}, u32[]{:S(2)}) collective-permute-start(bf16[64,1024]{1,0:T(8,128)(2,1)S(1)} %bitcast.7), channel_id=1, source_target_pairs={{0,15},{1,14},{2,13},{3,12},{4,11},{5,10},{6,9},{7,8},{8,7},{9,6},... | collective-permute-start | bytes 393224 | tf_op jit(solution)/shard_map/ppermute | solution.py:525
  16.0 20.9 %all-to-all-start = ((bf16[32,64,128]{2,1,0:T(8,128)(2,1)}), bf16[32,64,128]{2,1,0:T(8,128)(2,1)S(1)}, u32[]{:S(2)}, u32[]{:S(2)}) async-start(bf16[32,64,128]{2,1,0:T(8,128)(2,1)} %bitcast.6), calls=%async_computation | async-start | bytes 1048576 | tf_op jit(solution)/shard_map/all_to_all | solution.py:555
  21.6 15.3 %copy-start.1 = (f32[2,1024]{1,0:T(2,128)S(1)}, f32[2,1024]{1,0:T(2,128)}, u32[]{:S(2)}) copy-start(f32[2,1024]{1,0:T(2,128)} %constant.18.clone.half) | copy-start | bytes 24580
  21.6 22.3 %collective-permute-start.1 = (bf16[2,1024]{1,0:T(2,128)(2,1)S(1)}, bf16[2,1024]{1,0:T(2,128)(2,1)S(1)}, u32[]{:S(2)}, u32[]{:S(2)}) collective-permute-start(bf16[2,1024]{1,0:T(2,128)(2,1)S(1)} %get-tuple-element.29), channel_id=1, source_target_pairs={{1,15},{2,14},{3,13},{4,12},{5,11},{6,10},{7,9},{9,7},{10,6},{11,5... | collective-permute-start | bytes 12296 | tf_op jit(solution)/shard_map/ppermute | solution.py:554
  38.7 18.3 %collective-permute-start.2 = (bf16[64,1024]{1,0:T(8,128)(2,1)S(1)}, bf16[64,1024]{1,0:T(8,128)(2,1)S(1)}, u32[]{:S(2)}, u32[]{:S(2)}) collective-permute-start(bf16[64,1024]{1,0:T(8,128)(2,1)S(1)} %get-tuple-element.33), channel_id=1, source_target_pairs={{0,15},{1,14},{2,13},{3,12},{4,11},{5,10},{6,9},{7,8},{8,7},{9,6},... | collective-permute-start | bytes 393224 | tf_op jit(solution)/shard_map/ppermute | solution.py:608
  46.3 21.0 %all-to-all-start.1 = ((bf16[32,64,128]{2,1,0:T(8,128)(2,1)}), bf16[32,64,128]{2,1,0:T(8,128)(2,1)S(1)}, u32[]{:S(2)}, u32[]{:S(2)}) async-start(bf16[32,64,128]{2,1,0:T(8,128)(2,1)} %bitcast.4), calls=%async_computation.1 | async-start | bytes 1048576 | tf_op jit(solution)/shard_map/all_to_all | solution.py:624
  52.0 6.4 %copy-start = (f32[2,32,1024]{2,1,0:T(8,128)S(1)}, f32[2,32,1024]{2,1,0:T(8,128)}, u32[]{:S(2)}) copy-start(f32[2,32,1024]{2,1,0:T(8,128)} %get-tuple-element.36.own) | copy-start | bytes 786436
  52.0 7.7 %collective-permute-start.3 = (bf16[2,1024]{1,0:T(2,128)(2,1)S(1)}, bf16[2,1024]{1,0:T(2,128)(2,1)S(1)}, u32[]{:S(2)}, u32[]{:S(2)}) collective-permute-start(bf16[2,1024]{1,0:T(2,128)(2,1)S(1)} %get-tuple-element.39), channel_id=1, source_target_pairs={{1,15},{2,14},{3,13},{4,12},{5,11},{6,10},{7,9},{9,7},{10,6},{11,5... | collective-permute-start | bytes 12296 | tf_op jit(solution)/shard_map/ppermute | solution.py:609

commit v4 on v3

--- a/solution.py
+++ b/solution.py
@@ -98,25 +98,23 @@
         copy.start()
 
 
-def section_kernel(
-    rank, inp, val, outp, grad, table, turn, filt, out, row,
-    gates, sections, turns, ready, signals, lines, sems
+def gather_kernel(
+    rank, inp, val, outp, grad, table, turn, filt,
+    rows, row, signals, sections, turns, gates, lines, first, sems
 ):
+    line_copy = pltpu.make_async_copy(filt.at[0, :, pl.ds(SLOTS, SLOTS)], lines, sems.at[0])
+    row_copy = pltpu.make_async_copy(filt.at[0, :, pl.ds(0, 8)], first, sems.at[1])
     gate_copies = [
-        pltpu.make_async_copy(source, gates.at[which], sems.at[which])
+        pltpu.make_async_copy(source, gates.at[which], sems.at[2 + which])
         for which, source in enumerate((inp, val, outp, grad))
     ]
-    turn_copy = pltpu.make_async_copy(turn.at[rank[0]], turns, sems.at[4])
-    blocks = [pl.ds(WIDE * block, WIDE) for block in range(BLOCKS)]
-    table_copies = [
-        pltpu.make_async_copy(table.at[rows], sections.at[rows], sems.at[5 + block])
-        for block, rows in enumerate(blocks)
-    ]
-    row_copy = pltpu.make_async_copy(
-        filt.at[0, :, pl.ds(0, 8)], lines, sems.at[9 + 2 * BLOCKS]
-    )
-    start_all(gate_copies + table_copies[:1] + [turn_copy] + table_copies[1:] + [row_copy])
+    table_copy = pltpu.make_async_copy(table, sections, sems.at[6])
+    turn_copy = pltpu.make_async_copy(turn.at[rank[0]], turns, sems.at[7])
+    start_all([line_copy] + gate_copies + [table_copy, turn_copy, row_copy])
     middle = N // 2
+    line_copy.wait()
+    for part in range(2):
+        rows[SLOTS * part : SLOTS * part + SLOTS, :] = lines[part].astype(BF)
     for copy in gate_copies:
         copy.wait()
     for chan in range(2):
@@ -127,16 +125,22 @@
             lanes = slice(middle * part, middle * part + middle)
             signals[base : base + 64, :] = gated[:, lanes].astype(BF)
             signals[base + 64 : base + 128, :] = conv[:, lanes].astype(BF)
+    row_copy.wait()
+    row[...] = jnp.concatenate([first[0, 0:1], first[1, 0:1]], axis=0).astype(BF)
+    table_copy.wait()
+    turn_copy.wait()
+
+
+def section_kernel(signals, sections, turns, row, out, row_out, ready, sems):
+    row_out[...] = row[...]
     out_copies = []
-    for block, rows in enumerate(blocks):
-        table_copies[block].wait()
+    for block in range(BLOCKS):
+        rows = slice(WIDE * block, WIDE * block + WIDE)
         halves = lax.dot_general(
             sections[rows, :], signals[...], NT, preferred_element_type=F32
         )
         odd_rows = (rows_of((WIDE, 1)) + (block >= BLOCKS // 2)) % 2
         section = halves[:, :256] + (1 - 2 * odd_rows).astype(F32) * halves[:, 256:]
-        if block == 0:
-            turn_copy.wait()
         for pair in range(2):
             base = WIDE // 2 * block + 64 * pair
             cos, sin = split_turn(turns[base : base + 64, :])
@@ -154,12 +158,10 @@
         peers = pl.ds(4 * block, 4)
         for chan in range(2):
             copy = pltpu.make_async_copy(
-                ready.at[chan, peers], out.at[chan, peers], sems.at[9 + 2 * block + chan]
+                ready.at[chan, peers], out.at[chan, peers], sems.at[2 * block + chan]
             )
             copy.start()
             out_copies.append(copy)
-    row_copy.wait()
-    row[...] = jnp.concatenate([lines[0, 0:1], lines[1, 0:1]], axis=0).astype(BF)
     for copy in out_copies:
         copy.wait()
 
@@ -521,26 +523,26 @@
     special_of = [(r, RANKS - r) for r in range(1, RANKS) if r != half_ranks]
     special_of += [(0, half_ranks), (half_ranks, 0)]
 
-    filter_rows = filter_spectrum.reshape(2, ROWS, N)[:, 32:64, :].astype(BF)
-    other_rows = lax.ppermute(filter_rows.reshape(2 * SLOTS, N), "ctx", mirror_of)
-
-    turned, filter_row = pl.pallas_call(
-        section_kernel,
-        out_shape=[pltpu.HBM((2, RANKS, ROWS, 128), BF), pltpu.VMEM((2, N), BF)],
+    filter_rows, filter_row, signals, sections, turns = pl.pallas_call(
+        gather_kernel,
+        out_shape=[
+            pltpu.VMEM((2 * SLOTS, N), BF),
+            pltpu.VMEM((2, N), BF),
+            pltpu.VMEM((512, N // 2), BF),
+            pltpu.VMEM((N, N // 2), BF),
+            pltpu.VMEM((N // 2, 128), F32),
+        ],
         in_specs=[SMEM] + [HBM] * 7,
-        out_specs=[HBM, VMEM],
+        out_specs=[VMEM] * 5,
         scratch_shapes=[
             pltpu.VMEM((4, 2, ROWS, N), BF),
-            pltpu.VMEM((N, N // 2), BF),
-            pltpu.VMEM((N // 2, 128), F32),
-            pltpu.VMEM((2, RANKS, ROWS, 128), BF),
-            pltpu.VMEM((512, N // 2), BF),
+            pltpu.VMEM((2, SLOTS, N), F32),
             pltpu.VMEM((2, 8, N), F32),
-            pltpu.SemaphoreType.DMA((10 + 2 * BLOCKS,)),
-        ],
-        compiler_params=params(24),
-        cost_estimate=sizes(A_COST),
-        name="sections",
+            pltpu.SemaphoreType.DMA((8,)),
+        ],
+        compiler_params=params(16),
+        cost_estimate=sizes(2**24),
+        name="gather",
     )(
         rank,
         kept(input_proj),
@@ -551,6 +553,20 @@
         kept(turn_out),
         kept(filter_spectrum),
     )
+    other_rows = lax.ppermute(filter_rows, "ctx", mirror_of)
+    turned, filter_row = pl.pallas_call(
+        section_kernel,
+        out_shape=[pltpu.HBM((2, RANKS, ROWS, 128), BF), pltpu.VMEM((2, N), BF)],
+        in_specs=[VMEM] * 4,
+        out_specs=[HBM, VMEM],
+        scratch_shapes=[
+            pltpu.VMEM((2, RANKS, ROWS, 128), BF),
+            pltpu.SemaphoreType.DMA((2 * BLOCKS,)),
+        ],
+        compiler_params=params(16),
+        cost_estimate=sizes(A_COST),
+        name="sections",
+    )(signals, sections, turns, filter_row)
     other_row = lax.ppermute(filter_row, "ctx", special_of)
     arrived = lax.all_to_all(
         turned.reshape(2 * RANKS, ROWS, 128), ("core", "ctx"), 0, 0, tiled=True

time: 69.7 us -> 68.2 us (0.978)
  other arithmetic: 1.07 us -> 0 us
    pallas_call x1, Pallas kernels: 3.64 us -> 1.48 us  [local(): pl.pallas_call(section_kernel, out_shape=[pltpu.HBM((2, RANKS, ROWS, 128)...]
    pallas_call x0 -> x1, Pallas kernels: none -> 1.74 us  [local(): pl.pallas_call(gather_kernel, out_shape=[pltpu.VMEM((2 * SLOTS, N), BF),...]
    reshape x1 -> x0, other arithmetic: 1.07 us -> none  [local(): filter_rows = filter_spectrum.reshape(2, ROWS, N)[:, 32:64, :].astype(BF)]
  transfers between devices with their start and end apart: 6 -> 6, of which waited for: 2 -> 2; matrix products, arithmetic and copies ran while one was open for 0% -> 0% of each run, Pallas kernels for 21% -> 18%
where the time goes in v4:
time: 68.2 us; the launch traced here: 67.6 us
  starting transfers between devices  36.7 us (54%)
  Pallas kernels  16 us (23%)
  waiting for transfers between devices  14 us (21%)
  between operations  0.8 us (1%)
    ppermute x1, starting transfers between devices, local(): other_rows = lax.ppermute(filter_rows, 'ctx', mirror_of)  10.6 us
    all_to_all x1, waiting for transfers between devices, local(): lax.all_to_all(unturned.reshape(2 * RANKS, ROWS, 128), ('core', 'ctx'), 0...  7.58 us
    all_to_all x1, waiting for transfers between devices, local(): lax.all_to_all(turned.reshape(2 * RANKS, ROWS, 128), ('core', 'ctx'), 0,...  6.45 us
    all_to_all x1, starting transfers between devices, local(): lax.all_to_all(unturned.reshape(2 * RANKS, ROWS, 128), ('core', 'ctx'), 0...  5.63 us
    all_to_all x1, starting transfers between devices, local(): lax.all_to_all(turned.reshape(2 * RANKS, ROWS, 128), ('core', 'ctx'), 0,...  5.53 us
    ppermute x1, starting transfers between devices, local(): mirror_grad = lax.ppermute(grad_low, 'ctx', mirror_of)  5.2 us
    ppermute x1, starting transfers between devices, local(): mirror_row = lax.ppermute(grad_row, 'ctx', special_of)  4.93 us
    ppermute x1, starting transfers between devices, local(): other_row = lax.ppermute(filter_row, 'ctx', special_of)  4.8 us
  transfers between devices with their start and end apart: 6, of which 2 were waited for; matrix products, arithmetic and copies ran while one was open for 0% of the time, Pallas kernels for 18%

profile of v4, /device:TPU:1, one launch (start us, length us, event | category | flops | bytes accessed | tf_op | source)
XLA Modules:
  0.0 67.6 jit_solution(1846622629400118920)
XLA Ops:
  0.6 1.7 %gather.1 = (bf16[64,1024]{1,0:T(8,128)(2,1)S(1)}, bf16[2,1024]{1,0:T(2,128)(2,1)S(1)}, bf16[512,512]{1,0:T(8,128)(2,1)S(1)}, bf16[1024,512]{1,0:T(8,128)(2,1)S(1)}, f32[512,128]{1,0:T(8,128)S(1)}) custom-call(s32[1]{0:T(128)} %bitcast.rank, bf16[2,64,1024]{2,1,0:T(8,128)(2,1)} %first.1, bf16[2,64,1024]{2,1,0:T(8,128)(2,1)} %second.1, ...), custom_call_target="tpu_custom_call" | custom-call | flops 16777216 | bytes 1048576 | tf_op jit(solution)/shard_map/gather/pallas_call | solution.py:526
  2.4 10.6 %collective-permute-start = (bf16[64,1024]{1,0:T(8,128)(2,1)S(1)}, bf16[64,1024]{1,0:T(8,128)(2,1)S(1)}, u32[]{:S(2)}, u32[]{:S(2)}) collective-permute-start(bf16[64,1024]{1,0:T(8,128)(2,1)S(1)} %get-tuple-element.32), channel_id=1, source_target_pairs={{0,15},{1,14},{2,13},{3,12},{4,11},{5,10},{6,9},{7,8},{8,7},{9,6},... | collective-permute-start | bytes 393224 | tf_op jit(solution)/shard_map/ppermute | solution.py:556
  13.0 1.5 %sections.1 = (bf16[2,16,64,128]{3,2,1,0:T(8,128)(2,1)}, bf16[2,1024]{1,0:T(2,128)(2,1)S(1)}) custom-call(bf16[512,512]{1,0:T(8,128)(2,1)S(1)} %get-tuple-element.27.signals, bf16[1024,512]{1,0:T(8,128)(2,1)S(1)} %get-tuple-element.28.sections, f32[512,128]{1,0:T(8,128)S(1)} %get-tuple-element.29.turns, bf16[2,1024]{1,0:T(2,128)(2,1)S(1)} %get-tuple-element.30.row), custom_call_target="tpu_custom_call" | custom-call | flops 10000000000 | bytes 1048576 | tf_op jit(solution)/shard_map/sections/pallas_call | solution.py:557
  14.5 5.5 %all-to-all-start = ((bf16[32,64,128]{2,1,0:T(8,128)(2,1)}), bf16[32,64,128]{2,1,0:T(8,128)(2,1)S(1)}, u32[]{:S(2)}, u32[]{:S(2)}) async-start(bf16[32,64,128]{2,1,0:T(8,128)(2,1)} %bitcast.3), calls=%async_computation | async-start | bytes 1048576 | tf_op jit(solution)/shard_map/all_to_all | solution.py:571
  20.0 0.0 copy-start.1
  20.1 4.8 %collective-permute-start.1 = (bf16[2,1024]{1,0:T(2,128)(2,1)S(1)}, bf16[2,1024]{1,0:T(2,128)(2,1)S(1)}, u32[]{:S(2)}, u32[]{:S(2)}) collective-permute-start(bf16[2,1024]{1,0:T(2,128)(2,1)S(1)} %get-tuple-element.39), channel_id=1, source_target_pairs={{1,15},{2,14},{3,13},{4,12},{5,11},{6,10},{7,9},{9,7},{10,6},{11,5... | collective-permute-start | bytes 12296 | tf_op jit(solution)/shard_map/ppermute | solution.py:570
  24.9 0.0 collective-permute-done.after.other
  24.9 1.6 %bring_tables.1 = (bf16[256,1024]{1,0:T(8,128)(2,1)S(1)}, bf16[256,1024]{1,0:T(8,128)(2,1)S(1)}, bf16[256,1024]{1,0:T(8,128)(2,1)S(1)}, bf16[256,1024]{1,0:T(8,128)(2,1)S(1)}) custom-call(bf16[64,1024]{1,0:T(8,128)(2,1)S(1)} %collective-permute-done.after.other, bf16[4,256,1024]{2,1,0:T(8,128)(2,1)} %constant.14.clone.refs_0_), custom_call_target="tpu_custom_call" | custom-call | flops 40000000000 | bytes 1048576 | tf_op jit(solution)/shard_map/bring_tables/pallas_call | solution.py:575
  26.4 2.5 %fold_filter.1.filt_far = f32[2,32,1024]{2,1,0:T(8,128)} custom-call(s32[1]{0:T(128)} %bitcast.rank, f32[1,2,64,1024]{3,2,1,0:T(8,128)} %own.1, bf16[64,1024]{1,0:T(8,128)(2,1)S(1)} %collective-permute-done.after.other), custom_call_target="tpu_custom_call" | custom-call | flops 16777216 | bytes 1048576 | tf_op jit(solution)/shard_map/fold_filter/pallas_call | solution.py:585
  28.9 6.5 %all-to-all-done.turned = bf16[32,64,128]{2,1,0:T(8,128)(2,1)S(1)} async-done(((bf16[32,64,128]{2,1,0:T(8,128)(2,1)}), bf16[32,64,128]{2,1,0:T(8,128)(2,1)S(1)}, u32[]{:S(2)}, u32[]{:S(2)}) %all-to-all-start) | async-done | bytes 524320 | tf_op jit(solution)/shard_map/all_to_all | solution.py:571
  35.4 0.0 copy-done.1
  35.4 1.8 %spectra.1 = (bf16[272,1024]{1,0:T(8,128)(2,1)S(1)}, f32[2,32,1024]{2,1,0:T(8,128)S(1)}, bf16[64,1024]{1,0:T(8,128)(2,1)S(1)}, bf16[2,1024]{1,0:T(2,128)(2,1)S(1...) custom-call(s32[1]{0:T(128)} %bitcast.rank, bf16[32,64,128]{2,1,0:T(8,128)(2,1)S(1)} %all-to-all-done.turned, ...), custom_call_target="tpu_custom_call" | custom-call | flops 16777216 | bytes 1048576 | tf_op jit(solution)/shard_map/spectra/pallas_call | solution.py:596
  37.1 5.2 %collective-permute-start.2 = (bf16[64,1024]{1,0:T(8,128)(2,1)S(1)}, bf16[64,1024]{1,0:T(8,128)(2,1)S(1)}, u32[]{:S(2)}, u32[]{:S(2)}) collective-permute-start(bf16[64,1024]{1,0:T(8,128)(2,1)S(1)} %get-tuple-element.43), channel_id=1, source_target_pairs={{0,15},{1,14},{2,13},{3,12},{4,11},{5,10},{6,9},{7,8},{8,7},{9,6},... | collective-permute-start | bytes 393224 | tf_op jit(solution)/shard_map/ppermute | solution.py:624
  42.3 0.0 collective-permute-done.1.special
  42.4 2.5 %inverse.1 = (bf16[2,1024,128]{2,1,0:T(8,128)(2,1)}, f32[2,32,1024]{2,1,0:T(8,128)}) custom-call(s32[1]{0:T(128)} %bitcast.rank, bf16[272,1024]{1,0:T(8,128)(2,1)S(1)} %get-tuple-element.37.spec, f32[2,32,1024]{2,1,0:T(8,128)S(1)} %get-tuple-element.38.filt, bf16[2,1024]{1,0:T(2,128)(2,1)S(1)} %collective-permute-done.1.special, ...), custom_call_target="tpu_custom_call" | custom-call | flops 10000000000 | bytes 1048576 | tf_op jit(solution)/shard_map/inverse/pallas_call | solution.py:627
  44.8 5.6 %all-to-all-start.1 = ((bf16[32,64,128]{2,1,0:T(8,128)(2,1)}), bf16[32,64,128]{2,1,0:T(8,128)(2,1)S(1)}, u32[]{:S(2)}, u32[]{:S(2)}) async-start(bf16[32,64,128]{2,1,0:T(8,128)(2,1)} %bitcast.2), calls=%async_computation.1 | async-start | bytes 1048576 | tf_op jit(solution)/shard_map/all_to_all | solution.py:640
  50.5 0.0 copy-start
  50.5 4.9 %collective-permute-start.3 = (bf16[2,1024]{1,0:T(2,128)(2,1)S(1)}, bf16[2,1024]{1,0:T(2,128)(2,1)S(1)}, u32[]{:S(2)}, u32[]{:S(2)}) collective-permute-start(bf16[2,1024]{1,0:T(2,128)(2,1)S(1)} %get-tuple-element.49), channel_id=1, source_target_pairs={{1,15},{2,14},{3,13},{4,12},{5,11},{6,10},{7,9},{9,7},{10,6},{11,5... | collective-permute-start | bytes 12296 | tf_op jit(solution)/shard_map/ppermute | solution.py:625
  55.4 0.0 collective-permute-done.2.after.other
  55.4 1.5 %bring_near.1 = (bf16[1024,512]{1,0:T(8,128)(2,1)S(1)}, bf16[3,2,64,1024]{3,2,1,0:T(8,128)(2,1)S(1)}) custom-call(bf16[64,1024]{1,0:T(8,128)(2,1)S(1)} %collective-permute-done.2.after.other, bf16[1024,512]{1,0:T(8,128)(2,1)} %constant.15.clone.table, bf16[2,64,1024]{2,1,0:T(8,128)(2,1)} %first.1, bf16[2,64,1024]{2,1,0:T(8,128)(2,1)} %second.1, ...), custom_call_target="tpu_custom_call" | custom-call | flops 40000000000 | bytes 1048576 | tf_op jit(solution)/shard_map/bring_near/pallas_call | solution.py:644
  56.9 0.0 copy-done
  56.9 1.3 %assemble.1 = (f32[1,2,64,1024]{3,2,1,0:T(8,128)}, f32[2,8,1024]{2,1,0:T(8,128)S(1)}) custom-call(s32[1]{0:T(128)} %bitcast.rank, f32[2,32,1024]{2,1,0:T(8,128)S(1)} %copy-done, bf16[64,1024]{1,0:T(8,128)(2,1)S(1)} %collective-permute-done.2.after.other), custom_call_target="tpu_custom_call" | custom-call | flops 16777216 | bytes 1048576 | tf_op jit(solution)/shard_map/assemble/pallas_call | solution.py:654
  58.2 0.0 collective-permute-done.3.special
  58.2 7.6 %all-to-all-done.1.arrived = bf16[32,64,128]{2,1,0:T(8,128)(2,1)S(1)} async-done(((bf16[32,64,128]{2,1,0:T(8,128)(2,1)}), bf16[32,64,128]{2,1,0:T(8,128)(2,1)S(1)}, u32[]{:S(2)}, u32[]{:S(2)}) %all-to-all-start.1) | async-done | bytes 524320 | tf_op jit(solution)/shard_map/all_to_all | solution.py:640
  65.8 1.8 %results.1 = (bf16[2,64,1024]{2,1,0:T(8,128)(2,1)}, bf16[2,64,1024]{2,1,0:T(8,128)(2,1)}, bf16[2,64,1024]{2,1,0:T(8,128)(2,1)}, f32[1,2,64,1024]{3,2,1,0:T(8,128)}) custom-call(s32[1]{0:T(128)} %bitcast.rank, bf16[32,64,128]{2,1,0:T(8,128)(2,1)S(1)} %all-to-all-done.1.arrived, ...), custom_call_target="tpu_custom_call", output_to_operand_aliasing={{3}: (4, {})} | custom-call | flops 536870912 | bytes 1048576 | tf_op jit(solution)/shard_map/results/pallas_call | solution.py:668
Async XLA Ops:
  2.4 22.5 %collective-permute-start = (bf16[64,1024]{1,0:T(8,128)(2,1)S(1)}, bf16[64,1024]{1,0:T(8,128)(2,1)S(1)}, u32[]{:S(2)}, u32[]{:S(2)}) collective-permute-start(bf16[64,1024]{1,0:T(8,128)(2,1)S(1)} %get-tuple-element.32), channel_id=1, source_target_pairs={{0,15},{1,14},{2,13},{3,12},{4,11},{5,10},{6,9},{7,8},{8,7},{9,6},... | collective-permute-start | bytes 393224 | tf_op jit(solution)/shard_map/ppermute | solution.py:556
  14.5 20.9 %all-to-all-start = ((bf16[32,64,128]{2,1,0:T(8,128)(2,1)}), bf16[32,64,128]{2,1,0:T(8,128)(2,1)S(1)}, u32[]{:S(2)}, u32[]{:S(2)}) async-start(bf16[32,64,128]{2,1,0:T(8,128)(2,1)} %bitcast.3), calls=%async_computation | async-start | bytes 1048576 | tf_op jit(solution)/shard_map/all_to_all | solution.py:571
  20.0 15.3 %copy-start.1 = (f32[2,1024]{1,0:T(2,128)S(1)}, f32[2,1024]{1,0:T(2,128)}, u32[]{:S(2)}) copy-start(f32[2,1024]{1,0:T(2,128)} %constant.18.clone.half) | copy-start | bytes 24580
  20.1 22.3 %collective-permute-start.1 = (bf16[2,1024]{1,0:T(2,128)(2,1)S(1)}, bf16[2,1024]{1,0:T(2,128)(2,1)S(1)}, u32[]{:S(2)}, u32[]{:S(2)}) collective-permute-start(bf16[2,1024]{1,0:T(2,128)(2,1)S(1)} %get-tuple-element.39), channel_id=1, source_target_pairs={{1,15},{2,14},{3,13},{4,12},{5,11},{6,10},{7,9},{9,7},{10,6},{11,5... | collective-permute-start | bytes 12296 | tf_op jit(solution)/shard_map/ppermute | solution.py:570
  37.1 18.3 %collective-permute-start.2 = (bf16[64,1024]{1,0:T(8,128)(2,1)S(1)}, bf16[64,1024]{1,0:T(8,128)(2,1)S(1)}, u32[]{:S(2)}, u32[]{:S(2)}) collective-permute-start(bf16[64,1024]{1,0:T(8,128)(2,1)S(1)} %get-tuple-element.43), channel_id=1, source_target_pairs={{0,15},{1,14},{2,13},{3,12},{4,11},{5,10},{6,9},{7,8},{8,7},{9,6},... | collective-permute-start | bytes 393224 | tf_op jit(solution)/shard_map/ppermute | solution.py:624
  44.8 21.0 %all-to-all-start.1 = ((bf16[32,64,128]{2,1,0:T(8,128)(2,1)}), bf16[32,64,128]{2,1,0:T(8,128)(2,1)S(1)}, u32[]{:S(2)}, u32[]{:S(2)}) async-start(bf16[32,64,128]{2,1,0:T(8,128)(2,1)} %bitcast.2), calls=%async_computation.1 | async-start | bytes 1048576 | tf_op jit(solution)/shard_map/all_to_all | solution.py:640
  50.5 6.4 %copy-start = (f32[2,32,1024]{2,1,0:T(8,128)S(1)}, f32[2,32,1024]{2,1,0:T(8,128)}, u32[]{:S(2)}) copy-start(f32[2,32,1024]{2,1,0:T(8,128)} %get-tuple-element.46.own) | copy-start | bytes 786436
  50.5 7.7 %collective-permute-start.3 = (bf16[2,1024]{1,0:T(2,128)(2,1)S(1)}, bf16[2,1024]{1,0:T(2,128)(2,1)S(1)}, u32[]{:S(2)}, u32[]{:S(2)}) collective-permute-start(bf16[2,1024]{1,0:T(2,128)(2,1)S(1)} %get-tuple-element.49), channel_id=1, source_target_pairs={{1,15},{2,14},{3,13},{4,12},{5,11},{6,10},{7,9},{9,7},{10,6},{11,5... | collective-permute-start | bytes 12296 | tf_op jit(solution)/shard_map/ppermute | solution.py:625

commit v5 on v4

--- a/solution.py
+++ b/solution.py
@@ -21,6 +21,7 @@
 NT = (((1,), (1,)), ((), ()))
 BLOCKS = 4
 WIDE = N // BLOCKS
+BROAD = N // 2
 A_COST = 10**10
 B_COST = 10**10
 W_COST = 4 * 10**10
@@ -272,9 +273,9 @@
         left[lines, :middle] = jnp.concatenate([real, imag], axis=0).astype(BF)
         left[lines, middle:] = jnp.concatenate([imag, -real], axis=0).astype(BF)
 
-    sign = alternating((1, WIDE)).astype(F32)
-    for block in range(BLOCKS):
-        wide = slice(WIDE * block, WIDE * block + WIDE)
+    sign = alternating((1, BROAD)).astype(F32)
+    for block in range(N // BROAD):
+        wide = slice(BROAD * block, BROAD * block + BROAD)
         pieces = [table[:, wide] for table in (cos_0, cos_1, sin_0, sin_1)]
         halves = jnp.dot(
             left[...], jnp.concatenate(pieces, axis=0), preferred_element_type=F32
@@ -325,15 +326,15 @@
     copy = pltpu.make_async_copy(grad, grad_far, sem)
     copy.start()
     outer, inner = (0, 3), (1, 2)
-    sign = alternating((1, WIDE)).astype(BF)
-    top = rows_of((SLOTS, WIDE)) == 0
+    sign = alternating((1, BROAD)).astype(BF)
+    top = rows_of((SLOTS, BROAD)) == 0
     packed_row = jnp.logical_and(top, me == 0)
     lone, flipped = special_rows(special)
     lone_re, lone_im = 0.5 * lone[0:1], 0.5 * lone[8:9]
     flip_re, flip_im = 0.5 * flipped[0:1], -0.5 * flipped[8:9]
     patched_row = jnp.logical_and(top, jnp.logical_and(me > 0, me < RANKS // 2))
-    for block in range(BLOCKS):
-        wide = slice(WIDE * block, WIDE * block + WIDE)
+    for block in range(N // BROAD):
+        wide = slice(BROAD * block, BROAD * block + BROAD)
         values = spec[:, wide].astype(F32)
         h_re = filt[0, :, wide] + jnp.where(patched_row, flip_re[:, wide], 0.0)
         h_im = filt[1, :, wide] + jnp.where(patched_row, flip_im[:, wide], 0.0)

time: 68.2 us -> 67.9 us (level)
  no operation moved by 1% of the time
where the time goes in v5:
time: 67.9 us; the launch traced here: 67.4 us
  starting transfers between devices  36.7 us (54%)
  Pallas kernels  15.8 us (23%)
  waiting for transfers between devices  14 us (21%)
  between operations  0.8 us (1%)
    ppermute x1, starting transfers between devices, local(): other_rows = lax.ppermute(filter_rows, 'ctx', mirror_of)  10.6 us
    all_to_all x1, waiting for transfers between devices, local(): lax.all_to_all(unturned.reshape(2 * RANKS, ROWS, 128), ('core', 'ctx'), 0...  7.58 us
    all_to_all x1, waiting for transfers between devices, local(): lax.all_to_all(turned.reshape(2 * RANKS, ROWS, 128), ('core', 'ctx'), 0,...  6.45 us
    all_to_all x1, starting transfers between devices, local(): lax.all_to_all(unturned.reshape(2 * RANKS, ROWS, 128), ('core', 'ctx'), 0...  5.63 us
    all_to_all x1, starting transfers between devices, local(): lax.all_to_all(turned.reshape(2 * RANKS, ROWS, 128), ('core', 'ctx'), 0,...  5.53 us
    ppermute x1, starting transfers between devices, local(): mirror_grad = lax.ppermute(grad_low, 'ctx', mirror_of)  5.21 us
    ppermute x1, starting transfers between devices, local(): mirror_row = lax.ppermute(grad_row, 'ctx', special_of)  4.93 us
    ppermute x1, starting transfers between devices, local(): other_row = lax.ppermute(filter_row, 'ctx', special_of)  4.8 us
  transfers between devices with their start and end apart: 6, of which 2 were waited for; matrix products, arithmetic and copies ran while one was open for 0% of the time, Pallas kernels for 18%

profile of v5, /device:TPU:1, one launch (start us, length us, event | category | flops | bytes accessed | tf_op | source)
XLA Modules:
  0.0 67.4 jit_solution(10309227349097319839)
XLA Ops:
  0.6 1.7 %gather.1 = (bf16[64,1024]{1,0:T(8,128)(2,1)S(1)}, bf16[2,1024]{1,0:T(2,128)(2,1)S(1)}, bf16[512,512]{1,0:T(8,128)(2,1)S(1)}, bf16[1024,512]{1,0:T(8,128)(2,1)S(1)}, f32[512,128]{1,0:T(8,128)S(1)}) custom-call(s32[1]{0:T(128)} %bitcast.rank, bf16[2,64,1024]{2,1,0:T(8,128)(2,1)} %first.1, bf16[2,64,1024]{2,1,0:T(8,128)(2,1)} %second.1, ...), custom_call_target="tpu_custom_call" | custom-call | flops 16777216 | bytes 1048576 | tf_op jit(solution)/shard_map/gather/pallas_call | solution.py:527
  2.4 10.6 %collective-permute-start = (bf16[64,1024]{1,0:T(8,128)(2,1)S(1)}, bf16[64,1024]{1,0:T(8,128)(2,1)S(1)}, u32[]{:S(2)}, u32[]{:S(2)}) collective-permute-start(bf16[64,1024]{1,0:T(8,128)(2,1)S(1)} %get-tuple-element.32), channel_id=1, source_target_pairs={{0,15},{1,14},{2,13},{3,12},{4,11},{5,10},{6,9},{7,8},{8,7},{9,6},... | collective-permute-start | bytes 393224 | tf_op jit(solution)/shard_map/ppermute | solution.py:557
  13.0 1.5 %sections.1 = (bf16[2,16,64,128]{3,2,1,0:T(8,128)(2,1)}, bf16[2,1024]{1,0:T(2,128)(2,1)S(1)}) custom-call(bf16[512,512]{1,0:T(8,128)(2,1)S(1)} %get-tuple-element.27.signals, bf16[1024,512]{1,0:T(8,128)(2,1)S(1)} %get-tuple-element.28.sections, f32[512,128]{1,0:T(8,128)S(1)} %get-tuple-element.29.turns, bf16[2,1024]{1,0:T(2,128)(2,1)S(1)} %get-tuple-element.30.row), custom_call_target="tpu_custom_call" | custom-call | flops 10000000000 | bytes 1048576 | tf_op jit(solution)/shard_map/sections/pallas_call | solution.py:558
  14.5 5.5 %all-to-all-start = ((bf16[32,64,128]{2,1,0:T(8,128)(2,1)}), bf16[32,64,128]{2,1,0:T(8,128)(2,1)S(1)}, u32[]{:S(2)}, u32[]{:S(2)}) async-start(bf16[32,64,128]{2,1,0:T(8,128)(2,1)} %bitcast.3), calls=%async_computation | async-start | bytes 1048576 | tf_op jit(solution)/shard_map/all_to_all | solution.py:572
  20.0 0.0 copy-start.1
  20.1 4.8 %collective-permute-start.1 = (bf16[2,1024]{1,0:T(2,128)(2,1)S(1)}, bf16[2,1024]{1,0:T(2,128)(2,1)S(1)}, u32[]{:S(2)}, u32[]{:S(2)}) collective-permute-start(bf16[2,1024]{1,0:T(2,128)(2,1)S(1)} %get-tuple-element.39), channel_id=1, source_target_pairs={{1,15},{2,14},{3,13},{4,12},{5,11},{6,10},{7,9},{9,7},{10,6},{11,5... | collective-permute-start | bytes 12296 | tf_op jit(solution)/shard_map/ppermute | solution.py:571
  24.9 0.0 collective-permute-done.after.other
  24.9 1.6 %bring_tables.1 = (bf16[256,1024]{1,0:T(8,128)(2,1)S(1)}, bf16[256,1024]{1,0:T(8,128)(2,1)S(1)}, bf16[256,1024]{1,0:T(8,128)(2,1)S(1)}, bf16[256,1024]{1,0:T(8,128)(2,1)S(1)}) custom-call(bf16[64,1024]{1,0:T(8,128)(2,1)S(1)} %collective-permute-done.after.other, bf16[4,256,1024]{2,1,0:T(8,128)(2,1)} %constant.14.clone.refs_0_), custom_call_target="tpu_custom_call" | custom-call | flops 40000000000 | bytes 1048576 | tf_op jit(solution)/shard_map/bring_tables/pallas_call | solution.py:576
  26.4 2.5 %fold_filter.1.filt_far = f32[2,32,1024]{2,1,0:T(8,128)} custom-call(s32[1]{0:T(128)} %bitcast.rank, f32[1,2,64,1024]{3,2,1,0:T(8,128)} %own.1, bf16[64,1024]{1,0:T(8,128)(2,1)S(1)} %collective-permute-done.after.other), custom_call_target="tpu_custom_call" | custom-call | flops 16777216 | bytes 1048576 | tf_op jit(solution)/shard_map/fold_filter/pallas_call | solution.py:586
  28.9 6.5 %all-to-all-done.turned = bf16[32,64,128]{2,1,0:T(8,128)(2,1)S(1)} async-done(((bf16[32,64,128]{2,1,0:T(8,128)(2,1)}), bf16[32,64,128]{2,1,0:T(8,128)(2,1)S(1)}, u32[]{:S(2)}, u32[]{:S(2)}) %all-to-all-start) | async-done | bytes 524320 | tf_op jit(solution)/shard_map/all_to_all | solution.py:572
  35.4 0.0 copy-done.1
  35.4 1.5 %spectra.1 = (bf16[272,1024]{1,0:T(8,128)(2,1)S(1)}, f32[2,32,1024]{2,1,0:T(8,128)S(1)}, bf16[64,1024]{1,0:T(8,128)(2,1)S(1)}, bf16[2,1024]{1,0:T(2,128)(2,1)S(1...) custom-call(s32[1]{0:T(128)} %bitcast.rank, bf16[32,64,128]{2,1,0:T(8,128)(2,1)S(1)} %all-to-all-done.turned, ...), custom_call_target="tpu_custom_call" | custom-call | flops 16777216 | bytes 1048576 | tf_op jit(solution)/shard_map/spectra/pallas_call | solution.py:597
  36.9 5.2 %collective-permute-start.2 = (bf16[64,1024]{1,0:T(8,128)(2,1)S(1)}, bf16[64,1024]{1,0:T(8,128)(2,1)S(1)}, u32[]{:S(2)}, u32[]{:S(2)}) collective-permute-start(bf16[64,1024]{1,0:T(8,128)(2,1)S(1)} %get-tuple-element.43), channel_id=1, source_target_pairs={{0,15},{1,14},{2,13},{3,12},{4,11},{5,10},{6,9},{7,8},{8,7},{9,6},... | collective-permute-start | bytes 393224 | tf_op jit(solution)/shard_map/ppermute | solution.py:625
  42.1 0.0 collective-permute-done.1.special
  42.1 2.5 %inverse.1 = (bf16[2,1024,128]{2,1,0:T(8,128)(2,1)}, f32[2,32,1024]{2,1,0:T(8,128)}) custom-call(s32[1]{0:T(128)} %bitcast.rank, bf16[272,1024]{1,0:T(8,128)(2,1)S(1)} %get-tuple-element.37.spec, f32[2,32,1024]{2,1,0:T(8,128)S(1)} %get-tuple-element.38.filt, bf16[2,1024]{1,0:T(2,128)(2,1)S(1)} %collective-permute-done.1.special, ...), custom_call_target="tpu_custom_call" | custom-call | flops 10000000000 | bytes 1048576 | tf_op jit(solution)/shard_map/inverse/pallas_call | solution.py:628
  44.6 5.6 %all-to-all-start.1 = ((bf16[32,64,128]{2,1,0:T(8,128)(2,1)}), bf16[32,64,128]{2,1,0:T(8,128)(2,1)S(1)}, u32[]{:S(2)}, u32[]{:S(2)}) async-start(bf16[32,64,128]{2,1,0:T(8,128)(2,1)} %bitcast.2), calls=%async_computation.1 | async-start | bytes 1048576 | tf_op jit(solution)/shard_map/all_to_all | solution.py:641
  50.3 0.0 copy-start
  50.3 4.9 %collective-permute-start.3 = (bf16[2,1024]{1,0:T(2,128)(2,1)S(1)}, bf16[2,1024]{1,0:T(2,128)(2,1)S(1)}, u32[]{:S(2)}, u32[]{:S(2)}) collective-permute-start(bf16[2,1024]{1,0:T(2,128)(2,1)S(1)} %get-tuple-element.49), channel_id=1, source_target_pairs={{1,15},{2,14},{3,13},{4,12},{5,11},{6,10},{7,9},{9,7},{10,6},{11,5... | collective-permute-start | bytes 12296 | tf_op jit(solution)/shard_map/ppermute | solution.py:626
  55.2 0.0 collective-permute-done.2.after.other
  55.2 1.5 %bring_near.1 = (bf16[1024,512]{1,0:T(8,128)(2,1)S(1)}, bf16[3,2,64,1024]{3,2,1,0:T(8,128)(2,1)S(1)}) custom-call(bf16[64,1024]{1,0:T(8,128)(2,1)S(1)} %collective-permute-done.2.after.other, bf16[1024,512]{1,0:T(8,128)(2,1)} %constant.15.clone.table, bf16[2,64,1024]{2,1,0:T(8,128)(2,1)} %first.1, bf16[2,64,1024]{2,1,0:T(8,128)(2,1)} %second.1, ...), custom_call_target="tpu_custom_call" | custom-call | flops 40000000000 | bytes 1048576 | tf_op jit(solution)/shard_map/bring_near/pallas_call | solution.py:645
  56.7 0.0 copy-done
  56.7 1.3 %assemble.1 = (f32[1,2,64,1024]{3,2,1,0:T(8,128)}, f32[2,8,1024]{2,1,0:T(8,128)S(1)}) custom-call(s32[1]{0:T(128)} %bitcast.rank, f32[2,32,1024]{2,1,0:T(8,128)S(1)} %copy-done, bf16[64,1024]{1,0:T(8,128)(2,1)S(1)} %collective-permute-done.2.after.other), custom_call_target="tpu_custom_call" | custom-call | flops 16777216 | bytes 1048576 | tf_op jit(solution)/shard_map/assemble/pallas_call | solution.py:655
  58.0 0.0 collective-permute-done.3.special
  58.0 7.6 %all-to-all-done.1.arrived = bf16[32,64,128]{2,1,0:T(8,128)(2,1)S(1)} async-done(((bf16[32,64,128]{2,1,0:T(8,128)(2,1)}), bf16[32,64,128]{2,1,0:T(8,128)(2,1)S(1)}, u32[]{:S(2)}, u32[]{:S(2)}) %all-to-all-start.1) | async-done | bytes 524320 | tf_op jit(solution)/shard_map/all_to_all | solution.py:641
  65.6 1.8 %results.1 = (bf16[2,64,1024]{2,1,0:T(8,128)(2,1)}, bf16[2,64,1024]{2,1,0:T(8,128)(2,1)}, bf16[2,64,1024]{2,1,0:T(8,128)(2,1)}, f32[1,2,64,1024]{3,2,1,0:T(8,128)}) custom-call(s32[1]{0:T(128)} %bitcast.rank, bf16[32,64,128]{2,1,0:T(8,128)(2,1)S(1)} %all-to-all-done.1.arrived, ...), custom_call_target="tpu_custom_call", output_to_operand_aliasing={{3}: (4, {})} | custom-call | flops 536870912 | bytes 1048576 | tf_op jit(solution)/shard_map/results/pallas_call | solution.py:669
Async XLA Ops:
  2.4 22.5 %collective-permute-start = (bf16[64,1024]{1,0:T(8,128)(2,1)S(1)}, bf16[64,1024]{1,0:T(8,128)(2,1)S(1)}, u32[]{:S(2)}, u32[]{:S(2)}) collective-permute-start(bf16[64,1024]{1,0:T(8,128)(2,1)S(1)} %get-tuple-element.32), channel_id=1, source_target_pairs={{0,15},{1,14},{2,13},{3,12},{4,11},{5,10},{6,9},{7,8},{8,7},{9,6},... | collective-permute-start | bytes 393224 | tf_op jit(solution)/shard_map/ppermute | solution.py:557
  14.5 20.9 %all-to-all-start = ((bf16[32,64,128]{2,1,0:T(8,128)(2,1)}), bf16[32,64,128]{2,1,0:T(8,128)(2,1)S(1)}, u32[]{:S(2)}, u32[]{:S(2)}) async-start(bf16[32,64,128]{2,1,0:T(8,128)(2,1)} %bitcast.3), calls=%async_computation | async-start | bytes 1048576 | tf_op jit(solution)/shard_map/all_to_all | solution.py:572
  20.0 15.3 %copy-start.1 = (f32[2,1024]{1,0:T(2,128)S(1)}, f32[2,1024]{1,0:T(2,128)}, u32[]{:S(2)}) copy-start(f32[2,1024]{1,0:T(2,128)} %constant.18.clone.half) | copy-start | bytes 24580
  20.1 22.1 %collective-permute-start.1 = (bf16[2,1024]{1,0:T(2,128)(2,1)S(1)}, bf16[2,1024]{1,0:T(2,128)(2,1)S(1)}, u32[]{:S(2)}, u32[]{:S(2)}) collective-permute-start(bf16[2,1024]{1,0:T(2,128)(2,1)S(1)} %get-tuple-element.39), channel_id=1, source_target_pairs={{1,15},{2,14},{3,13},{4,12},{5,11},{6,10},{7,9},{9,7},{10,6},{11,5... | collective-permute-start | bytes 12296 | tf_op jit(solution)/shard_map/ppermute | solution.py:571
  36.9 18.3 %collective-permute-start.2 = (bf16[64,1024]{1,0:T(8,128)(2,1)S(1)}, bf16[64,1024]{1,0:T(8,128)(2,1)S(1)}, u32[]{:S(2)}, u32[]{:S(2)}) collective-permute-start(bf16[64,1024]{1,0:T(8,128)(2,1)S(1)} %get-tuple-element.43), channel_id=1, source_target_pairs={{0,15},{1,14},{2,13},{3,12},{4,11},{5,10},{6,9},{7,8},{8,7},{9,6},... | collective-permute-start | bytes 393224 | tf_op jit(solution)/shard_map/ppermute | solution.py:625
  44.6 21.0 %all-to-all-start.1 = ((bf16[32,64,128]{2,1,0:T(8,128)(2,1)}), bf16[32,64,128]{2,1,0:T(8,128)(2,1)S(1)}, u32[]{:S(2)}, u32[]{:S(2)}) async-start(bf16[32,64,128]{2,1,0:T(8,128)(2,1)} %bitcast.2), calls=%async_computation.1 | async-start | bytes 1048576 | tf_op jit(solution)/shard_map/all_to_all | solution.py:641
  50.3 6.4 %copy-start = (f32[2,32,1024]{2,1,0:T(8,128)S(1)}, f32[2,32,1024]{2,1,0:T(8,128)}, u32[]{:S(2)}) copy-start(f32[2,32,1024]{2,1,0:T(8,128)} %get-tuple-element.46.own) | copy-start | bytes 786436
  50.3 7.7 %collective-permute-start.3 = (bf16[2,1024]{1,0:T(2,128)(2,1)S(1)}, bf16[2,1024]{1,0:T(2,128)(2,1)S(1)}, u32[]{:S(2)}, u32[]{:S(2)}) collective-permute-start(bf16[2,1024]{1,0:T(2,128)(2,1)S(1)} %get-tuple-element.49), channel_id=1, source_target_pairs={{1,15},{2,14},{3,13},{4,12},{5,11},{6,10},{7,9},{9,7},{10,6},{11,5... | collective-permute-start | bytes 12296 | tf_op jit(solution)/shard_map/ppermute | solution.py:626

commit v6 on v5

--- a/solution.py
+++ b/solution.py
@@ -320,11 +320,13 @@
 
 
 def inverse_kernel(
-    rank, spec, filt, special, cos_0, cos_1, sin_0, sin_1, turn, grad, out, grad_far, total, sem
+    rank, spec, filt, special, cos_0, cos_1, sin_0, sin_1, turn, grad,
+    out, grad_far, total, ready, sems
 ):
     me = rank[0]
-    copy = pltpu.make_async_copy(grad, grad_far, sem)
+    copy = pltpu.make_async_copy(grad, grad_far, sems.at[0])
     copy.start()
+    out_copies = []
     outer, inner = (0, 3), (1, 2)
     sign = alternating((1, BROAD)).astype(BF)
     top = rows_of((SLOTS, BROAD)) == 0
@@ -401,8 +403,15 @@
         packed = jnp.logical_and(lanes_of((WIDE, 128)) % SLOTS == 0, me == 0)
         un_im = jnp.where(packed, imag * turn_sin, 2.0 * un_im).astype(BF)
         un_re = jnp.where(packed, real, 2.0 * un_re).astype(BF)
-        out[0, rows, :] = jnp.concatenate([un_re[:, :64], un_im[:, :64]], axis=1)
-        out[1, rows, :] = jnp.concatenate([un_re[:, 64:], un_im[:, 64:]], axis=1)
+        ready[0, rows, :] = jnp.concatenate([un_re[:, :64], un_im[:, :64]], axis=1)
+        ready[1, rows, :] = jnp.concatenate([un_re[:, 64:], un_im[:, 64:]], axis=1)
+        place = pl.ds(WIDE * piece, WIDE)
+        out_copies.append(
+            pltpu.make_async_copy(ready.at[:, place], out.at[:, place], sems.at[1 + piece])
+        )
+        out_copies[-1].start()
+    for out_copy in out_copies:
+        out_copy.wait()
     copy.wait()
 
 
@@ -628,12 +637,16 @@
     unturned, grad_far = pl.pallas_call(
         inverse_kernel,
         out_shape=[
-            jax.ShapeDtypeStruct((2, N, 128), BF),
+            pltpu.HBM((2, N, 128), BF),
             pltpu.HBM((2, SLOTS, N), F32),
         ],
         in_specs=[SMEM] + [VMEM] * 9,
-        out_specs=[VMEM, HBM],
-        scratch_shapes=[pltpu.VMEM((N, 256), F32), pltpu.SemaphoreType.DMA(())],
+        out_specs=[HBM, HBM],
+        scratch_shapes=[
+            pltpu.VMEM((N, 256), F32),
+            pltpu.VMEM((2, N, 128), BF),
+            pltpu.SemaphoreType.DMA((1 + BLOCKS,)),
+        ],
         compiler_params=params(24),
         cost_estimate=sizes(B_COST),
         name="inverse",

time: 67.9 us -> 67.9 us (level)
  no operation moved by 1% of the time
where the time goes in v6:
time: 67.9 us; the launch traced here: 67.3 us
  starting transfers between devices  36.7 us (54%)
  Pallas kernels  15.7 us (23%)
  waiting for transfers between devices  14 us (21%)
  between operations  0.8 us (1%)
    ppermute x1, starting transfers between devices, local(): other_rows = lax.ppermute(filter_rows, 'ctx', mirror_of)  10.6 us
    all_to_all x1, waiting for transfers between devices, local(): lax.all_to_all(unturned.reshape(2 * RANKS, ROWS, 128), ('core', 'ctx'), 0...  7.58 us
    all_to_all x1, waiting for transfers between devices, local(): lax.all_to_all(turned.reshape(2 * RANKS, ROWS, 128), ('core', 'ctx'), 0,...  6.45 us
    all_to_all x1, starting transfers between devices, local(): lax.all_to_all(unturned.reshape(2 * RANKS, ROWS, 128), ('core', 'ctx'), 0...  5.63 us
    all_to_all x1, starting transfers between devices, local(): lax.all_to_all(turned.reshape(2 * RANKS, ROWS, 128), ('core', 'ctx'), 0,...  5.53 us
    ppermute x1, starting transfers between devices, local(): mirror_grad = lax.ppermute(grad_low, 'ctx', mirror_of)  5.21 us
    ppermute x1, starting transfers between devices, local(): mirror_row = lax.ppermute(grad_row, 'ctx', special_of)  4.93 us
    ppermute x1, starting transfers between devices, local(): other_row = lax.ppermute(filter_row, 'ctx', special_of)  4.8 us
  transfers between devices with their start and end apart: 6, of which 2 were waited for; matrix products, arithmetic and copies ran while one was open for 0% of the time, Pallas kernels for 18%

profile of v6, /device:TPU:1, one launch (start us, length us, event | category | flops | bytes accessed | tf_op | source)
XLA Modules:
  0.0 67.3 jit_solution(1070089603638722226)
XLA Ops:
  0.6 1.7 %gather.1 = (bf16[64,1024]{1,0:T(8,128)(2,1)S(1)}, bf16[2,1024]{1,0:T(2,128)(2,1)S(1)}, bf16[512,512]{1,0:T(8,128)(2,1)S(1)}, bf16[1024,512]{1,0:T(8,128)(2,1)S(1)}, f32[512,128]{1,0:T(8,128)S(1)}) custom-call(s32[1]{0:T(128)} %bitcast.rank, bf16[2,64,1024]{2,1,0:T(8,128)(2,1)} %first.1, bf16[2,64,1024]{2,1,0:T(8,128)(2,1)} %second.1, ...), custom_call_target="tpu_custom_call" | custom-call | flops 16777216 | bytes 1048576 | tf_op jit(solution)/shard_map/gather/pallas_call | solution.py:536
  2.4 10.6 %collective-permute-start = (bf16[64,1024]{1,0:T(8,128)(2,1)S(1)}, bf16[64,1024]{1,0:T(8,128)(2,1)S(1)}, u32[]{:S(2)}, u32[]{:S(2)}) collective-permute-start(bf16[64,1024]{1,0:T(8,128)(2,1)S(1)} %get-tuple-element.32), channel_id=1, source_target_pairs={{0,15},{1,14},{2,13},{3,12},{4,11},{5,10},{6,9},{7,8},{8,7},{9,6},... | collective-permute-start | bytes 393224 | tf_op jit(solution)/shard_map/ppermute | solution.py:566
  13.0 1.5 %sections.1 = (bf16[2,16,64,128]{3,2,1,0:T(8,128)(2,1)}, bf16[2,1024]{1,0:T(2,128)(2,1)S(1)}) custom-call(bf16[512,512]{1,0:T(8,128)(2,1)S(1)} %get-tuple-element.27.signals, bf16[1024,512]{1,0:T(8,128)(2,1)S(1)} %get-tuple-element.28.sections, f32[512,128]{1,0:T(8,128)S(1)} %get-tuple-element.29.turns, bf16[2,1024]{1,0:T(2,128)(2,1)S(1)} %get-tuple-element.30.row), custom_call_target="tpu_custom_call" | custom-call | flops 10000000000 | bytes 1048576 | tf_op jit(solution)/shard_map/sections/pallas_call | solution.py:567
  14.5 5.5 %all-to-all-start = ((bf16[32,64,128]{2,1,0:T(8,128)(2,1)}), bf16[32,64,128]{2,1,0:T(8,128)(2,1)S(1)}, u32[]{:S(2)}, u32[]{:S(2)}) async-start(bf16[32,64,128]{2,1,0:T(8,128)(2,1)} %bitcast.4), calls=%async_computation | async-start | bytes 1048576 | tf_op jit(solution)/shard_map/all_to_all | solution.py:581
  20.0 0.0 copy-start.1
  20.1 4.8 %collective-permute-start.1 = (bf16[2,1024]{1,0:T(2,128)(2,1)S(1)}, bf16[2,1024]{1,0:T(2,128)(2,1)S(1)}, u32[]{:S(2)}, u32[]{:S(2)}) collective-permute-start(bf16[2,1024]{1,0:T(2,128)(2,1)S(1)} %get-tuple-element.39), channel_id=1, source_target_pairs={{1,15},{2,14},{3,13},{4,12},{5,11},{6,10},{7,9},{9,7},{10,6},{11,5... | collective-permute-start | bytes 12296 | tf_op jit(solution)/shard_map/ppermute | solution.py:580
  24.9 0.0 collective-permute-done.after.other
  24.9 1.6 %bring_tables.1 = (bf16[256,1024]{1,0:T(8,128)(2,1)S(1)}, bf16[256,1024]{1,0:T(8,128)(2,1)S(1)}, bf16[256,1024]{1,0:T(8,128)(2,1)S(1)}, bf16[256,1024]{1,0:T(8,128)(2,1)S(1)}) custom-call(bf16[64,1024]{1,0:T(8,128)(2,1)S(1)} %collective-permute-done.after.other, bf16[4,256,1024]{2,1,0:T(8,128)(2,1)} %constant.14.clone.refs_0_), custom_call_target="tpu_custom_call" | custom-call | flops 40000000000 | bytes 1048576 | tf_op jit(solution)/shard_map/bring_tables/pallas_call | solution.py:585
  26.4 2.5 %fold_filter.1.filt_far = f32[2,32,1024]{2,1,0:T(8,128)} custom-call(s32[1]{0:T(128)} %bitcast.rank, f32[1,2,64,1024]{3,2,1,0:T(8,128)} %own.1, bf16[64,1024]{1,0:T(8,128)(2,1)S(1)} %collective-permute-done.after.other), custom_call_target="tpu_custom_call" | custom-call | flops 16777216 | bytes 1048576 | tf_op jit(solution)/shard_map/fold_filter/pallas_call | solution.py:595
  28.9 6.5 %all-to-all-done.turned = bf16[32,64,128]{2,1,0:T(8,128)(2,1)S(1)} async-done(((bf16[32,64,128]{2,1,0:T(8,128)(2,1)}), bf16[32,64,128]{2,1,0:T(8,128)(2,1)S(1)}, u32[]{:S(2)}, u32[]{:S(2)}) %all-to-all-start) | async-done | bytes 524320 | tf_op jit(solution)/shard_map/all_to_all | solution.py:581
  35.4 0.0 copy-done.1
  35.4 1.5 %spectra.1 = (bf16[272,1024]{1,0:T(8,128)(2,1)S(1)}, f32[2,32,1024]{2,1,0:T(8,128)S(1)}, bf16[64,1024]{1,0:T(8,128)(2,1)S(1)}, bf16[2,1024]{1,0:T(2,128)(2,1)S(1...) custom-call(s32[1]{0:T(128)} %bitcast.rank, bf16[32,64,128]{2,1,0:T(8,128)(2,1)S(1)} %all-to-all-done.turned, ...), custom_call_target="tpu_custom_call" | custom-call | flops 16777216 | bytes 1048576 | tf_op jit(solution)/shard_map/spectra/pallas_call | solution.py:606
  36.9 5.2 %collective-permute-start.2 = (bf16[64,1024]{1,0:T(8,128)(2,1)S(1)}, bf16[64,1024]{1,0:T(8,128)(2,1)S(1)}, u32[]{:S(2)}, u32[]{:S(2)}) collective-permute-start(bf16[64,1024]{1,0:T(8,128)(2,1)S(1)} %get-tuple-element.43), channel_id=1, source_target_pairs={{0,15},{1,14},{2,13},{3,12},{4,11},{5,10},{6,9},{7,8},{8,7},{9,6},... | collective-permute-start | bytes 393224 | tf_op jit(solution)/shard_map/ppermute | solution.py:634
  42.1 0.0 collective-permute-done.1.special
  42.1 2.5 %inverse.1 = (bf16[2,1024,128]{2,1,0:T(8,128)(2,1)}, f32[2,32,1024]{2,1,0:T(8,128)}) custom-call(s32[1]{0:T(128)} %bitcast.rank, bf16[272,1024]{1,0:T(8,128)(2,1)S(1)} %get-tuple-element.37.spec, f32[2,32,1024]{2,1,0:T(8,128)S(1)} %get-tuple-element.38.filt, bf16[2,1024]{1,0:T(2,128)(2,1)S(1)} %collective-permute-done.1.special, ...), custom_call_target="tpu_custom_call" | custom-call | flops 10000000000 | bytes 1048576 | tf_op jit(solution)/shard_map/inverse/pallas_call | solution.py:637
  44.6 5.6 %all-to-all-start.1 = ((bf16[32,64,128]{2,1,0:T(8,128)(2,1)}), bf16[32,64,128]{2,1,0:T(8,128)(2,1)S(1)}, u32[]{:S(2)}, u32[]{:S(2)}) async-start(bf16[32,64,128]{2,1,0:T(8,128)(2,1)} %bitcast.3), calls=%async_computation.1 | async-start | bytes 1048576 | tf_op jit(solution)/shard_map/all_to_all | solution.py:654
  50.2 0.0 copy-start
  50.2 4.9 %collective-permute-start.3 = (bf16[2,1024]{1,0:T(2,128)(2,1)S(1)}, bf16[2,1024]{1,0:T(2,128)(2,1)S(1)}, u32[]{:S(2)}, u32[]{:S(2)}) collective-permute-start(bf16[2,1024]{1,0:T(2,128)(2,1)S(1)} %get-tuple-element.49), channel_id=1, source_target_pairs={{1,15},{2,14},{3,13},{4,12},{5,11},{6,10},{7,9},{9,7},{10,6},{11,5... | collective-permute-start | bytes 12296 | tf_op jit(solution)/shard_map/ppermute | solution.py:635
  55.2 0.0 collective-permute-done.2.after.other
  55.2 1.5 %bring_near.1 = (bf16[1024,512]{1,0:T(8,128)(2,1)S(1)}, bf16[3,2,64,1024]{3,2,1,0:T(8,128)(2,1)S(1)}) custom-call(bf16[64,1024]{1,0:T(8,128)(2,1)S(1)} %collective-permute-done.2.after.other, bf16[1024,512]{1,0:T(8,128)(2,1)} %constant.15.clone.table, bf16[2,64,1024]{2,1,0:T(8,128)(2,1)} %first.1, bf16[2,64,1024]{2,1,0:T(8,128)(2,1)} %second.1, ...), custom_call_target="tpu_custom_call" | custom-call | flops 40000000000 | bytes 1048576 | tf_op jit(solution)/shard_map/bring_near/pallas_call | solution.py:658
  56.7 0.0 copy-done
  56.7 1.3 %assemble.1 = (f32[1,2,64,1024]{3,2,1,0:T(8,128)}, f32[2,8,1024]{2,1,0:T(8,128)S(1)}) custom-call(s32[1]{0:T(128)} %bitcast.rank, f32[2,32,1024]{2,1,0:T(8,128)S(1)} %copy-done, bf16[64,1024]{1,0:T(8,128)(2,1)S(1)} %collective-permute-done.2.after.other), custom_call_target="tpu_custom_call" | custom-call | flops 16777216 | bytes 1048576 | tf_op jit(solution)/shard_map/assemble/pallas_call | solution.py:668
  58.0 0.0 collective-permute-done.3.special
  58.0 7.6 %all-to-all-done.1.arrived = bf16[32,64,128]{2,1,0:T(8,128)(2,1)S(1)} async-done(((bf16[32,64,128]{2,1,0:T(8,128)(2,1)}), bf16[32,64,128]{2,1,0:T(8,128)(2,1)S(1)}, u32[]{:S(2)}, u32[]{:S(2)}) %all-to-all-start.1) | async-done | bytes 524320 | tf_op jit(solution)/shard_map/all_to_all | solution.py:654
  65.6 1.8 %results.1 = (bf16[2,64,1024]{2,1,0:T(8,128)(2,1)}, bf16[2,64,1024]{2,1,0:T(8,128)(2,1)}, bf16[2,64,1024]{2,1,0:T(8,128)(2,1)}, f32[1,2,64,1024]{3,2,1,0:T(8,128)}) custom-call(s32[1]{0:T(128)} %bitcast.rank, bf16[32,64,128]{2,1,0:T(8,128)(2,1)S(1)} %all-to-all-done.1.arrived, ...), custom_call_target="tpu_custom_call", output_to_operand_aliasing={{3}: (4, {})} | custom-call | flops 536870912 | bytes 1048576 | tf_op jit(solution)/shard_map/results/pallas_call | solution.py:682
Async XLA Ops:
  2.4 22.5 %collective-permute-start = (bf16[64,1024]{1,0:T(8,128)(2,1)S(1)}, bf16[64,1024]{1,0:T(8,128)(2,1)S(1)}, u32[]{:S(2)}, u32[]{:S(2)}) collective-permute-start(bf16[64,1024]{1,0:T(8,128)(2,1)S(1)} %get-tuple-element.32), channel_id=1, source_target_pairs={{0,15},{1,14},{2,13},{3,12},{4,11},{5,10},{6,9},{7,8},{8,7},{9,6},... | collective-permute-start | bytes 393224 | tf_op jit(solution)/shard_map/ppermute | solution.py:566
  14.5 20.9 %all-to-all-start = ((bf16[32,64,128]{2,1,0:T(8,128)(2,1)}), bf16[32,64,128]{2,1,0:T(8,128)(2,1)S(1)}, u32[]{:S(2)}, u32[]{:S(2)}) async-start(bf16[32,64,128]{2,1,0:T(8,128)(2,1)} %bitcast.4), calls=%async_computation | async-start | bytes 1048576 | tf_op jit(solution)/shard_map/all_to_all | solution.py:581
  20.0 15.3 %copy-start.1 = (f32[2,1024]{1,0:T(2,128)S(1)}, f32[2,1024]{1,0:T(2,128)}, u32[]{:S(2)}) copy-start(f32[2,1024]{1,0:T(2,128)} %constant.18.clone.half) | copy-start | bytes 24580
  20.1 22.1 %collective-permute-start.1 = (bf16[2,1024]{1,0:T(2,128)(2,1)S(1)}, bf16[2,1024]{1,0:T(2,128)(2,1)S(1)}, u32[]{:S(2)}, u32[]{:S(2)}) collective-permute-start(bf16[2,1024]{1,0:T(2,128)(2,1)S(1)} %get-tuple-element.39), channel_id=1, source_target_pairs={{1,15},{2,14},{3,13},{4,12},{5,11},{6,10},{7,9},{9,7},{10,6},{11,5... | collective-permute-start | bytes 12296 | tf_op jit(solution)/shard_map/ppermute | solution.py:580
  36.9 18.3 %collective-permute-start.2 = (bf16[64,1024]{1,0:T(8,128)(2,1)S(1)}, bf16[64,1024]{1,0:T(8,128)(2,1)S(1)}, u32[]{:S(2)}, u32[]{:S(2)}) collective-permute-start(bf16[64,1024]{1,0:T(8,128)(2,1)S(1)} %get-tuple-element.43), channel_id=1, source_target_pairs={{0,15},{1,14},{2,13},{3,12},{4,11},{5,10},{6,9},{7,8},{8,7},{9,6},... | collective-permute-start | bytes 393224 | tf_op jit(solution)/shard_map/ppermute | solution.py:634
  44.6 21.0 %all-to-all-start.1 = ((bf16[32,64,128]{2,1,0:T(8,128)(2,1)}), bf16[32,64,128]{2,1,0:T(8,128)(2,1)S(1)}, u32[]{:S(2)}, u32[]{:S(2)}) async-start(bf16[32,64,128]{2,1,0:T(8,128)(2,1)} %bitcast.3), calls=%async_computation.1 | async-start | bytes 1048576 | tf_op jit(solution)/shard_map/all_to_all | solution.py:654
  50.2 6.4 %copy-start = (f32[2,32,1024]{2,1,0:T(8,128)S(1)}, f32[2,32,1024]{2,1,0:T(8,128)}, u32[]{:S(2)}) copy-start(f32[2,32,1024]{2,1,0:T(8,128)} %get-tuple-element.46.own) | copy-start | bytes 786436
  50.2 7.7 %collective-permute-start.3 = (bf16[2,1024]{1,0:T(2,128)(2,1)S(1)}, bf16[2,1024]{1,0:T(2,128)(2,1)S(1)}, u32[]{:S(2)}, u32[]{:S(2)}) collective-permute-start(bf16[2,1024]{1,0:T(2,128)(2,1)S(1)} %get-tuple-element.49), channel_id=1, source_target_pairs={{1,15},{2,14},{3,13},{4,12},{5,11},{6,10},{7,9},{9,7},{10,6},{11,5... | collective-permute-start | bytes 12296 | tf_op jit(solution)/shard_map/ppermute | solution.py:635

commit v7 on v6

--- a/solution.py
+++ b/solution.py
@@ -21,7 +21,7 @@
 NT = (((1,), (1,)), ((), ()))
 BLOCKS = 4
 WIDE = N // BLOCKS
-BROAD = N // 2
+BROAD = N
 A_COST = 10**10
 B_COST = 10**10
 W_COST = 4 * 10**10

time: 67.9 us -> 68.4 us (level)
  transfers between devices with their start and end apart: 6 -> 6, of which waited for: 2 -> 2; matrix products, arithmetic and copies ran while one was open for 0% -> 0% of each run, Pallas kernels for 18% -> 19%
where the time goes in v7:
time: 68.4 us; the launch traced here: 67.8 us
  starting transfers between devices  36.7 us (54%)
  Pallas kernels  16.3 us (24%)
  waiting for transfers between devices  14 us (20%)
  between operations  0.8 us (1%)
    ppermute x1, starting transfers between devices, local(): other_rows = lax.ppermute(filter_rows, 'ctx', mirror_of)  10.6 us
    all_to_all x1, waiting for transfers between devices, local(): lax.all_to_all(unturned.reshape(2 * RANKS, ROWS, 128), ('core', 'ctx'), 0...  7.58 us
    all_to_all x1, waiting for transfers between devices, local(): lax.all_to_all(turned.reshape(2 * RANKS, ROWS, 128), ('core', 'ctx'), 0,...  6.45 us
    all_to_all x1, starting transfers between devices, local(): lax.all_to_all(unturned.reshape(2 * RANKS, ROWS, 128), ('core', 'ctx'), 0...  5.63 us
    all_to_all x1, starting transfers between devices, local(): lax.all_to_all(turned.reshape(2 * RANKS, ROWS, 128), ('core', 'ctx'), 0,...  5.53 us
    ppermute x1, starting transfers between devices, local(): mirror_grad = lax.ppermute(grad_low, 'ctx', mirror_of)  5.2 us
    ppermute x1, starting transfers between devices, local(): mirror_row = lax.ppermute(grad_row, 'ctx', special_of)  4.93 us
    ppermute x1, starting transfers between devices, local(): other_row = lax.ppermute(filter_row, 'ctx', special_of)  4.8 us
  transfers between devices with their start and end apart: 6, of which 2 were waited for; matrix products, arithmetic and copies ran while one was open for 0% of the time, Pallas kernels for 19%

profile of v7, /device:TPU:1, one launch (start us, length us, event | category | flops | bytes accessed | tf_op | source)
XLA Modules:
  0.0 67.8 jit_solution(1225891465637919806)
XLA Ops:
  0.6 1.7 %gather.1 = (bf16[64,1024]{1,0:T(8,128)(2,1)S(1)}, bf16[2,1024]{1,0:T(2,128)(2,1)S(1)}, bf16[512,512]{1,0:T(8,128)(2,1)S(1)}, bf16[1024,512]{1,0:T(8,128)(2,1)S(1)}, f32[512,128]{1,0:T(8,128)S(1)}) custom-call(s32[1]{0:T(128)} %bitcast.rank, bf16[2,64,1024]{2,1,0:T(8,128)(2,1)} %first.1, bf16[2,64,1024]{2,1,0:T(8,128)(2,1)} %second.1, ...), custom_call_target="tpu_custom_call" | custom-call | flops 16777216 | bytes 1048576 | tf_op jit(solution)/shard_map/gather/pallas_call | solution.py:536
  2.4 10.6 %collective-permute-start = (bf16[64,1024]{1,0:T(8,128)(2,1)S(1)}, bf16[64,1024]{1,0:T(8,128)(2,1)S(1)}, u32[]{:S(2)}, u32[]{:S(2)}) collective-permute-start(bf16[64,1024]{1,0:T(8,128)(2,1)S(1)} %get-tuple-element.32), channel_id=1, source_target_pairs={{0,15},{1,14},{2,13},{3,12},{4,11},{5,10},{6,9},{7,8},{8,7},{9,6},... | collective-permute-start | bytes 393224 | tf_op jit(solution)/shard_map/ppermute | solution.py:566
  13.0 1.5 %sections.1 = (bf16[2,16,64,128]{3,2,1,0:T(8,128)(2,1)}, bf16[2,1024]{1,0:T(2,128)(2,1)S(1)}) custom-call(bf16[512,512]{1,0:T(8,128)(2,1)S(1)} %get-tuple-element.27.signals, bf16[1024,512]{1,0:T(8,128)(2,1)S(1)} %get-tuple-element.28.sections, f32[512,128]{1,0:T(8,128)S(1)} %get-tuple-element.29.turns, bf16[2,1024]{1,0:T(2,128)(2,1)S(1)} %get-tuple-element.30.row), custom_call_target="tpu_custom_call" | custom-call | flops 10000000000 | bytes 1048576 | tf_op jit(solution)/shard_map/sections/pallas_call | solution.py:567
  14.5 5.5 %all-to-all-start = ((bf16[32,64,128]{2,1,0:T(8,128)(2,1)}), bf16[32,64,128]{2,1,0:T(8,128)(2,1)S(1)}, u32[]{:S(2)}, u32[]{:S(2)}) async-start(bf16[32,64,128]{2,1,0:T(8,128)(2,1)} %bitcast.4), calls=%async_computation | async-start | bytes 1048576 | tf_op jit(solution)/shard_map/all_to_all | solution.py:581
  20.0 0.0 copy-start.1
  20.1 4.8 %collective-permute-start.1 = (bf16[2,1024]{1,0:T(2,128)(2,1)S(1)}, bf16[2,1024]{1,0:T(2,128)(2,1)S(1)}, u32[]{:S(2)}, u32[]{:S(2)}) collective-permute-start(bf16[2,1024]{1,0:T(2,128)(2,1)S(1)} %get-tuple-element.39), channel_id=1, source_target_pairs={{1,15},{2,14},{3,13},{4,12},{5,11},{6,10},{7,9},{9,7},{10,6},{11,5... | collective-permute-start | bytes 12296 | tf_op jit(solution)/shard_map/ppermute | solution.py:580
  24.9 0.0 collective-permute-done.after.other
  24.9 1.6 %bring_tables.1 = (bf16[256,1024]{1,0:T(8,128)(2,1)S(1)}, bf16[256,1024]{1,0:T(8,128)(2,1)S(1)}, bf16[256,1024]{1,0:T(8,128)(2,1)S(1)}, bf16[256,1024]{1,0:T(8,128)(2,1)S(1)}) custom-call(bf16[64,1024]{1,0:T(8,128)(2,1)S(1)} %collective-permute-done.after.other, bf16[4,256,1024]{2,1,0:T(8,128)(2,1)} %constant.14.clone.refs_0_), custom_call_target="tpu_custom_call" | custom-call | flops 40000000000 | bytes 1048576 | tf_op jit(solution)/shard_map/bring_tables/pallas_call | solution.py:585
  26.4 2.5 %fold_filter.1.filt_far = f32[2,32,1024]{2,1,0:T(8,128)} custom-call(s32[1]{0:T(128)} %bitcast.rank, f32[1,2,64,1024]{3,2,1,0:T(8,128)} %own.1, bf16[64,1024]{1,0:T(8,128)(2,1)S(1)} %collective-permute-done.after.other), custom_call_target="tpu_custom_call" | custom-call | flops 16777216 | bytes 1048576 | tf_op jit(solution)/shard_map/fold_filter/pallas_call | solution.py:595
  28.9 6.5 %all-to-all-done.turned = bf16[32,64,128]{2,1,0:T(8,128)(2,1)S(1)} async-done(((bf16[32,64,128]{2,1,0:T(8,128)(2,1)}), bf16[32,64,128]{2,1,0:T(8,128)(2,1)S(1)}, u32[]{:S(2)}, u32[]{:S(2)}) %all-to-all-start) | async-done | bytes 524320 | tf_op jit(solution)/shard_map/all_to_all | solution.py:581
  35.4 0.0 copy-done.1
  35.4 2.0 %spectra.1 = (bf16[272,1024]{1,0:T(8,128)(2,1)S(1)}, f32[2,32,1024]{2,1,0:T(8,128)S(1)}, bf16[64,1024]{1,0:T(8,128)(2,1)S(1)}, bf16[2,1024]{1,0:T(2,128)(2,1)S(1...) custom-call(s32[1]{0:T(128)} %bitcast.rank, bf16[32,64,128]{2,1,0:T(8,128)(2,1)S(1)} %all-to-all-done.turned, ...), custom_call_target="tpu_custom_call" | custom-call | flops 16777216 | bytes 1048576 | tf_op jit(solution)/shard_map/spectra/pallas_call | solution.py:606
  37.4 5.2 %collective-permute-start.2 = (bf16[64,1024]{1,0:T(8,128)(2,1)S(1)}, bf16[64,1024]{1,0:T(8,128)(2,1)S(1)}, u32[]{:S(2)}, u32[]{:S(2)}) collective-permute-start(bf16[64,1024]{1,0:T(8,128)(2,1)S(1)} %get-tuple-element.43), channel_id=1, source_target_pairs={{0,15},{1,14},{2,13},{3,12},{4,11},{5,10},{6,9},{7,8},{8,7},{9,6},... | collective-permute-start | bytes 393224 | tf_op jit(solution)/shard_map/ppermute | solution.py:634
  42.6 0.0 collective-permute-done.1.special
  42.6 2.5 %inverse.1 = (bf16[2,1024,128]{2,1,0:T(8,128)(2,1)}, f32[2,32,1024]{2,1,0:T(8,128)}) custom-call(s32[1]{0:T(128)} %bitcast.rank, bf16[272,1024]{1,0:T(8,128)(2,1)S(1)} %get-tuple-element.37.spec, f32[2,32,1024]{2,1,0:T(8,128)S(1)} %get-tuple-element.38.filt, bf16[2,1024]{1,0:T(2,128)(2,1)S(1)} %collective-permute-done.1.special, ...), custom_call_target="tpu_custom_call" | custom-call | flops 10000000000 | bytes 1048576 | tf_op jit(solution)/shard_map/inverse/pallas_call | solution.py:637
  45.1 5.6 %all-to-all-start.1 = ((bf16[32,64,128]{2,1,0:T(8,128)(2,1)}), bf16[32,64,128]{2,1,0:T(8,128)(2,1)S(1)}, u32[]{:S(2)}, u32[]{:S(2)}) async-start(bf16[32,64,128]{2,1,0:T(8,128)(2,1)} %bitcast.3), calls=%async_computation.1 | async-start | bytes 1048576 | tf_op jit(solution)/shard_map/all_to_all | solution.py:654
  50.7 0.0 copy-start
  50.8 4.9 %collective-permute-start.3 = (bf16[2,1024]{1,0:T(2,128)(2,1)S(1)}, bf16[2,1024]{1,0:T(2,128)(2,1)S(1)}, u32[]{:S(2)}, u32[]{:S(2)}) collective-permute-start(bf16[2,1024]{1,0:T(2,128)(2,1)S(1)} %get-tuple-element.49), channel_id=1, source_target_pairs={{1,15},{2,14},{3,13},{4,12},{5,11},{6,10},{7,9},{9,7},{10,6},{11,5... | collective-permute-start | bytes 12296 | tf_op jit(solution)/shard_map/ppermute | solution.py:635
  55.7 0.0 collective-permute-done.2.after.other
  55.7 1.5 %bring_near.1 = (bf16[1024,512]{1,0:T(8,128)(2,1)S(1)}, bf16[3,2,64,1024]{3,2,1,0:T(8,128)(2,1)S(1)}) custom-call(bf16[64,1024]{1,0:T(8,128)(2,1)S(1)} %collective-permute-done.2.after.other, bf16[1024,512]{1,0:T(8,128)(2,1)} %constant.15.clone.table, bf16[2,64,1024]{2,1,0:T(8,128)(2,1)} %first.1, bf16[2,64,1024]{2,1,0:T(8,128)(2,1)} %second.1, ...), custom_call_target="tpu_custom_call" | custom-call | flops 40000000000 | bytes 1048576 | tf_op jit(solution)/shard_map/bring_near/pallas_call | solution.py:658
  57.2 0.0 copy-done
  57.2 1.3 %assemble.1 = (f32[1,2,64,1024]{3,2,1,0:T(8,128)}, f32[2,8,1024]{2,1,0:T(8,128)S(1)}) custom-call(s32[1]{0:T(128)} %bitcast.rank, f32[2,32,1024]{2,1,0:T(8,128)S(1)} %copy-done, bf16[64,1024]{1,0:T(8,128)(2,1)S(1)} %collective-permute-done.2.after.other), custom_call_target="tpu_custom_call" | custom-call | flops 16777216 | bytes 1048576 | tf_op jit(solution)/shard_map/assemble/pallas_call | solution.py:668
  58.5 0.0 collective-permute-done.3.special
  58.5 7.6 %all-to-all-done.1.arrived = bf16[32,64,128]{2,1,0:T(8,128)(2,1)S(1)} async-done(((bf16[32,64,128]{2,1,0:T(8,128)(2,1)}), bf16[32,64,128]{2,1,0:T(8,128)(2,1)S(1)}, u32[]{:S(2)}, u32[]{:S(2)}) %all-to-all-start.1) | async-done | bytes 524320 | tf_op jit(solution)/shard_map/all_to_all | solution.py:654
  66.1 1.8 %results.1 = (bf16[2,64,1024]{2,1,0:T(8,128)(2,1)}, bf16[2,64,1024]{2,1,0:T(8,128)(2,1)}, bf16[2,64,1024]{2,1,0:T(8,128)(2,1)}, f32[1,2,64,1024]{3,2,1,0:T(8,128)}) custom-call(s32[1]{0:T(128)} %bitcast.rank, bf16[32,64,128]{2,1,0:T(8,128)(2,1)S(1)} %all-to-all-done.1.arrived, ...), custom_call_target="tpu_custom_call", output_to_operand_aliasing={{3}: (4, {})} | custom-call | flops 536870912 | bytes 1048576 | tf_op jit(solution)/shard_map/results/pallas_call | solution.py:682
Async XLA Ops:
  2.4 22.5 %collective-permute-start = (bf16[64,1024]{1,0:T(8,128)(2,1)S(1)}, bf16[64,1024]{1,0:T(8,128)(2,1)S(1)}, u32[]{:S(2)}, u32[]{:S(2)}) collective-permute-start(bf16[64,1024]{1,0:T(8,128)(2,1)S(1)} %get-tuple-element.32), channel_id=1, source_target_pairs={{0,15},{1,14},{2,13},{3,12},{4,11},{5,10},{6,9},{7,8},{8,7},{9,6},... | collective-permute-start | bytes 393224 | tf_op jit(solution)/shard_map/ppermute | solution.py:566
  14.5 20.9 %all-to-all-start = ((bf16[32,64,128]{2,1,0:T(8,128)(2,1)}), bf16[32,64,128]{2,1,0:T(8,128)(2,1)S(1)}, u32[]{:S(2)}, u32[]{:S(2)}) async-start(bf16[32,64,128]{2,1,0:T(8,128)(2,1)} %bitcast.4), calls=%async_computation | async-start | bytes 1048576 | tf_op jit(solution)/shard_map/all_to_all | solution.py:581
  20.0 15.3 %copy-start.1 = (f32[2,1024]{1,0:T(2,128)S(1)}, f32[2,1024]{1,0:T(2,128)}, u32[]{:S(2)}) copy-start(f32[2,1024]{1,0:T(2,128)} %constant.18.clone.half) | copy-start | bytes 24580
  20.1 22.6 %collective-permute-start.1 = (bf16[2,1024]{1,0:T(2,128)(2,1)S(1)}, bf16[2,1024]{1,0:T(2,128)(2,1)S(1)}, u32[]{:S(2)}, u32[]{:S(2)}) collective-permute-start(bf16[2,1024]{1,0:T(2,128)(2,1)S(1)} %get-tuple-element.39), channel_id=1, source_target_pairs={{1,15},{2,14},{3,13},{4,12},{5,11},{6,10},{7,9},{9,7},{10,6},{11,5... | collective-permute-start | bytes 12296 | tf_op jit(solution)/shard_map/ppermute | solution.py:580
  37.4 18.3 %collective-permute-start.2 = (bf16[64,1024]{1,0:T(8,128)(2,1)S(1)}, bf16[64,1024]{1,0:T(8,128)(2,1)S(1)}, u32[]{:S(2)}, u32[]{:S(2)}) collective-permute-start(bf16[64,1024]{1,0:T(8,128)(2,1)S(1)} %get-tuple-element.43), channel_id=1, source_target_pairs={{0,15},{1,14},{2,13},{3,12},{4,11},{5,10},{6,9},{7,8},{8,7},{9,6},... | collective-permute-start | bytes 393224 | tf_op jit(solution)/shard_map/ppermute | solution.py:634
  45.1 21.0 %all-to-all-start.1 = ((bf16[32,64,128]{2,1,0:T(8,128)(2,1)}), bf16[32,64,128]{2,1,0:T(8,128)(2,1)S(1)}, u32[]{:S(2)}, u32[]{:S(2)}) async-start(bf16[32,64,128]{2,1,0:T(8,128)(2,1)} %bitcast.3), calls=%async_computation.1 | async-start | bytes 1048576 | tf_op jit(solution)/shard_map/all_to_all | solution.py:654
  50.7 6.4 %copy-start = (f32[2,32,1024]{2,1,0:T(8,128)S(1)}, f32[2,32,1024]{2,1,0:T(8,128)}, u32[]{:S(2)}) copy-start(f32[2,32,1024]{2,1,0:T(8,128)} %get-tuple-element.46.own) | copy-start | bytes 786436
  50.8 7.7 %collective-permute-start.3 = (bf16[2,1024]{1,0:T(2,128)(2,1)S(1)}, bf16[2,1024]{1,0:T(2,128)(2,1)S(1)}, u32[]{:S(2)}, u32[]{:S(2)}) collective-permute-start(bf16[2,1024]{1,0:T(2,128)(2,1)S(1)} %get-tuple-element.49), channel_id=1, source_target_pairs={{1,15},{2,14},{3,13},{4,12},{5,11},{6,10},{7,9},{9,7},{10,6},{11,5... | collective-permute-start | bytes 12296 | tf_op jit(solution)/shard_map/ppermute | solution.py:635
